TPU v7x, 32 devices: a whole 2x2x4 slice. The times are simulated.
32 devices in a mesh: row: 8 (over y, x, core), seq: 4 (over z).
Axes of the slice: x: 2, y: 2, z: 4, core: 2. Of those that a mesh axis runs over, the one named last changes fastest.
Arguments:
- activations: bfloat16 [8, 2048, 1280], P('row', 'seq'), may hold values from -6 to 6
- cotangent: bfloat16 [8, 2048, 1280], P('row', 'seq'), may hold values from -6 to 6
- pic_lengths: int32 [8, 8], P('row'), may hold values from 0 to 1536, as said below
- pic_widths: int32 [8, 8], P('row'), may hold values from 8 to 32
- ln1_gain: bfloat16 [1280], P(('row', 'seq')), may hold values from 0.5 to 1.5
- ln1_bias: bfloat16 [1280], P(('row', 'seq')), may hold values from -4 to 4
- qkv_weight: bfloat16 [1280, 3840], P(('row', 'seq')), may hold values from -0.15625 to 0.15625
- qkv_bias: bfloat16 [3840], P(('row', 'seq')), may hold values from -4 to 4
- proj_weight: bfloat16 [1280, 1280], P(('row', 'seq')), may hold values from -1.25 to 1.25
- proj_bias: bfloat16 [1280], P(('row', 'seq')), may hold values from -4 to 4
- ln2_gain: bfloat16 [1280], P(('row', 'seq')), may hold values from 0.5 to 1.5
- ln2_bias: bfloat16 [1280], P(('row', 'seq')), may hold values from -4 to 4
- fc1_weight: bfloat16 [1280, 5120], P(('row', 'seq')), may hold values from -0.15625 to 0.15625
- fc1_bias: bfloat16 [5120], P(('row', 'seq')), may hold values from -4 to 4
- fc2_weight: bfloat16 [5120, 1280], P(('row', 'seq')), may hold values from -0.078125 to 0.078125
- fc2_bias: bfloat16 [1280], P(('row', 'seq')), may hold values from -4 to 4
Outputs:
- layer_out: bfloat16 [8, 2048, 1280], P('row', 'seq')
- grad_activations: bfloat16 [8, 2048, 1280], P('row', 'seq')
- grad_ln1_gain: float32 [1280], P(('row', 'seq'))
- grad_ln1_bias: float32 [1280], P(('row', 'seq'))
- grad_qkv_weight: float32 [1280, 3840], P(('row', 'seq'))
- grad_qk_bias: float32 [2560], P(('row', 'seq'))
- grad_value_bias: float32 [1280], P(('row', 'seq'))
- grad_proj_weight: float32 [1280, 1280], P(('row', 'seq'))
- grad_proj_bias: float32 [1280], P(('row', 'seq'))
- grad_ln2_gain: float32 [1280], P(('row', 'seq'))
- grad_ln2_bias: float32 [1280], P(('row', 'seq'))
- grad_fc1_weight: float32 [1280, 5120], P(('row', 'seq'))
- grad_fc1_bias: float32 [5120], P(('row', 'seq'))
- grad_fc2_weight: float32 [5120, 1280], P(('row', 'seq'))
- grad_fc2_bias: float32 [1280], P(('row', 'seq'))
Inputs may be any that keep to these rules, and one draw needn't show every extreme that they name: `pic_lengths`: patches of each picture packed into a row, in order from the row's start; 0 marks an unused slot. Each row's lengths sum to between 1792 and 2047; the rest of the row is padding. `pic_widths`: patch i of a picture, in row-major order, lies at grid row i // width and grid column i % width.
All inputs are finite; a program needn't handle non-finite values.
Results may differ from a plain program's by a relative error of at most 0.015.
Values may be sent and summed in bfloat16 or wider, within the bound.
A program may use at most 512 MiB of HBM per device.

v0:
```python
import math

import jax
import jax.numpy as jnp
from jax import lax
from jax.sharding import PartitionSpec as P

HEADS = 16
HEAD_DIM = 80
ROW_LEN = 2048


NORM_EPS = 1e-06


def layer_norm(values, norm_gain, norm_shift):
    centre = jnp.mean(values, axis=-1, keepdims=True)
    centered = values - centre
    variance = jnp.mean(centered * centered, axis=-1, keepdims=True)
    return centered * lax.rsqrt(variance + NORM_EPS) * norm_gain + norm_shift


def quick_gelu(values):
    return values * jax.nn.sigmoid(1.702 * values)


def rotate_half(values):
    half_width = values.shape[-1] // 2
    return jnp.concatenate([-values[..., half_width:], values[..., :half_width]], axis=-1)


def rotate(values, cosine, sine_all):
    return values * cosine + rotate_half(values) * sine_all


def unrotate(grads, cosine, sine_all):
    return grads * cosine - rotate_half(grads * sine_all)


def token_layout(lengths, widths):
    slot_count = lengths.shape[1]
    pic_ends = jnp.cumsum(lengths, axis=1)
    pic_starts = pic_ends - lengths
    positions = jnp.arange(ROW_LEN, dtype=jnp.int32)
    picture = jnp.sum((positions[None, :, None] >= pic_ends[:, None, :]).astype(jnp.int32), axis=2)
    matches = picture[:, :, None] == jnp.arange(slot_count, dtype=jnp.int32)[None, None, :]
    pic_first = jnp.sum(jnp.where(matches, pic_starts[:, None, :], 0), axis=2)
    grid_width = jnp.sum(jnp.where(matches, widths[:, None, :], 0), axis=2)
    grid_width = jnp.maximum(grid_width, 1)
    within = positions[None, :] - pic_first
    down_pos = (within // grid_width).astype(jnp.float32)
    side_pos = (within % grid_width).astype(jnp.float32)
    quarter = HEAD_DIM // 4
    frequency = 1.0 / 10000.0 ** (jnp.arange(quarter, dtype=jnp.float32) * 4.0 / HEAD_DIM)
    angles = jnp.concatenate(
        [down_pos[..., None] * frequency, side_pos[..., None] * frequency], axis=-1
    )
    angles = jnp.concatenate([angles, angles], axis=-1)
    return (picture, jnp.cos(angles), jnp.sin(angles))


def shards(
    activations,
    cotangent,
    pic_lengths,
    pic_widths,
    ln1_gain,
    ln1_bias,
    qkv_weight,
    qkv_bias,
    proj_weight,
    proj_bias,
    ln2_gain,
    ln2_bias,
    fc1_weight,
    fc1_bias,
    fc2_weight,
    fc2_bias,
):
    row_count, tok_count, model_width = activations.shape
    token_count = row_count * tok_count
    row_len = tok_count * lax.axis_size("seq")
    seq_base = lax.axis_index("seq") * tok_count
    score_scale = 1.0 / math.sqrt(HEAD_DIM)
    head_group = HEADS // 2
    gathered = (
        lax.all_gather(ln1_gain, ("row", "seq"), axis=0, tiled=True),
        lax.all_gather(ln1_bias, ("row", "seq"), axis=0, tiled=True),
        lax.all_gather(qkv_weight, ("row", "seq"), axis=0, tiled=True),
        lax.all_gather(qkv_bias, ("row", "seq"), axis=0, tiled=True),
        lax.all_gather(proj_weight, ("row", "seq"), axis=0, tiled=True),
        lax.all_gather(proj_bias, ("row", "seq"), axis=0, tiled=True),
        lax.all_gather(ln2_gain, ("row", "seq"), axis=0, tiled=True),
        lax.all_gather(ln2_bias, ("row", "seq"), axis=0, tiled=True),
        lax.all_gather(fc1_weight, ("row", "seq"), axis=0, tiled=True),
        lax.all_gather(fc1_bias, ("row", "seq"), axis=0, tiled=True),
        lax.all_gather(fc2_weight, ("row", "seq"), axis=0, tiled=True),
        lax.all_gather(fc2_bias, ("row", "seq"), axis=0, tiled=True),
    )
    (
        gain_one,
        shift_one,
        w_qkv,
        b_qkv,
        w_proj,
        b_proj,
        gain_two,
        shift_two,
        w_up,
        b_up,
        w_down,
        b_down,
    ) = gathered
    picture, cosine, sine_all = token_layout(pic_lengths, pic_widths)
    own_picture = lax.dynamic_slice_in_dim(picture, seq_base, tok_count, 1)
    own_cos = lax.dynamic_slice_in_dim(cosine, seq_base, tok_count, 1)[:, :, None, :]
    own_sin = lax.dynamic_slice_in_dim(sine_all, seq_base, tok_count, 1)[:, :, None, :]
    inputs = activations.reshape(token_count, model_width).astype(jnp.float32)
    normed_one, norm_one_back = jax.vjp(
        layer_norm, inputs, gain_one.astype(jnp.float32), shift_one.astype(jnp.float32)
    )
    normed_one_low = normed_one.astype(jnp.bfloat16)
    mixed_qkv = jnp.dot(normed_one_low, w_qkv, preferred_element_type=jnp.float32) + b_qkv.astype(
        jnp.float32
    )
    mixed_qkv = mixed_qkv.reshape(row_count, tok_count, 3, HEADS, HEAD_DIM)
    queries = rotate(mixed_qkv[:, :, 0], own_cos, own_sin).astype(jnp.bfloat16)
    keys_rot = (
        rotate(mixed_qkv[:, :, 1], own_cos, own_sin)
        .astype(jnp.bfloat16)
        .reshape(row_count, tok_count, model_width)
    )
    values_own = mixed_qkv[:, :, 2].astype(jnp.bfloat16).reshape(row_count, tok_count, model_width)
    keys_all, values_all = (
        lax.all_gather(keys_rot, "seq", axis=1, tiled=True),
        lax.all_gather(values_own, "seq", axis=1, tiled=True),
    )

    def row_scores(number, key_block, first_head):
        query_part = queries[number][:, first_head : first_head + head_group]
        key_part = key_block[:, first_head : first_head + head_group]
        scores = (
            jnp.einsum("qhe,khe->hqk", query_part, key_part, preferred_element_type=jnp.float32)
            * score_scale
        )
        same_pic = own_picture[number][:, None] == picture[number][None, :]
        return jnp.where(same_pic[None], scores, -1e30)

    number = 0
    key_block = keys_all[number].reshape(row_len, HEADS, HEAD_DIM)
    value_block = values_all[number].reshape(row_len, HEADS, HEAD_DIM)
    attended_parts = []
    lse_parts = []
    for first_head in range(0, HEADS, head_group):
        scores = row_scores(number, key_block, first_head)
        row_top = jnp.max(scores, axis=-1, keepdims=True)
        weights_exp = jnp.exp(scores - row_top)
        row_total = jnp.sum(weights_exp, axis=-1, keepdims=True)
        prob_low = (weights_exp / row_total).astype(jnp.bfloat16)
        attended_parts.append(
            jnp.einsum(
                "hqk,khe->qhe",
                prob_low,
                value_block[:, first_head : first_head + head_group],
                preferred_element_type=jnp.float32,
            )
        )
        lse_parts.append(row_top + jnp.log(row_total))
    attended_rows = [jnp.concatenate(attended_parts, axis=1)]
    lse_rows = [lse_parts]
    attended = jnp.stack(attended_rows).reshape(token_count, model_width).astype(jnp.bfloat16)
    branch = jnp.dot(attended, w_proj, preferred_element_type=jnp.float32) + b_proj.astype(
        jnp.float32
    )
    middle = inputs + branch
    normed_two, norm_two_back = jax.vjp(
        layer_norm, middle, gain_two.astype(jnp.float32), shift_two.astype(jnp.float32)
    )
    normed_two_low = normed_two.astype(jnp.bfloat16)
    before = jnp.dot(normed_two_low, w_up, preferred_element_type=jnp.float32) + b_up.astype(
        jnp.float32
    )
    activated, gelu_back = jax.vjp(quick_gelu, before)
    activated_low = activated.astype(jnp.bfloat16)
    result = jnp.dot(activated_low, w_down, preferred_element_type=jnp.float32) + b_down.astype(
        jnp.float32
    )
    layer_out = (middle + result).astype(jnp.bfloat16).reshape(activations.shape)
    gathered = (
        lax.all_gather(ln1_gain, ("row", "seq"), axis=0, tiled=True),
        lax.all_gather(ln1_bias, ("row", "seq"), axis=0, tiled=True),
        lax.all_gather(qkv_weight, ("row", "seq"), axis=0, tiled=True),
        lax.all_gather(qkv_bias, ("row", "seq"), axis=0, tiled=True),
        lax.all_gather(proj_weight, ("row", "seq"), axis=0, tiled=True),
        lax.all_gather(proj_bias, ("row", "seq"), axis=0, tiled=True),
        lax.all_gather(ln2_gain, ("row", "seq"), axis=0, tiled=True),
        lax.all_gather(ln2_bias, ("row", "seq"), axis=0, tiled=True),
        lax.all_gather(fc1_weight, ("row", "seq"), axis=0, tiled=True),
        lax.all_gather(fc1_bias, ("row", "seq"), axis=0, tiled=True),
        lax.all_gather(fc2_weight, ("row", "seq"), axis=0, tiled=True),
        lax.all_gather(fc2_bias, ("row", "seq"), axis=0, tiled=True),
    )
    w_qkv = gathered[2]
    w_proj = gathered[4]
    w_up = gathered[8]
    w_down = gathered[10]
    grad_out = cotangent.reshape(token_count, model_width)
    grad_out_wide = grad_out.astype(jnp.float32)
    grad_down = jnp.dot(activated_low.T, grad_out, preferred_element_type=jnp.float32)
    grad_down_bias = jnp.sum(grad_out_wide, axis=0)
    grad_gelu_out = jnp.dot(grad_out, w_down.T, preferred_element_type=jnp.float32)
    (grad_before,) = gelu_back(grad_gelu_out)
    grad_before_low = grad_before.astype(jnp.bfloat16)
    grad_up_bias = jnp.sum(grad_before_low.astype(jnp.float32), axis=0)
    grad_up = jnp.dot(normed_two_low.T, grad_before_low, preferred_element_type=jnp.float32)
    grad_normed_two = jnp.dot(grad_before_low, w_up.T, preferred_element_type=jnp.float32)
    grad_middle, grad_gain_two, grad_shift_two = norm_two_back(grad_normed_two)
    grad_middle = grad_middle + grad_out_wide
    grad_branch_low = grad_middle.astype(jnp.bfloat16)
    grad_proj_bias = jnp.sum(grad_branch_low.astype(jnp.float32), axis=0)
    grad_proj = jnp.dot(attended.T, grad_branch_low, preferred_element_type=jnp.float32)
    grad_attended = jnp.dot(grad_branch_low, w_proj.T, preferred_element_type=jnp.float32)
    grad_attended = grad_attended.astype(jnp.bfloat16).reshape(
        row_count, tok_count, HEADS, HEAD_DIM
    )
    number = 0
    key_block = keys_all[number].reshape(row_len, HEADS, HEAD_DIM)
    value_block = values_all[number].reshape(row_len, HEADS, HEAD_DIM)
    query_parts = []
    score_parts = []
    prob_parts = []
    for part_number, first_head in enumerate(range(0, HEADS, head_group)):
        head_span = slice(first_head, first_head + head_group)
        scores = row_scores(number, key_block, first_head)
        probs_wide = jnp.exp(scores - lse_rows[number][part_number])
        grad_probs = jnp.einsum(
            "qhe,khe->hqk",
            grad_attended[number][:, head_span],
            value_block[:, head_span],
            preferred_element_type=jnp.float32,
        )
        row_delta = jnp.sum(probs_wide * grad_probs, axis=-1, keepdims=True)
        grad_scores_part = (probs_wide * (grad_probs - row_delta)).astype(jnp.bfloat16)
        query_parts.append(
            jnp.einsum(
                "hqk,khe->qhe",
                grad_scores_part,
                key_block[:, head_span],
                preferred_element_type=jnp.float32,
            )
            * score_scale
        )
        score_parts.append(grad_scores_part)
        prob_parts.append(probs_wide.astype(jnp.bfloat16))
    grad_query_rows = [jnp.concatenate(query_parts, axis=1)]
    grad_scores = jnp.concatenate(score_parts, axis=0)
    probs_low = jnp.concatenate(prob_parts, axis=0)

    def key_terms(
        first_row,
        row_span,
        grad_scores=grad_scores,
        probs_low=probs_low,
        query_row=queries[number],
        grad_att_row=grad_attended[number],
    ):
        grad_keys_part = (
            jnp.einsum("hqk,qhe->khe", grad_scores, query_row, preferred_element_type=jnp.float32)
            * score_scale
        )
        grad_values_part = jnp.einsum(
            "hqk,qhe->khe", probs_low, grad_att_row, preferred_element_type=jnp.float32
        )
        return jnp.concatenate(
            [
                grad_keys_part.reshape(row_span, model_width),
                grad_values_part.reshape(row_span, model_width),
            ],
            axis=1,
        )

    grad_kv_rows = [
        lax.psum_scatter(
            key_terms(jnp.int32(0), lax.axis_size("seq") * tok_count).astype(jnp.bfloat16),
            "seq",
            scatter_dimension=0,
            tiled=True,
        ).astype(jnp.float32)
    ]
    grad_queries = jnp.stack(grad_query_rows)
    grad_kv = jnp.stack(grad_kv_rows)
    grad_keys = grad_kv[..., :model_width].reshape(row_count, tok_count, HEADS, HEAD_DIM)
    grad_values = grad_kv[..., model_width:].reshape(row_count, tok_count, HEADS, HEAD_DIM)
    grad_mixed = jnp.stack(
        [
            unrotate(grad_queries, own_cos, own_sin),
            unrotate(grad_keys, own_cos, own_sin),
            grad_values,
        ],
        axis=2,
    )
    grad_mixed_low = grad_mixed.reshape(token_count, 3 * model_width).astype(jnp.bfloat16)
    grad_qkv_bias = jnp.sum(grad_mixed_low.astype(jnp.float32), axis=0)
    grad_qk_part = grad_qkv_bias[: 2 * model_width]
    grad_value_part = grad_qkv_bias[2 * model_width :]
    grad_qkv = jnp.dot(normed_one_low.T, grad_mixed_low, preferred_element_type=jnp.float32)
    grad_normed_one = jnp.dot(grad_mixed_low, w_qkv.T, preferred_element_type=jnp.float32)
    grad_inputs, grad_gain_one, grad_shift_one = norm_one_back(grad_normed_one)
    grad_acts = (grad_inputs + grad_middle).astype(jnp.bfloat16).reshape(activations.shape)
    owned = (
        lax.psum_scatter(grad_gain_one, ("row", "seq"), scatter_dimension=0, tiled=True),
        lax.psum_scatter(grad_shift_one, ("row", "seq"), scatter_dimension=0, tiled=True),
        lax.psum_scatter(grad_qkv, ("row", "seq"), scatter_dimension=0, tiled=True),
        lax.psum_scatter(grad_qk_part, ("row", "seq"), scatter_dimension=0, tiled=True),
        lax.psum_scatter(grad_value_part, ("row", "seq"), scatter_dimension=0, tiled=True),
        lax.psum_scatter(grad_proj, ("row", "seq"), scatter_dimension=0, tiled=True),
        lax.psum_scatter(grad_proj_bias, ("row", "seq"), scatter_dimension=0, tiled=True),
        lax.psum_scatter(grad_gain_two, ("row", "seq"), scatter_dimension=0, tiled=True),
        lax.psum_scatter(grad_shift_two, ("row", "seq"), scatter_dimension=0, tiled=True),
        lax.psum_scatter(grad_up, ("row", "seq"), scatter_dimension=0, tiled=True),
        lax.psum_scatter(grad_up_bias, ("row", "seq"), scatter_dimension=0, tiled=True),
        lax.psum_scatter(grad_down, ("row", "seq"), scatter_dimension=0, tiled=True),
        lax.psum_scatter(grad_down_bias, ("row", "seq"), scatter_dimension=0, tiled=True),
    )
    return (
        layer_out,
        grad_acts,
        owned[0],
        owned[1],
        owned[2],
        owned[3],
        owned[4],
        owned[5],
        owned[6],
        owned[7],
        owned[8],
        owned[9],
        owned[10],
        owned[11],
        owned[12],
    )


def solution(mesh):
    return jax.shard_map(
        shards,
        mesh=mesh,
        in_specs=(
            P("row", "seq", None),
            P("row", "seq", None),
            P("row", None),
            P("row", None),
            P(("row", "seq")),
            P(("row", "seq")),
            P(("row", "seq"), None),
            P(("row", "seq")),
            P(("row", "seq"), None),
            P(("row", "seq")),
            P(("row", "seq")),
            P(("row", "seq")),
            P(("row", "seq"), None),
            P(("row", "seq")),
            P(("row", "seq"), None),
            P(("row", "seq")),
        ),
        out_specs=(
            P("row", "seq", None),
            P("row", "seq", None),
            P(("row", "seq")),
            P(("row", "seq")),
            P(("row", "seq"), None),
            P(("row", "seq")),
            P(("row", "seq")),
            P(("row", "seq"), None),
            P(("row", "seq")),
            P(("row", "seq")),
            P(("row", "seq")),
            P(("row", "seq"), None),
            P(("row", "seq")),
            P(("row", "seq"), None),
            P(("row", "seq")),
        ),
        check_vma=False,
    )
```

profile of v0, /device:TPU:0, one launch (start us, length us, event | category | flops | bytes accessed | tf_op | source)
XLA Modules:
  0.0 2614.5 jit_solution(2506992323540822752)
XLA Ops:
  15.6 43.6 %all-reduce.18 = (bf16[3840]{0:T(1024)(128)(2,1)S(1)}, bf16[1280]{0:T(1024)(128)(2,1)S(1)}, bf16[1280]{0:T(1024)(128)(2,1)S(1)}, bf16[1280]{0:T(1024)(128)(2,1)S...) all-reduce(bf16[3840]{0:T(1024)(128)(2,1)S(1)} %dynamic-update-slic, ...), channel_id=1, replica_groups=mesh['row'=8,'seq'=4] {'row','seq'}, use_global_device_ids=true, to_apply=%add.2 | all-reduce | flops 16640 | bytes 66560
  62.5 34.9 %all-gather.7.cloned.1.call-done = bf16[1280,3840]{1,0:T(8,128)(2,1)} async-done(((bf16[40,3840]{1,0:T(8,128)(2,1)}), bf16[1280,3840]{1,0:T(8,128)(2,1)}) %all-gather.7.cloned.1.call-update) | async-done | bytes 9830416 | tf_op jit(solution)/shard_map/all_gather | solution.py:89
  136.1 84.6 %all-gather.11.cloned.1.call-done = bf16[1,2048,1280]{1,2,0:T(8,128)(2,1)} async-done(((bf16[1,512,1280]{1,2,0:T(8,128)(2,1)}), bf16[1,2048,1280]{1,2,0:T(8,128)(2,1)}) %all-gather.11.cloned.1.call-update) | async-done | bytes 5242896 | tf_op jit(solution)/shard_map/all_gather | solution.py:135
  220.7 17.8 fusion.104
  238.5 14.0 fusion.9
  252.5 14.8 fusion.105
  267.3 13.6 fusion.8
  280.9 38.4 %all-gather.9.cloned.1.call-done = bf16[1,2048,1280]{1,2,0:T(8,128)(2,1)} async-done(((bf16[1,512,1280]{1,2,0:T(8,128)(2,1)}), bf16[1,2048,1280]{1,2,0:T(8,128)(2,1)}) %all-gather.9.cloned.1.call-update) | async-done | bytes 5242896 | tf_op jit(solution)/shard_map/all_gather | solution.py:136
  319.3 14.9 fusion.83
  334.2 15.3 fusion.82
  350.8 28.9 %all-gather.13.cloned.1.call-done = bf16[1280,1280]{1,0:T(8,128)(2,1)} async-done(((bf16[40,1280]{1,0:T(8,128)(2,1)}), bf16[1280,1280]{1,0:T(8,128)(2,1)}) %all-gather.13.cloned.1.call-update) | async-done | bytes 3276816 | tf_op jit(solution)/shard_map/all_gather | solution.py:91
  385.7 94.0 %all-gather.15.cloned.1.call-done = bf16[1280,5120]{1,0:T(8,128)(2,1)} async-done(((bf16[40,5120]{1,0:T(8,128)(2,1)}), bf16[1280,5120]{1,0:T(8,128)(2,1)}) %all-gather.15.cloned.1.call-update) | async-done | bytes 13107216 | tf_op jit(solution)/shard_map/all_gather | solution.py:95
  479.8 14.9 fusion.99
  494.7 84.4 %all-gather.17.cloned.1.call-done = bf16[5120,1280]{1,0:T(8,128)(2,1)} async-done(((bf16[160,1280]{1,0:T(8,128)(2,1)}), bf16[5120,1280]{1,0:T(8,128)(2,1)}) %all-gather.17.cloned.1.call-update) | async-done | bytes 13107216 | tf_op jit(solution)/shard_map/all_gather | solution.py:97
  579.2 16.9 convert_reduce_fusion
  596.1 14.9 multiply_reduce_fusion.2
  619.6 24.2 multiply_reduce_fusion
  643.9 24.0 multiply_reduce_fusion.1
  667.8 64.9 %multiply_convert_fusion = (bf16[8,512,2048]{2,1,0:T(8,128)(2,1)}, bf16[8,512,2048]{2,1,0:T(8,128)(2,1)}, bf16[8,512,2048]{2,1,0:T(8,128)(2,1)}, bf16[8,512,2048]{2,1,0:T(8,128)(2,1)}) fusion(f32[8,512,2048]{2,1,0:T(8,128)} %get-tuple-element.87, f32[8,512,2048]{2,1,0:T(8,128)} %get-tuple-element.80, f32[8,512]{1,0:T(8,128)S(1)} %get-tuple-element.86, ...), kind=kLoop, calls=%fused_computation.8 | loop fusion | flops 83886080 | bytes 201392128 | tf_op jit(solution)/shard_map/convert_element_type | solution.py:243
  732.7 13.5 fusion.20
  746.2 13.6 multiply_convert_fusion.2
  759.9 12.7 pad_maximum_fusion
  772.7 12.7 convolution_multiply_fusion
  797.3 151.7 %reduce-scatter.6.cloned.1.call-done = bf16[512,2560]{0,1:T(8,128)(2,1)} async-done(((bf16[2048,2560]{0,1:T(8,128)(2,1)}), bf16[512,2560]{0,1:T(8,128)(2,1)}) %reduce-scatter.6.cloned.1.call-update) | async-done | bytes 2621456 | tf_op jit(solution)/shard_map/reduce_scatter | solution.py:283
  995.0 18.2 fusion.70
  1013.9 15.6 fusion.98
  1030.2 16.3 fusion.33
  1048.7 52.6 %all-reduce.21.cloned.1.call-done = (f32[1280]{0:T(1024)}, f32[1280]{0:T(1024)}, f32[2560]{0:T(1024)}, f32[1280]{0:T(1024)}, f32[1280]{0:T(1024)}, /*index=5*/f3...) async-done(((f32[1280]{0:T(1024)}, f32[1280]{0:T(1024)}, f32[2560]{0:T(1024)}, f32[1280]{0:T(1024)}, f32[1280]{0:T(1024)}, /*index=5*/f32[1280]{0:T(1024)}, ...) | async-done | bytes 66576
  1112.9 152.2 %reduce-scatter.10.cloned.1.call-done = f32[40,1280]{1,0:T(8,128)} async-done(((f32[1280,1280]{1,0:T(8,128)}), f32[40,1280]{1,0:T(8,128)}) %reduce-scatter.10.cloned.1.call-update) | async-done | bytes 204816 | tf_op jit(solution)/shard_map/reduce_scatter | solution.py:316
  1265.1 218.2 %reduce-scatter.8.cloned.1.call-done = f32[40,3840]{1,0:T(8,128)} async-done(((f32[1280,3840]{1,0:T(8,128)}), f32[40,3840]{1,0:T(8,128)}) %reduce-scatter.8.cloned.1.call-update) | async-done | bytes 614416 | tf_op jit(solution)/shard_map/reduce_scatter | solution.py:313
  1483.3 562.3 %reduce-scatter.14.cloned.1.call-done = f32[160,1280]{1,0:T(8,128)} async-done(((f32[5120,1280]{1,0:T(8,128)}), f32[160,1280]{1,0:T(8,128)}) %reduce-scatter.14.cloned.1.call-update) | async-done | bytes 819216 | tf_op jit(solution)/shard_map/reduce_scatter | solution.py:322
  2045.6 561.7 %reduce-scatter.12.cloned.1.call-done = f32[40,5120]{1,0:T(8,128)} async-done(((f32[1280,5120]{1,0:T(8,128)}), f32[40,5120]{1,0:T(8,128)}) %reduce-scatter.12.cloned.1.call-update) | async-done | bytes 819216 | tf_op jit(solution)/shard_map/reduce_scatter | solution.py:320
  (215 shorter events, 138.7 us)
Async XLA Ops:
  7.2 54.5 %copy-start = (bf16[1,512,1280]{2,1,0:T(8,128)(2,1)S(1)}, bf16[1,512,1280]{2,1,0:T(8,128)(2,1)}, u32[]{:S(2)}) copy-start(bf16[1,512,1280]{2,1,0:T(8,128)(2,1)} %param.16) | copy-start | bytes 3932164
  7.2 90.3 %all-gather.7.cloned.1.call-start = ((), (), s32[]{:S(2)}) async-start(), calls=%async_computation.5 | async-start | bytes 10137600 | tf_op jit(solution)/shard_map/all_gather | solution.py:89
  7.9 212.8 %all-gather.11.cloned.1.call-start = ((), (), s32[]{:S(2)}) async-start(), calls=%async_computation.7 | async-start | bytes 6553600 | tf_op jit(solution)/shard_map/all_gather | solution.py:135
  59.2 49.7 %copy-start.21 = (f32[1280]{0:T(1024)}, f32[1280]{0:T(1024)S(1)}, u32[]{:S(2)}) copy-start(f32[1280]{0:T(1024)S(1)} %convert_element_type.188) | copy-start | bytes 15364
  59.2 49.7 %copy-start.38 = (f32[1280]{0:T(1024)}, f32[1280]{0:T(1024)S(1)}, u32[]{:S(2)}) copy-start(f32[1280]{0:T(1024)S(1)} %convert_element_type.189) | copy-start | bytes 15364
  61.7 71.7 %copy-start.13 = (f32[512,80]{0,1:T(8,128)}, f32[512,80]{0,1:T(8,128)S(1)}, u32[]{:S(2)}) copy-start(f32[512,80]{0,1:T(8,128)S(1)} %get-tuple-element.67) | copy-start | bytes 491524
  61.7 71.7 %copy-start.15 = (f32[512,80]{0,1:T(8,128)}, f32[512,80]{0,1:T(8,128)S(1)}, u32[]{:S(2)}) copy-start(f32[512,80]{0,1:T(8,128)S(1)} %get-tuple-element.68) | copy-start | bytes 491524
  62.0 47.0 %copy-start.23 = (f32[512]{0:T(512)}, f32[512]{0:T(512)S(1)}, u32[]{:S(2)}) copy-start(f32[512]{0:T(512)S(1)} %broadcast_multiply_fusion.2) | copy-start | bytes 6148
  62.5 46.5 %copy-start.34 = (f32[512]{0:T(512)}, f32[512]{0:T(512)S(1)}, u32[]{:S(2)}) copy-start(f32[512]{0:T(512)S(1)} %fusion.37) | copy-start | bytes 6148
  62.5 46.5 %copy-start.30 = (f32[512]{0:T(512)}, f32[512]{0:T(512)S(1)}, u32[]{:S(2)}) copy-start(f32[512]{0:T(512)S(1)} %fusion.93) | copy-start | bytes 6148
  123.9 195.4 %all-gather.9.cloned.1.call-start = ((), (), s32[]{:S(2)}) async-start(), calls=%async_computation.6 | async-start | bytes 6553600 | tf_op jit(solution)/shard_map/all_gather | solution.py:136
  127.0 252.7 %all-gather.13.cloned.1.call-start = ((), (), s32[]{:S(2)}) async-start(), calls=%async_computation.8 | async-start | bytes 3379200 | tf_op jit(solution)/shard_map/all_gather | solution.py:91
  127.6 352.2 %all-gather.15.cloned.1.call-start = ((), (), s32[]{:S(2)}) async-start(), calls=%async_computation.9 | async-start | bytes 13516800 | tf_op jit(solution)/shard_map/all_gather | solution.py:95
  128.2 451.0 %all-gather.17.cloned.1.call-start = ((), (), s32[]{:S(2)}) async-start(), calls=%async_computation.10 | async-start | bytes 13516800 | tf_op jit(solution)/shard_map/all_gather | solution.py:97
  128.8 820.2 %reduce-scatter.6.cloned.1.call-start = ((), (), s32[]{:S(2)}) async-start(), calls=%async_computation.11 | async-start | bytes 13107200 | tf_op jit(solution)/shard_map/reduce_scatter | solution.py:283
  133.4 87.3 %copy-start.20 = (pred[512,2048]{1,0:T(8,128)(4,1)S(1)}, pred[512,2048]{1,0:T(8,128)(4,1)}, u32[]{:S(2)}) copy-start(pred[512,2048]{1,0:T(8,128)(4,1)} %broadcast_compare_fusion) | copy-start | bytes 3145732
  136.0 116.4 %copy-start.18 = (bf16[512,16,80]{0,2,1:T(8,128)(2,1)}, bf16[512,16,80]{0,2,1:T(8,128)(2,1)S(1)}, u32[]{:S(2)}) copy-start(bf16[512,16,80]{0,2,1:T(8,128)(2,1)S(1)} %fusion.50) | copy-start | bytes 3932164
  349.5 30.2 %copy-start.1 = (bf16[1,512,1280]{2,1,0:T(8,128)(2,1)S(1)}, bf16[1,512,1280]{2,1,0:T(8,128)(2,1)}, u32[]{:S(2)}) copy-start(bf16[1,512,1280]{2,1,0:T(8,128)(2,1)} %param.16) | copy-start | bytes 3932164
  349.5 30.2 %copy-start.27 = (f32[1280]{0:T(1024)S(1)}, f32[1280]{0:T(1024)}, u32[]{:S(2)}) copy-start(f32[1280]{0:T(1024)} %convert_element_type.201) | copy-start | bytes 15364
  350.8 33.0 %copy-start.9 = (bf16[512,16,80]{0,2,1:T(8,128)(2,1)}, bf16[512,16,80]{0,2,1:T(8,128)(2,1)S(1)}, u32[]{:S(2)}) copy-start(bf16[512,16,80]{0,2,1:T(8,128)(2,1)S(1)} %pad_maximum_fusion.4) | copy-start | bytes 3932164
  383.8 96.0 %copy-start.25 = (f32[1280]{0:T(1024)S(1)}, f32[1280]{0:T(1024)}, u32[]{:S(2)}) copy-start(f32[1280]{0:T(1024)} %convert_element_type.202) | copy-start | bytes 15364
  383.8 96.0 %copy-start.40 = (f32[1280]{0:T(1024)S(1)}, f32[1280]{0:T(1024)}, u32[]{:S(2)}) copy-start(f32[1280]{0:T(1024)} %convert_element_type.203) | copy-start | bytes 15364
  383.8 227.2 %copy-start.36 = (f32[512]{0:T(512)}, f32[512]{0:T(512)S(1)}, u32[]{:S(2)}) copy-start(f32[512]{0:T(512)S(1)} %broadcast_multiply_fusion.1) | copy-start | bytes 6148
  385.7 225.4 %copy-start.42 = (f32[512]{0:T(512)}, f32[512]{0:T(512)S(1)}, u32[]{:S(2)}) copy-start(f32[512]{0:T(512)S(1)} %fusion.94) | copy-start | bytes 6148
  385.7 193.4 %copy-start.28 = (f32[5120]{0:T(1024)S(1)}, f32[5120]{0:T(1024)}, u32[]{:S(2)}) copy-start(f32[5120]{0:T(1024)} %convert_element_type.205) | copy-start | bytes 61444
  494.7 101.4 %copy-start.6 = (f32[512,1280]{1,0:T(8,128)S(1)}, f32[512,1280]{1,0:T(8,128)}, u32[]{:S(2)}) copy-start(f32[512,1280]{1,0:T(8,128)} %copy-done.5) | copy-start | bytes 7864324
  772.6 328.7 %all-reduce.21.cloned.1.call-start = ((), (), s32[]{:S(2)}) async-start(), calls=%async_computation.16 | async-start | bytes 180224
  974.9 290.2 %reduce-scatter.10.cloned.1.call-start = ((), (), s32[]{:S(2)}) async-start(), calls=%async_computation.13 | async-start | bytes 6758400 | tf_op jit(solution)/shard_map/reduce_scatter | solution.py:316
  980.9 502.5 %reduce-scatter.8.cloned.1.call-start = ((), (), s32[]{:S(2)}) async-start(), calls=%async_computation.12 | async-start | bytes 20275200 | tf_op jit(solution)/shard_map/reduce_scatter | solution.py:313
  993.7 1051.9 %reduce-scatter.14.cloned.1.call-start = ((), (), s32[]{:S(2)}) async-start(), calls=%async_computation.15 | async-start | bytes 27033600 | tf_op jit(solution)/shard_map/reduce_scatter | solution.py:322
  1013.3 1594.0 %reduce-scatter.12.cloned.1.call-start = ((), (), s32[]{:S(2)}) async-start(), calls=%async_computation.14 | async-start | bytes 27033600 | tf_op jit(solution)/shard_map/reduce_scatter | solution.py:320
  1030.2 16.3 copy-start.33
  (29 other events, 117.3 us)
Sparse Core Ops, SparseCore 0:
  10.8 86.5 all-gather.6
  124.1 96.5 all-gather.10
  222.8 96.3 all-gather.8
  322.0 57.6 all-gather.12
  382.4 97.3 all-gather.14
  482.5 96.6 all-gather.16
  772.7 176.1 reduce-scatter.5
  975.0 126.2 all-reduce.20
  1104.3 160.7 reduce-scatter.9
  1273.1 210.1 reduce-scatter.7
  1486.3 559.2 reduce-scatter.13
  2048.5 558.7 reduce-scatter.11
where the time goes:
time: 2620 us; the launch traced here: 2610 us
  waiting for transfers between devices  2070 us (79%)
  matrix products  303 us (12%)
  other arithmetic  140 us (5%)
  local copies, waits for them, and re-layouts  45.7 us (2%)
  blocking collectives  43.6 us (2%)
    reduce_scatter x1, waiting for transfers between devices, shards(): lax.psum_scatter(grad_down, ('row', 'seq'), scatter_dimension=0, tiled=True)  562 us
    reduce_scatter x1, waiting for transfers between devices, shards(): lax.psum_scatter(grad_up, ('row', 'seq'), scatter_dimension=0, tiled=True)  562 us
    reduce_scatter x1, waiting for transfers between devices, shards(): lax.psum_scatter(grad_qkv, ('row', 'seq'), scatter_dimension=0, tiled=True)  218 us
    reduce_scatter x1, waiting for transfers between devices, shards(): lax.psum_scatter(grad_proj, ('row', 'seq'), scatter_dimension=0, tiled=True)  152 us
    reduce_scatter x1, waiting for transfers between devices, shards(): lax.psum_scatter(key_terms(jnp.int32(0), lax.axis_size('seq') * tok_count...  152 us
    all_gather x1, waiting for transfers between devices, shards(): lax.all_gather(fc1_weight, ('row', 'seq'), axis=0, tiled=True)  94 us
    all_gather x1, waiting for transfers between devices, shards(): lax.all_gather(keys_rot, 'seq', axis=1, tiled=True)  84.6 us
    all_gather x1, waiting for transfers between devices, shards(): lax.all_gather(fc2_weight, ('row', 'seq'), axis=0, tiled=True)  84.4 us
  transfers between devices with their start and end apart: 12, of which 12 were waited for; matrix products, arithmetic and copies ran while one was open for 9% of the time, Pallas kernels for 0%

commit v1 on v0

v1 whole, which is shorter than its diff:
```python
import functools
import math

import jax
import jax.numpy as jnp
from jax import lax
from jax.experimental import pallas as pl
from jax.experimental.pallas import tpu as pltpu
from jax.sharding import PartitionSpec as P

HEADS = 16
HEAD_DIM = 80
HALF = HEAD_DIM // 2
LANE = 128
NORM_EPS = 1e-06
SCALE = 1.0 / math.sqrt(HEAD_DIM)
LOG2E = 1.4426950408889634
EXP_SCALE = SCALE * LOG2E
QBLK = 256
MESH = pl.DeviceIdType.MESH
ANY = pl.BlockSpec(memory_space=pl.ANY)
VMEM = pl.BlockSpec(memory_space=pltpu.VMEM)


def round_up(value, unit):
    return -(-value // unit) * unit


def flip(index, bit):
    return index + bit - 2 * bit * ((index // bit) % 2)


def remote(src, dst, send_sem, recv_sem, row, seq):
    return pltpu.make_async_remote_copy(
        src_ref=src,
        dst_ref=dst,
        send_sem=send_sem,
        recv_sem=recv_sem,
        device_id=(row, seq),
        device_id_type=MESH,
    )


class Sems:
    def __init__(self, ref):
        self.ref = ref
        self.used = 0

    def take(self, count):
        first = self.used
        self.used += count
        assert self.used <= self.ref.shape[0]
        return [self.ref.at[first + i] for i in range(count)]


class Chain:
    def __init__(self, own, buf, base, row, seq, size, sems):
        self.own, self.buf, self.base = own, buf, base
        self.row, self.seq, self.size = row, seq, size
        self.sems = [[(sems.take(1)[0], sems.take(1)[0]) for _ in range(size - 1)] for _ in range(2)]
        (self.local,) = sems.take(1)

    def _copies(self, step):
        seq, size = self.seq, self.size
        out = []
        for way in range(2):
            sign = 1 - 2 * way
            block = seq - sign * (step - 1)
            peer = seq + sign
            going = (peer >= 0) & (peer < size) & (block >= 0) & (block < size)
            slot = self.buf.at[self.base + block]
            src = self.own if step == 1 else slot
            copy = functools.partial(remote, src, slot, *self.sems[way][step - 1], self.row, peer)
            come = seq - sign * step
            coming = (come >= 0) & (come < size)
            into = self.buf.at[self.base + come]
            arrive = functools.partial(remote, into, into, *self.sems[way][step - 1], self.row, peer)
            out.append((going, copy, coming, arrive))
        return out

    def keep(self):
        return pltpu.make_async_copy(self.own, self.buf.at[self.base + self.seq], self.local)

    def send(self, step):
        if step == 1:
            self.keep().start()
        for going, copy, _, _ in self._copies(step):
            pl.when(going)(lambda copy=copy: copy().start())

    def recv(self, step):
        for _, _, coming, arrive in self._copies(step):
            pl.when(coming)(lambda arrive=arrive: arrive().wait_recv())

    def finish(self):
        for step in range(1, self.size):
            for going, copy, _, _ in self._copies(step):
                pl.when(going)(lambda copy=copy: copy().wait_send())


class Scatter:
    def __init__(self, src, dst_of, row, seq, size, sems):
        self.src, self.dst_of = src, dst_of
        self.row, self.seq, self.size = row, seq, size
        self.sems = [(sems.take(1)[0], sems.take(1)[0]) for _ in range(size - 1)]
        (self.local,) = sems.take(1)

    def _to(self, step):
        peer = (self.seq + step) % self.size
        return remote(self.src.at[peer], self.dst_of(self.seq), *self.sems[step - 1], self.row, peer)

    def _from(self, step):
        peer = (self.seq + self.size - step) % self.size
        into = self.dst_of(peer)
        return remote(into, into, *self.sems[step - 1], self.row, peer)

    def keep(self):
        return pltpu.make_async_copy(self.src.at[self.seq], self.dst_of(self.seq), self.local)

    def send(self, step):
        self._to(step).start()

    def send_all(self):
        self.keep().start()
        for step in range(1, self.size):
            self.send(step)

    def recv(self):
        self.keep().wait()
        for step in range(1, self.size):
            self._from(step).wait_recv()

    def finish(self):
        for step in range(1, self.size):
            self._to(step).wait_send()


class Spread:
    def __init__(self, buf, row, seq, rows, size, sems):
        self.buf, self.row, self.seq, self.size = buf, row, seq, size
        bits = [1 << i for i in range(1, rows.bit_length() - 1)]
        self.stages = len(bits)
        self.orders = (bits, bits[::-1])
        self.half = buf.shape[2] // 2
        self.sems = [
            [[(sems.take(1)[0], sems.take(1)[0]) for _ in range(1 << j)] for j in range(self.stages)]
            for _ in range(2)
        ]
        self.core_sems = [(sems.take(1)[0], sems.take(1)[0])]
        self.core_sems += [
            (sems.take(1)[0], sems.take(1)[0]) for _ in range(2 * ((1 << self.stages) - 1))
        ]

    def _block(self, row, half):
        first = row * self.size
        if half is None:
            return self.buf.at[pl.ds(first, self.size)]
        return self.buf.at[pl.ds(first, self.size), :, pl.ds(half * self.half, self.half)]

    def _rows(self, start, half, stage):
        rows = [start]
        for bit in self.orders[half][:stage]:
            rows += [flip(row, bit) for row in rows]
        return rows

    def _pairs(self, stage):
        out = []
        for half in range(2):
            bit = self.orders[half][stage]
            peer = flip(self.row, bit)
            for i, row in enumerate(self._rows(self.row, half, stage)):
                here = self._block(row, half)
                there = self._block(flip(row, bit), half)
                pair = self.sems[half][stage][i]
                out.append((here, there, pair, peer))
        return out

    def _core(self, index, block):
        return remote(block, block, *self.core_sems[index], flip(self.row, 1), self.seq)

    def _core_blocks(self, row):
        out = [[self._block(row, None)]]
        for stage in range(self.stages):
            out.append([])
            for half in range(2):
                bit = self.orders[half][stage]
                for other in self._rows(row, half, stage):
                    out[-1].append(self._block(flip(other, bit), half))
        return out

    def _first(self, stage):
        return 0 if stage == 0 else 1 + 2 * ((1 << (stage - 1)) - 1)

    def send(self, stage):
        if stage < self.stages:
            for here, _, pair, peer in self._pairs(stage):
                remote(here, here, *pair, peer, self.seq).start()
        for i, block in enumerate(self._core_blocks(self.row)[stage]):
            self._core(self._first(stage) + i, block).start()

    def recv(self, stage):
        for _, there, pair, peer in self._pairs(stage):
            remote(there, there, *pair, peer, self.seq).wait_recv()

    def finish(self):
        for stage in range(self.stages):
            for here, _, pair, peer in self._pairs(stage):
                remote(here, here, *pair, peer, self.seq).wait_send()
        mine, theirs = self._core_blocks(self.row), self._core_blocks(flip(self.row, 1))
        for stage in range(self.stages + 1):
            for i, block in enumerate(theirs[stage]):
                self._core(self._first(stage) + i, block).wait_recv()
            for i, block in enumerate(mine[stage]):
                self._core(self._first(stage) + i, block).wait_send()


def greet(row, seq, rows, size):
    barrier = pltpu.get_barrier_semaphore()
    count = 0
    bit = 1
    while bit < rows:
        pl.semaphore_signal(barrier, inc=1, device_id=(flip(row, bit), seq), device_id_type=MESH)
        bit *= 2
        count += 1
    for step in range(1, size):
        pl.semaphore_signal(barrier, inc=1, device_id=(row, (seq + step) % size), device_id_type=MESH)
        count += 1
    pl.semaphore_wait(barrier, count)


def forward_kernel(
    rows, size, shard, group,
    x, wq, wp, w1, w2, small, cos, sin, pic_col, pic_row,
    wp_all, w1_all, w2_all, att, small_sum, normed, qkv, wq_full, lse,
    xg, wq_buf, small_buf, wq_wide, v_turn, o_part, o_send, sem_ref,
):
    row, seq = lax.axis_index("row"), lax.axis_index("seq")
    toks, width = x.shape
    length = toks * size
    part = group * LANE
    sems = Sems(sem_ref)
    base = row * size
    g_small = Chain(small, small_buf, base, row, seq, size, sems)
    g_wp = Chain(wp, wp_all, base, row, seq, size, sems)
    g_w1 = Chain(w1, w1_all, base, row, seq, size, sems)
    g_w2 = Chain(w2, w2_all, base, row, seq, size, sems)
    g_x = Chain(x, xg, 0, row, seq, size, sems)
    a_wq = Scatter(wq, lambda j: wq_buf.at[base + j], row, seq, size, sems)
    s_small = Spread(small_buf, row, seq, rows, size, sems)
    s_wq = Spread(wq_buf, row, seq, rows, size, sems)
    s_wp = Spread(wp_all, row, seq, rows, size, sems)
    s_w1 = Spread(w1_all, row, seq, rows, size, sems)
    s_w2 = Spread(w2_all, row, seq, rows, size, sems)
    a_o = Scatter(o_send, lambda j: att.at[j], row, seq, size, sems)
    last = s_small.stages

    greet(row, seq, rows, size)
    g_small.send(1)
    a_wq.send_all()
    g_wp.send(1)
    g_w1.send(1)
    g_x.send(1)
    for step in range(1, size):
        for g in (g_small, g_wp, g_w1):
            g.recv(step)
            if step < size - 1:
                g.send(step + 1)
    a_wq.recv()
    for g in (g_small, g_wp, g_w1, g_x):
        g.keep().wait()
    for s in (s_small, s_wq, s_wp, s_w1):
        s.send(0)
    for stage in range(last):
        for s in (s_small, s_wq):
            s.recv(stage)
            s.send(stage + 1)
    s_small.finish()
    s_wq.finish()

    total = jnp.zeros(small_sum.shape, jnp.float32)
    for i in range(rows * size):
        total += small_buf[i].astype(jnp.float32)
    small_sum[...] = total
    bias = jnp.zeros((1, 3 * part), jnp.float32)
    for i in range(rows * size):
        block = wq_buf[i].astype(jnp.float32)
        wq_wide[pl.ds(i * shard, shard), :] = block[:shard]
        bias += block[shard : shard + 1]
    for i in range(0, width, LANE):
        wq_full[pl.ds(i, LANE), :] = wq_wide[pl.ds(i, LANE), :].astype(jnp.bfloat16)
    wq_wide[0:1, :] = bias

    def project(chunk):
        first = pl.multiple_of(chunk * toks, toks)
        block = 128

        def norm(i, carry):
            at = pl.multiple_of(i * block, block)
            values = xg[chunk, pl.ds(at, block), :].astype(jnp.float32)
            centered = values - jnp.mean(values, axis=-1, keepdims=True)
            variance = jnp.mean(centered * centered, axis=-1, keepdims=True)
            out = centered * lax.rsqrt(variance + NORM_EPS) * small_sum[0:1, :] + small_sum[1:2, :]
            normed[pl.ds(pl.multiple_of(first + at, block), block), :] = out.astype(jnp.bfloat16)
            return carry

        lax.fori_loop(0, toks // block, norm, 0)
        span = pl.ds(first, toks)

        def turned(i, carry):
            at = pl.multiple_of(i * 2 * LANE, 2 * LANE)
            mixed = jnp.dot(normed[span, :], wq_full[:, pl.ds(at, 2 * LANE)], preferred_element_type=jnp.float32)
            mixed += wq_wide[0:1, pl.ds(at, 2 * LANE)]
            for j in range(2):
                u = mixed[:, j * LANE : (j + 1) * LANE]
                u = u * cos[span, :] + pltpu.roll(u, LANE // 2, 1) * sin[span, :]
                qkv[span, pl.ds(pl.multiple_of(at + j * LANE, LANE), LANE)] = u.astype(jnp.bfloat16)
            return carry

        lax.fori_loop(0, part // LANE, turned, 0)

        def plain(i, carry):
            at = pl.multiple_of(i * 2 * LANE, 2 * LANE)
            col = pl.ds(pl.multiple_of(2 * part + at, 2 * LANE), 2 * LANE)
            mixed = jnp.dot(normed[span, :], wq_full[:, col], preferred_element_type=jnp.float32)
            mixed += wq_wide[0:1, col]
            qkv[span, col] = mixed.astype(jnp.bfloat16)
            v_turn[pl.ds(at, 2 * LANE), span] = mixed.T.astype(jnp.bfloat16)
            return carry

        lax.fori_loop(0, part // (2 * LANE), plain, 0)

    project(seq)
    for step in range(1, size):
        g_x.recv(step)
        if step < size - 1:
            g_x.send(step + 1)
        if step == 1:
            g_w2.send(1)
            if last > 0:
                for s in (s_wp, s_w1):
                    s.recv(0)
                    s.send(1)

        def arrived(i, carry):
            chunk = seq + (2 * i - 1) * step
            pl.when((chunk >= 0) & (chunk < size))(lambda: project(chunk))
            return carry

        lax.fori_loop(0, 2, arrived, 0)

    def attend(chunk):
        def one(i, carry):
            head = i % group
            block = chunk * (toks // QBLK) + i // group
            span = pl.ds(pl.multiple_of(block * QBLK, QBLK), QBLK)
            at = pl.multiple_of(head * LANE, LANE)
            q = qkv[span, pl.ds(at, LANE)]
            k = qkv[:, pl.ds(pl.multiple_of(part + at, LANE), LANE)]
            scores = lax.dot_general(k, q, (((1,), (1,)), ((), ())), preferred_element_type=jnp.float32)
            scores = jnp.where(pic_col[...] == pic_row[:, span], scores, -1e30)
            top = jnp.max(scores, axis=0, keepdims=True)
            weights = jnp.exp2((scores - top) * EXP_SCALE)
            sums = jnp.sum(weights, axis=0, keepdims=True)
            out = jnp.dot(v_turn[pl.ds(at, LANE), :], weights.astype(jnp.bfloat16), preferred_element_type=jnp.float32)
            out = out / sums
            o_part[pl.ds(pl.multiple_of(head * HEAD_DIM, 8), HEAD_DIM), :] = out[:HEAD_DIM]
            lse[head, :, span] = top * EXP_SCALE + jnp.log2(sums)

            @pl.when(head == group - 1)
            def _():
                within = pl.multiple_of((i // group) * QBLK, QBLK)
                o_send[chunk, pl.ds(within, QBLK), :] = o_part[...].T.astype(jnp.bfloat16)

            return carry

        lax.fori_loop(0, group * (toks // QBLK), one, 0)

    o_part[...] = jnp.zeros_like(o_part)
    for step in range(1, size + 1):
        attend((seq + step) % size)
        if step < size:
            a_o.send(step)
        else:
            a_o.keep().start()
        if step < size:
            g_w2.recv(step)
            if step < size - 1:
                g_w2.send(step + 1)
            else:
                g_w2.keep().wait()
                s_w2.send(0)
        if step == 1:
            for stage in range(1, last):
                for s in (s_wp, s_w1):
                    s.recv(stage)
                    s.send(stage + 1)
    for stage in range(last):
        s_w2.recv(stage)
        s_w2.send(stage + 1)
    for s in (s_wp, s_w1, s_w2):
        s.finish()
    a_o.recv()
    for g in (g_small, g_wp, g_w1, g_w2, g_x, a_wq, a_o):
        g.finish()


def forward_call(mesh, x, wq, wp, w1, w2, small, cos, sin, pic_col, pic_row):
    rows, size = mesh.shape["row"], mesh.shape["seq"]
    toks, width = x.shape
    length = toks * size
    group = HEADS // size
    part = group * LANE
    shard = wp.shape[0]
    out_width = round_up(group * HEAD_DIM, LANE)
    total = rows * size
    bf, f32 = jnp.bfloat16, jnp.float32
    shape = jax.ShapeDtypeStruct
    return pl.pallas_call(
        functools.partial(forward_kernel, rows, size, shard, group),
        out_shape=(
            shape((total,) + wp.shape, bf),
            shape((total,) + w1.shape, bf),
            shape((total,) + w2.shape, bf),
            shape((size, toks, out_width), bf),
            shape(small.shape, f32),
            shape((length, width), bf),
            shape((length, 3 * part), bf),
            shape((width, 3 * part), bf),
            shape((group, 1, length), f32),
        ),
        in_specs=[ANY] * 6 + [VMEM] * 4,
        out_specs=(ANY,) * 4 + (VMEM,) * 5,
        scratch_shapes=[
            pltpu.VMEM((size, toks, width), bf),
            pltpu.VMEM((total,) + wq.shape[1:], bf),
            pltpu.VMEM((total,) + small.shape, bf),
            pltpu.VMEM((width, 3 * part), f32),
            pltpu.VMEM((part, length), bf),
            pltpu.VMEM((out_width, QBLK), f32),
            pltpu.VMEM((size, toks, out_width), bf),
            pltpu.SemaphoreType.DMA((512,)),
        ],
        compiler_params=pltpu.CompilerParams(
            collective_id=0, has_side_effects=True, vmem_limit_bytes=62 * 1024 * 1024
        ),
        name="forward",
    )(x, wq, wp, w1, w2, small, cos, sin, pic_col, pic_row)


def token_layout(lengths, widths, row_len):
    pic_ends = jnp.cumsum(lengths)
    pic_starts = pic_ends - lengths
    positions = jnp.arange(row_len, dtype=jnp.int32)
    picture = jnp.sum((positions[:, None] >= pic_ends[None, :]).astype(jnp.int32), axis=1)
    matches = picture[:, None] == jnp.arange(lengths.shape[0], dtype=jnp.int32)[None, :]
    first = jnp.sum(jnp.where(matches, pic_starts[None, :], 0), axis=1)
    grid_width = jnp.maximum(jnp.sum(jnp.where(matches, widths[None, :], 0), axis=1), 1)
    within = positions - first
    down = (within // grid_width).astype(jnp.float32)
    side = (within % grid_width).astype(jnp.float32)
    quarter = HEAD_DIM // 4
    frequency = 1.0 / 10000.0 ** (jnp.arange(quarter, dtype=jnp.float32) * 4.0 / HEAD_DIM)
    angles = jnp.concatenate([down[:, None] * frequency, side[:, None] * frequency], axis=-1)
    cosine, sine = jnp.cos(angles), jnp.sin(angles)
    gap = jnp.zeros((row_len, LANE // 2 - HALF), jnp.float32)
    return (
        picture,
        jnp.concatenate([cosine, gap, cosine, gap], axis=-1),
        jnp.concatenate([-sine, gap, sine, gap], axis=-1),
    )


def head_columns(values, size, pieces):
    a = values.shape[0]
    group = HEADS // size
    values = values.reshape(a, size, group, pieces, HEAD_DIM // pieces)
    values = jnp.pad(values, ((0, 0),) * 4 + ((0, (LANE - HEAD_DIM) // pieces),))
    return values.reshape(a, size, group * LANE).transpose(1, 0, 2)


def head_columns_back(values, pieces):
    size, a, lanes = values.shape
    group = lanes // LANE
    values = values.transpose(1, 0, 2).reshape(a, size, group, pieces, LANE // pieces)
    return values[..., : HEAD_DIM // pieces].reshape(a, HEADS * HEAD_DIM)


def qkv_columns(values, size):
    width = HEADS * HEAD_DIM
    return jnp.concatenate(
        [
            head_columns(values[:, :width], size, 2),
            head_columns(values[:, width : 2 * width], size, 2),
            head_columns(values[:, 2 * width :], size, 1),
        ],
        axis=-1,
    )


def layer_norm(values, norm_gain, norm_shift):
    centre = jnp.mean(values, axis=-1, keepdims=True)
    centered = values - centre
    variance = jnp.mean(centered * centered, axis=-1, keepdims=True)
    return centered * lax.rsqrt(variance + NORM_EPS) * norm_gain + norm_shift


def quick_gelu(values):
    return values * jax.nn.sigmoid(1.702 * values)


def pack_small(vectors, width, index, total):
    lines = []
    for values in vectors:
        full = values.shape[0] * total
        line = lax.dynamic_update_slice(jnp.zeros((full,), values.dtype), values, (index * values.shape[0],))
        lines.append(line.reshape(-1, width))
    lines = jnp.concatenate(lines, axis=0)
    return jnp.pad(lines, ((0, 16 - lines.shape[0]), (0, 0)))


def shards(
    mesh,
    activations,
    cotangent,
    pic_lengths,
    pic_widths,
    ln1_gain,
    ln1_bias,
    qkv_weight,
    qkv_bias,
    proj_weight,
    proj_bias,
    ln2_gain,
    ln2_bias,
    fc1_weight,
    fc1_bias,
    fc2_weight,
    fc2_bias,
):
    rows, size = mesh.shape["row"], mesh.shape["seq"]
    total = rows * size
    index = lax.axis_index("row") * size + lax.axis_index("seq")
    _, toks, width = activations.shape
    length = toks * size
    group = HEADS // size
    part = group * LANE
    shard = proj_weight.shape[0]
    bf, f32 = jnp.bfloat16, jnp.float32

    picture, cos, sin = token_layout(pic_lengths[0], pic_widths[0], length)
    small = pack_small((ln1_gain, ln1_bias, proj_bias, ln2_gain, ln2_bias, fc2_bias, fc1_bias), width, index, total)
    bias_line = lax.dynamic_update_slice(jnp.zeros((1, 3 * width), bf), qkv_bias[None], (0, index * qkv_bias.shape[0]))
    wq = jnp.concatenate([qkv_weight, bias_line], axis=0)
    wq = jnp.pad(qkv_columns(wq, size), ((0, 0), (0, round_up(shard + 3, 16) - shard - 1), (0, 0)))
    x = activations[0]
    wp, w1, w2, att, lines, normed, qkv, wq_full, lse = forward_call(
        mesh, x, wq, proj_weight, fc1_weight, fc2_weight, small, cos, sin, picture[:, None], picture[None, :]
    )
    wp, w1, w2 = (w.reshape(-1, w.shape[-1]) for w in (wp, w1, w2))
    b_proj, gain_two, shift_two, b_down = lines[2], lines[3], lines[4], lines[5]
    b_up = lines[6 : 6 + w1.shape[1] // width].reshape(-1)

    inputs = x.astype(f32)
    attended = jnp.concatenate([att[g, :, : group * HEAD_DIM] for g in range(size)], axis=-1)
    middle = inputs + jnp.dot(attended, wp, preferred_element_type=f32) + b_proj
    normed_two, norm_two_back = jax.vjp(layer_norm, middle, gain_two, shift_two)
    normed_two_low = normed_two.astype(bf)
    before = jnp.dot(normed_two_low, w1, preferred_element_type=f32) + b_up
    activated, gelu_back = jax.vjp(quick_gelu, before)
    activated_low = activated.astype(bf)
    result = jnp.dot(activated_low, w2, preferred_element_type=f32) + b_down
    layer_out = (middle + result).astype(bf)

    grad_out = cotangent[0]
    grad_out_wide = grad_out.astype(f32)
    grad_down = jnp.dot(activated_low.T, grad_out, preferred_element_type=f32)
    grad_down_bias = jnp.sum(grad_out_wide, axis=0)
    (grad_before,) = gelu_back(jnp.dot(grad_out, w2.T, preferred_element_type=f32))
    grad_before_low = grad_before.astype(bf)
    grad_up_bias = jnp.sum(grad_before_low.astype(f32), axis=0)
    grad_up = jnp.dot(normed_two_low.T, grad_before_low, preferred_element_type=f32)
    grad_normed_two = jnp.dot(grad_before_low, w1.T, preferred_element_type=f32)
    grad_middle, grad_gain_two, grad_shift_two = norm_two_back(grad_normed_two)
    grad_middle = grad_middle + grad_out_wide
    grad_branch = grad_middle.astype(bf)
    grad_proj_bias = jnp.sum(grad_branch.astype(f32), axis=0)
    grad_proj = jnp.dot(attended.T, grad_branch, preferred_element_type=f32)
    grad_attended = jnp.dot(grad_branch, wp.T, preferred_element_type=f32).astype(bf)

    grad_att = lax.all_to_all(
        grad_attended.reshape(toks, size, group * HEAD_DIM), "seq", split_axis=1, concat_axis=0, tiled=True
    ).reshape(length, group, HEAD_DIM)
    heads = qkv.reshape(length, 3, group, LANE)
    q, k, v = heads[:, 0], heads[:, 1], heads[:, 2, :, :HEAD_DIM]
    scores = jnp.einsum("khe,qhe->hkq", k, q, preferred_element_type=f32)
    scores = jnp.where((picture[:, None] == picture[None, :])[None], scores, -1e30)
    probs = jnp.exp2(scores * EXP_SCALE - lse)
    grad_probs = jnp.einsum("khe,qhe->hkq", v, grad_att, preferred_element_type=f32)
    delta = jnp.sum(probs * grad_probs, axis=1, keepdims=True)
    grad_scores = (probs * (grad_probs - delta)).astype(bf)
    grad_q = jnp.einsum("hkq,khe->qhe", grad_scores, k, preferred_element_type=f32) * SCALE
    grad_k = jnp.einsum("hkq,qhe->khe", grad_scores, q, preferred_element_type=f32) * SCALE
    grad_v = jnp.einsum("hkq,qhe->khe", probs.astype(bf), grad_att, preferred_element_type=f32)
    grad_v = jnp.pad(grad_v, ((0, 0), (0, 0), (0, LANE - HEAD_DIM)))

    def unturn(g):
        return g * cos[:, None] + jnp.roll(g * sin[:, None], LANE // 2, axis=-1)

    grad_mixed = jnp.concatenate(
        [g.reshape(length, part) for g in (unturn(grad_q), unturn(grad_k), grad_v)], axis=-1
    ).astype(bf)
    grad_normed = jnp.dot(grad_mixed, wq_full.T, preferred_element_type=f32).astype(bf)
    grad_normed = lax.psum_scatter(grad_normed, "seq", scatter_dimension=0, tiled=True).astype(f32)
    grad_qkv = jnp.dot(normed.T, grad_mixed, preferred_element_type=f32).astype(bf)
    grad_qkv = lax.psum_scatter(grad_qkv, "row", scatter_dimension=0, tiled=True).reshape(size, shard, 3 * part)
    grad_qkv = lax.all_to_all(grad_qkv, "seq", split_axis=0, concat_axis=0, tiled=True).astype(f32)

    def natural(g):
        return jnp.concatenate(
            [
                head_columns_back(g[:, :, :part], 2),
                head_columns_back(g[:, :, part : 2 * part], 2),
                head_columns_back(g[:, :, 2 * part :], 1),
            ],
            axis=-1,
        )

    grad_qkv = natural(grad_qkv)
    grad_bias = jnp.sum(grad_mixed.astype(f32), axis=0)
    grad_bias = natural(lax.all_gather(lax.psum(grad_bias, "row"), "seq")[:, None, :])[0]
    grad_qk = lax.dynamic_slice_in_dim(grad_bias[: 2 * width], index * 2 * shard, 2 * shard)
    grad_value = lax.dynamic_slice_in_dim(grad_bias[2 * width :], index * shard, shard)
    _, norm_one_back = jax.vjp(layer_norm, inputs, lines[0], lines[1])
    grad_inputs, grad_gain_one, grad_shift_one = norm_one_back(grad_normed)
    grad_acts = (grad_inputs + grad_middle).astype(bf)

    def owned(values):
        return lax.psum_scatter(values, ("row", "seq"), scatter_dimension=0, tiled=True)

    def owned_low(values):
        return owned(values.astype(bf)).astype(f32)

    return (
        layer_out[None],
        grad_acts[None],
        owned(grad_gain_one),
        owned(grad_shift_one),
        grad_qkv,
        grad_qk,
        grad_value,
        owned_low(grad_proj),
        owned(grad_proj_bias),
        owned(grad_gain_two),
        owned(grad_shift_two),
        owned_low(grad_up),
        owned(grad_up_bias),
        owned_low(grad_down),
        owned(grad_down_bias),
    )


def solution(mesh):
    one, two = P(("row", "seq")), P(("row", "seq"), None)
    tokens = P("row", "seq", None)
    return jax.shard_map(
        functools.partial(shards, mesh),
        mesh=mesh,
        in_specs=(tokens, tokens, P("row", None), P("row", None), one, one, two, one, two, one, one, one, two, one, two, one),
        out_specs=(tokens, tokens, one, one, two, one, one, two, one, one, one, two, one, two, one),
        check_vma=False,
    )
```

time: 2620 us -> 1550 us (0.59)
  waiting for transfers between devices: 2070 us -> 696 us
  Pallas kernels: 0 us -> 311 us
  other arithmetic: 140 us -> 92.4 us
  local copies, waits for them, and re-layouts: 45.7 us -> 75 us
  blocking collectives: 43.6 us -> 72.7 us
    reduce_scatter x5, waiting for transfers between devices: 1650 us -> 691 us  [the longest x3 605 us: owned(): lax.psum_scatter(values, ('row', 'seq'), scatter_dimension=0, tiled=True)]
    all_gather x6 -> x0, waiting for transfers between devices: 365 us -> none  [the longest x1 94 us: shards(): lax.all_gather(fc1_weight, ('row', 'seq'), axis=0, tiled=True)]
    pallas_call x0 -> x1, Pallas kernels: none -> 311 us  [forward_call(): pl.pallas_call(functools.partial(forward_kernel, rows, size, shard, group...]
    unnamed x13 -> x5, waiting for transfers between devices: 55 us -> 0.08 us
    reduce_sum x6 -> x4, other arithmetic: 32.1 us -> 4.8 us  [the longest x1 3.41 us: shards(): grad_bias = jnp.sum(grad_mixed.astype(f32), axis=0)]
    dot_general x22 -> x16, matrix products: 303 us -> 278 us  [the longest x1 51.6 us: shards(): scores = jnp.einsum('khe,qhe->hkq', k, q, preferred_element_type=f32)]
    convert_element_type x12 -> x6, other arithmetic: 71.9 us -> 60 us  [the longest x1 53.2 us: shards(): grad_scores = (probs * (grad_probs - delta)).astype(bf)]
  transfers between devices with their start and end apart: 12 -> 7, of which waited for: 12 -> 5; matrix products, arithmetic and copies ran while one was open for 9% -> 8% of each run, Pallas kernels for 0% -> 0%
where the time goes in v1:
time: 1550 us
  waiting for transfers between devices  696 us (45%)
  Pallas kernels  311 us (20%)
  matrix products  278 us (18%)
  other arithmetic  92.4 us (6%)
  local copies, waits for them, and re-layouts  75 us (5%)
  blocking collectives  72.7 us (5%)
    reduce_scatter x3, waiting for transfers between devices, owned(): lax.psum_scatter(values, ('row', 'seq'), scatter_dimension=0, tiled=True)  605 us
    pallas_call x1, Pallas kernels, forward_call(): pl.pallas_call(functools.partial(forward_kernel, rows, size, shard, group...  311 us
    reduce_scatter x1, waiting for transfers between devices, shards(): lax.psum_scatter(grad_normed, 'seq', scatter_dimension=0, tiled=True)  86.5 us
    convert_element_type x1, other arithmetic, shards(): grad_scores = (probs * (grad_probs - delta)).astype(bf)  53.2 us
    dot_general x1, matrix products, shards(): scores = jnp.einsum('khe,qhe->hkq', k, q, preferred_element_type=f32)  51.6 us
    unnamed x1, blocking collectives  45.8 us
  transfers between devices with their start and end apart: 7, of which 5 were waited for; matrix products, arithmetic and copies ran while one was open for 8% of the time, Pallas kernels for 0%

profile of v1, /device:TPU:0, one launch (start us, length us, event | category | flops | bytes accessed | tf_op | source)
XLA Modules:
  0.0 1548.4 jit_solution(2173568630441894956)
XLA Ops:
  28.2 311.2 %forward.1 = (bf16[32,40,1280]{2,1,0:T(8,128)(2,1)}, bf16[32,40,5120]{2,1,0:T(8,128)(2,1)}, bf16[32,160,1280]{2,1,0:T(8,128)(2,1)}, bf16[4,512,384]{2,1,0:T(8,12...) custom-call(bf16[512,1280]{1,0:T(8,128)(2,1)} %bitcast.158, ...), custom_call_target="tpu_custom_call" | custom-call | tf_op jit(solution)/shard_map/forward/pallas_call | solution.py:417
  346.3 4.3 fusion.61
  351.1 22.2 %fusion.55 = f32[512,5120]{1,0:T(8,128)} fusion(bf16[1280,5120]{1,0:T(8,128)(2,1)} %bitcast.194, f32[512,1280]{1,0:T(8,128)S(1)} %get-tuple-element.98, f32[1280]{0:T(1024)S(1)} %get-tuple-element.43, f32[1280]{0:T(1024)S(1)} %get-tuple-element.44, f32[512]{0:T(512)S(1)} %fusion.49, f32[512]{0:T(512)S(1)} %broadcast_multiply_fusion.5), kind=kOutput, calls=%fused_computation.152 | convolution fusion | flops 6714163200 | bytes 26228736 | tf_op jit(solution)/shard_map/dot_general | solution.py:567
  373.3 14.9 convert_reduce_fusion.1
  388.2 15.0 multiply_reduce_fusion.1
  412.5 3.8 all-to-all-start
  419.1 11.7 reshape.307
  435.3 4.0 fusion.58
  439.3 4.2 broadcast_compare_fusion
  443.5 4.9 all-to-all-done
  453.5 24.4 %fusion.32 = f32[4,2048,2048]{2,1,0:T(8,128)} fusion(bf16[2048,4,80]{0,2,1:T(8,128)(2,1)S(1)} %reshape.309, bf16[2048,1,4,80]{0,3,2,1:T(8,128)(2,1)} %copy.122), kind=kOutput, calls=%fused_computation.75 | convolution fusion | flops 2684354560 | bytes 69730304 | tf_op jit(solution)/shard_map/khe,qhe->hkq/dot_general | solution.py:597
  477.9 51.6 %multiply_reduce_fusion = (f32[4,2048]{1,0:T(4,128)S(1)}, f32[4,2048,2048]{2,1,0:T(8,128)}) fusion(f32[4,2048,2048]{2,1,0:T(8,128)} %fusion.32, f32[4,2048]{1,0:T(4,128)S(1)} %bitcast.178, bf16[2048,1,4,128]{3,2,1,0:T(4,128)(2,1)} %get-tuple-element.63, bf16[2048,1,4,128]{3,2,1,0:T(4,128)(2,1)S(1)} %get-tuple-element.64, ...), kind=kOutput, calls=%fused_computation.1 | convolution fusion | flops 4395622400 | bytes 142671872 | tf_op jit(solution)/shard_map/khe,qhe->hkq/dot_general | solution.py:594
  529.5 24.5 %fusion.23 = bf16[2048,4,80]{0,2,1:T(8,128)(2,1)} fusion(bf16[2048,4,80]{0,2,1:T(8,128)(2,1)S(1)} %reshape.309, f32[4,2048,2048]{2,1,0:T(8,128)} %get-tuple-element.101), kind=kOutput, calls=%fused_computation.62 | convolution fusion | flops 2701787136 | bytes 69730304 | tf_op jit(solution)/shard_map/hkq,qhe->khe/dot_general | solution.py:602
  553.9 53.2 %multiply_convert_fusion = bf16[4,2048,2048]{2,1,0:T(8,128)(2,1)} fusion(f32[4,2048,2048]{2,1,0:T(8,128)} %get-tuple-element.101, f32[4,2048,2048]{2,1,0:T(8,128)} %fusion.32, f32[4,2048]{1,0:T(4,128)S(1)} %get-tuple-element.100), kind=kLoop, calls=%fused_computation | loop fusion | flops 50331648 | bytes 167804928 | tf_op jit(solution)/shard_map/convert_element_type | solution.py:599
  607.1 19.3 %fusion.27 = f32[4,128,2048]{2,1,0:T(8,128)} fusion(bf16[4,2048,2048]{2,1,0:T(8,128)(2,1)} %multiply_convert_fusion, bf16[2048,1,4,128]{3,2,1,0:T(4,128)(2,1)} %get-tuple-element.63), kind=kOutput, calls=%fused_computation.66 | convolution fusion | flops 4294967296 | bytes 39845888 | tf_op jit(solution)/shard_map/hkq,qhe->khe/dot_general | solution.py:601
  626.4 21.4 %bitcast_multiply_fusion.4 = (f32[2048,4,128]{0,2,1:T(8,128)}, f32[2048,4,128]{0,2,1:T(8,128)}, f32[4,128,2048]{2,1,0:T(8,128)}) fusion(f32[2048,128]{0,1:T(8,128)S(1)} %copy-done.6, f32[4,128,2048]{2,1,0:T(8,128)} %fusion.27, bf16[4,2048,2048]{2,1,0:T(8,128)(2,1)} %multiply_convert_fusion, bf16[2048,1,4,128]{3,2,1,0:T(4,128)(2,1)S(1)} %get-tuple-element.64), kind=kOutput, calls=%fused_computation.29 | convolution fusion | flops 4297064448 | bytes 53477376 | tf_op jit(solution)/shard_map/hkq,khe->qhe/dot_general | solution.py:600
  660.1 14.5 convolution_convert_fusion.4
  675.9 4.9 convolution_convert_fusion.2
  680.9 13.4 convolution_convert_fusion.3
  696.0 16.4 %convolution_convert_fusion = bf16[5120,1280]{1,0:T(8,128)(2,1)} fusion(bf16[1,512,1280]{2,1,0:T(8,128)(2,1)S(1)} %copy-done.17, f32[512,5120]{1,0:T(8,128)} %fusion.55, f32[5120]{0:T(1024)S(1)} %copy-done.32), kind=kOutput, calls=%fused_computation.5 | convolution fusion | flops 6735790080 | bytes 24924160 | tf_op jit(solution)/shard_map/dot_general | solution.py:575
  714.2 12.9 convolution_convert_fusion.1
  728.7 16.3 %fusion.16 = bf16[1,512,1280]{2,1,0:T(8,128)(2,1)} fusion(f32[512,1280]{1,0:T(8,128)} %copy-done.9, bf16[5120,1280]{1,0:T(8,128)(2,1)} %bitcast.190, f32[1280]{0:T(1024)S(1)} %copy-done.40, f32[512,5120]{1,0:T(8,128)} %fusion.55, f32[5120]{0:T(1024)S(1)} %copy-done.32), kind=kOutput, calls=%fused_computation.51 | convolution fusion | flops 6731202560 | bytes 27550720 | tf_op jit(solution)/shard_map/dot_general | solution.py:570
  745.0 4.1 all-to-all-start.1
  749.1 3.4 convert_reduce_fusion
  752.6 13.5 psum.7
  766.1 13.4 all-gather
  781.2 91.5 %reduce-scatter.10.cloned.1.call-done = bf16[40,1280]{1,0:T(8,128)(2,1)} async-done(((bf16[1280,1280]{1,0:T(8,128)(2,1)}), bf16[40,1280]{1,0:T(8,128)(2,1)}) %reduce-scatter.10.cloned.1.call-update) | async-done | bytes 102416 | tf_op jit(solution)/shard_map/reduce_scatter | solution.py:637
  880.4 86.5 %reduce-scatter.6.cloned.1.call-done = bf16[512,1280]{1,0:T(8,128)(2,1)} async-done(((bf16[2048,1280]{1,0:T(8,128)(2,1)}), bf16[512,1280]{1,0:T(8,128)(2,1)}) %reduce-scatter.6.cloned.1.call-update) | async-done | bytes 1310736 | tf_op jit(solution)/shard_map/reduce_scatter | solution.py:612
  970.8 45.8 %all-reduce.13 = (f32[1280]{0:T(1024)S(1)}, f32[1280]{0:T(1024)S(1)}, f32[1280]{0:T(1024)S(1)}, f32[1280]{0:T(1024)S(1)}, f32[1280]{0:T(1024)S(1)}, /*index=5*/f32[5120]{0:T(1024)S(1)}, f32[1280]{0:T(1024)S(1)}) all-reduce(f32[1280]{0:T(1024)S(1)} %get-tuple-element.35, ...), channel_id=3, replica_groups=mesh['row'=8,'seq'=4] {'row','seq'}, use_global_device_ids=true, to_apply=%region_15.16.clone | all-reduce | flops 12800 | bytes 102400
  1020.7 3.7 fusion.34
  1024.4 229.7 %reduce-scatter.14.cloned.1.call-done = bf16[160,1280]{1,0:T(8,128)(2,1)} async-done(((bf16[5120,1280]{1,0:T(8,128)(2,1)}), bf16[160,1280]{1,0:T(8,128)(2,1)}) %reduce-scatter.14.cloned.1.call-update) | async-done | bytes 409616 | tf_op jit(solution)/shard_map/reduce_scatter | solution.py:637
  1256.1 283.5 %reduce-scatter.12.cloned.1.call-done = bf16[40,5120]{1,0:T(8,128)(2,1)} async-done(((bf16[1280,5120]{1,0:T(8,128)(2,1)}), bf16[40,5120]{1,0:T(8,128)(2,1)}) %reduce-scatter.12.cloned.1.call-update) | async-done | bytes 409616 | tf_op jit(solution)/shard_map/reduce_scatter | solution.py:637
  (235 shorter events, 89.3 us)
Async XLA Ops:
  8.8 10.0 copy-start.23
  10.5 5.8 copy-start.45
  341.9 9.1 copy-start.41
  341.9 61.2 %copy-start.29 = (f32[1280]{0:T(1024)}, f32[1280]{0:T(1024)S(1)}, u32[]{:S(2)}) copy-start(f32[1280]{0:T(1024)S(1)} %get-tuple-element.44) | copy-start | bytes 15364
  341.9 4.4 copy-start.4
  343.6 29.7 %copy-start.31 = (f32[5120]{0:T(1024)}, f32[5120]{0:T(1024)S(1)}, u32[]{:S(2)}) copy-start(f32[5120]{0:T(1024)S(1)} %add.166) | copy-start | bytes 61444
  350.6 22.7 %copy-start.9 = (f32[512,1280]{1,0:T(8,128)}, f32[512,1280]{1,0:T(8,128)S(1)}, u32[]{:S(2)}) copy-start(f32[512,1280]{1,0:T(8,128)S(1)} %get-tuple-element.98) | copy-start | bytes 7864324
  350.6 52.6 %copy-start.36 = (f32[512]{0:T(512)}, f32[512]{0:T(512)S(1)}, u32[]{:S(2)}) copy-start(f32[512]{0:T(512)S(1)} %broadcast_multiply_fusion.5) | copy-start | bytes 6148
  350.6 22.6 %slice-start = ((s8[13107200]{0:T(1024)(128)(4,1)}), s8[4194304]{0:T(1024)(128)(4,1)S(1)}, s32[]{:S(2)}) async-start(s8[13107200]{0:T(1024)(128)(4,1)} %bitcast.191), calls=%async_computation.12 | async-start | bytes 8388608
  351.0 52.1 %copy-start.43 = (f32[512]{0:T(512)}, f32[512]{0:T(512)S(1)}, u32[]{:S(2)}) copy-start(f32[512]{0:T(512)S(1)} %fusion.49) | copy-start | bytes 6148
  351.1 22.2 %copy-start.16 = (bf16[1,512,1280]{2,1,0:T(8,128)(2,1)S(1)}, bf16[1,512,1280]{2,1,0:T(8,128)(2,1)}, u32[]{:S(2)}) copy-start(bf16[1,512,1280]{2,1,0:T(8,128)(2,1)} %param.17) | copy-start | bytes 3932164
  351.1 22.2 %slice-start.1 = ((s8[13107200]{0:T(1024)(128)(4,1)}), s8[4194304]{0:T(1024)(128)(4,1)S(1)}, s32[]{:S(2)}) async-start(s8[13107200]{0:T(1024)(128)(4,1)} %bitcast.191), calls=%async_computation.13 | async-start | bytes 8388608
  351.1 22.2 %slice-start.2 = ((s8[13107200]{0:T(1024)(128)(4,1)}), s8[4194304]{0:T(1024)(128)(4,1)S(1)}, s32[]{:S(2)}) async-start(s8[13107200]{0:T(1024)(128)(4,1)} %bitcast.191), calls=%async_computation.14 | async-start | bytes 8388608
  351.1 22.2 %slice-start.3 = ((s8[13107200]{0:T(1024)(128)(4,1)}), s8[524288]{0:T(1024)(128)(4,1)S(1)}, s32[]{:S(2)}) async-start(s8[13107200]{0:T(1024)(128)(4,1)} %bitcast.191), calls=%async_computation.15 | async-start | bytes 1048576
  373.3 14.9 copy-start.10
  411.1 5.3 copy-start.19
  412.5 5.2 copy-start.18
  412.5 35.8 %all-to-all-start = ((bf16[512,4,320]{0,2,1:T(8,128)(2,1)}), bf16[512,4,320]{0,2,1:T(8,128)(2,1)S(1)}, u32[]{:S(2)}, u32[]{:S(2)}) async-start(bf16[512,4,320]{0,2,1:T(8,128)(2,1)} %bitcast.31), calls=%async_computation | async-start | bytes 2621440 | tf_op jit(solution)/shard_map/all_to_all | solution.py:589
  416.4 328.6 %reduce-scatter.8.cloned.1.call-start = ((), (), s32[]{:S(2)}) async-start(), calls=%async_computation.8 | async-start | bytes 4423680 | tf_op jit(solution)/shard_map/reduce_scatter | solution.py:614
  435.3 4.0 copy-start.24
  607.1 19.3 %copy-start.6 = (f32[2048,128]{0,1:T(8,128)S(1)}, f32[2048,128]{0,1:T(8,128)}, u32[]{:S(2)}) copy-start(f32[2048,128]{0,1:T(8,128)} %copy.112) | copy-start | bytes 3145732
  651.3 4.3 copy-start.2
  651.8 4.0 copy-start.20
  652.1 28.8 %copy-start.12 = (bf16[2048,4,128]{0,2,1:T(8,128)(2,1)}, bf16[2048,4,128]{0,2,1:T(8,128)(2,1)S(1)}, u32[]{:S(2)}) copy-start(bf16[2048,4,128]{0,2,1:T(8,128)(2,1)S(1)} %pad.29) | copy-start | bytes 6291460
  674.6 198.0 %reduce-scatter.10.cloned.1.call-start = ((), (), s32[]{:S(2)}) async-start(), calls=%async_computation.9 | async-start | bytes 3379200 | tf_op jit(solution)/shard_map/reduce_scatter | solution.py:637
  680.9 286.0 %reduce-scatter.6.cloned.1.call-start = ((), (), s32[]{:S(2)}) async-start(), calls=%async_computation.7 | async-start | bytes 6553600 | tf_op jit(solution)/shard_map/reduce_scatter | solution.py:612
  694.4 559.8 %reduce-scatter.14.cloned.1.call-start = ((), (), s32[]{:S(2)}) async-start(), calls=%async_computation.11 | async-start | bytes 13516800 | tf_op jit(solution)/shard_map/reduce_scatter | solution.py:637
  712.5 827.2 %reduce-scatter.12.cloned.1.call-start = ((), (), s32[]{:S(2)}) async-start(), calls=%async_computation.10 | async-start | bytes 13516800 | tf_op jit(solution)/shard_map/reduce_scatter | solution.py:637
  728.7 20.5 %copy-start.13 = (bf16[2048,4,128]{0,2,1:T(8,128)(2,1)S(1)}, bf16[2048,4,128]{0,2,1:T(8,128)(2,1)}, u32[]{:S(2)}) copy-start(bf16[2048,4,128]{0,2,1:T(8,128)(2,1)} %copy-done.12) | copy-start | bytes 6291460
  745.0 129.3 %all-to-all-start.1 = ((bf16[4,40,1536]{2,1,0:T(8,128)(2,1)}), bf16[4,40,1536]{2,1,0:T(8,128)(2,1)}, u32[]{:S(2)}, u32[]{:S(2)}) async-start(bf16[4,40,1536]{2,1,0:T(8,128)(2,1)} %bitcast.173), calls=%async_computation.3 | async-start | bytes 983040 | tf_op jit(solution)/shard_map/all_to_all | solution.py:615
  877.5 89.4 %copy-start.25 = (f32[1280]{0:T(1024)S(1)}, f32[1280]{0:T(1024)}, u32[]{:S(2)}) copy-start(f32[1280]{0:T(1024)} %get-tuple-element.41) | copy-start | bytes 15364
  966.9 53.8 %copy-start.35 = (f32[512]{0:T(512)S(1)}, f32[512]{0:T(512)}, u32[]{:S(2)}) copy-start(f32[512]{0:T(512)} %copy-done.34) | copy-start | bytes 6148
  (32 other events, 76.3 us)
Sparse Core Ops, SparseCore 0:
  674.7 48.3 reduce-scatter.7
  725.6 147.0 reduce-scatter.9
  875.0 91.8 reduce-scatter.5
  969.0 285.0 reduce-scatter.13
  1256.4 283.1 reduce-scatter.11

commit v2 on v1

--- a/solution.py
+++ b/solution.py
@@ -230,8 +230,8 @@
 def forward_kernel(
     rows, size, shard, group,
     x, wq, wp, w1, w2, small, cos, sin, pic_col, pic_row,
-    wp_all, w1_all, w2_all, att, small_sum, normed, qkv, wq_full, lse,
-    xg, wq_buf, small_buf, wq_wide, v_turn, o_part, o_send, sem_ref,
+    wp_all, w1_all, w2_all, att, small_sum, xg, qkv, wq_full, lse,
+    normed, wq_buf, small_buf, wq_wide, v_turn, o_part, o_send, sem_ref,
 ):
     row, seq = lax.axis_index("row"), lax.axis_index("seq")
     toks, width = x.shape
@@ -422,7 +422,7 @@
             shape((total,) + w2.shape, bf),
             shape((size, toks, out_width), bf),
             shape(small.shape, f32),
-            shape((length, width), bf),
+            shape((size, toks, width), bf),
             shape((length, 3 * part), bf),
             shape((width, 3 * part), bf),
             shape((group, 1, length), f32),
@@ -430,7 +430,7 @@
         in_specs=[ANY] * 6 + [VMEM] * 4,
         out_specs=(ANY,) * 4 + (VMEM,) * 5,
         scratch_shapes=[
-            pltpu.VMEM((size, toks, width), bf),
+            pltpu.VMEM((length, width), bf),
             pltpu.VMEM((total,) + wq.shape[1:], bf),
             pltpu.VMEM((total,) + small.shape, bf),
             pltpu.VMEM((width, 3 * part), f32),
@@ -494,6 +494,521 @@
         ],
         axis=-1,
     )
+
+
+def add_blocks(out, first, second, count, block, first_map, second_map):
+    def body(a, b, o):
+        o[...] = (a[...].astype(jnp.float32) + b[...].astype(jnp.float32)).astype(o.dtype)
+
+    pltpu.emit_pipeline(
+        body,
+        grid=(count,),
+        in_specs=[pl.BlockSpec(block, first_map), pl.BlockSpec(block, second_map)],
+        out_specs=[pl.BlockSpec(block, lambda i: (i, 0, 0))],
+    )(first, second, out)
+
+
+class Reduce:
+    def __init__(self, src, core, acc, come, done, row, seq, rows, size, sems, in_vmem):
+        self.src, self.core, self.acc, self.come, self.done = src, core, acc, come, done
+        self.row, self.seq, self.size, self.in_vmem = row, seq, size, in_vmem
+        bits = [1 << i for i in range(1, rows.bit_length() - 1)]
+        self.orders = (bits, bits[::-1])
+        self.stages = len(bits)
+        self.chips = rows // 2
+        self.half = src.shape[2] // 2
+        self.block = (size, src.shape[1], self.half)
+        self.core_sems = [(sems.take(1)[0], sems.take(1)[0]) for _ in range(self.chips)]
+        self.sems = [[(sems.take(1)[0], sems.take(1)[0]) for _ in bits] for _ in range(2)]
+
+    def _core_copies(self):
+        size = self.size
+        other = flip(self.row, 1)
+        for chip in range(self.chips):
+            theirs = 2 * chip + other % 2
+            yield remote(
+                self.src.at[pl.ds(theirs * size, size)],
+                self.core.at[pl.ds(chip * size, size)],
+                *self.core_sems[chip],
+                other,
+                self.seq,
+            )
+
+    def core_send(self):
+        for copy in self._core_copies():
+            copy.start()
+
+    def _chip(self, half, i):
+        chip = self.row // 2
+        for k in range(self.stages):
+            bit = self.orders[half][self.stages - 1 - k] // 2
+            chip = chip + ((i // (1 << k)) % 2) * (flip(chip, bit) - chip)
+        return chip
+
+    def core_add(self):
+        size = self.size
+        for copy in self._core_copies():
+            copy.wait_recv()
+        core = self.row % 2
+        for half in range(2):
+            if self.in_vmem:
+                cols = pl.ds(half * self.half, self.half)
+
+                def body(i, carry, half=half, cols=cols):
+                    chip, z = self._chip(half, i // size), i % size
+                    mine = self.src[(2 * chip + core) * size + z, :, cols].astype(jnp.float32)
+                    total = mine + self.core[chip * size + z, :, cols].astype(jnp.float32)
+                    self.acc[half][i] = total.astype(self.acc[half].dtype)
+                    return carry
+
+                lax.fori_loop(0, self.chips * size, body, 0)
+            else:
+                add_blocks(
+                    self.acc[half],
+                    self.src,
+                    self.core,
+                    self.chips,
+                    self.block,
+                    lambda i, half=half: (2 * self._chip(half, i) + core, 0, half),
+                    lambda i, half=half: (self._chip(half, i), 0, half),
+                )
+
+    def _held(self, half, stage):
+        return self.acc[half] if stage == 0 else self.done[half][stage - 1]
+
+    def _stage_copy(self, half, stage):
+        count = (self.chips >> (stage + 1)) * self.size
+        return remote(
+            self._held(half, stage).at[pl.ds(count, count)],
+            self.come[half][stage],
+            *self.sems[half][stage],
+            flip(self.row, self.orders[half][stage]),
+            self.seq,
+        )
+
+    def stage_send(self, stage):
+        for half in range(2):
+            self._stage_copy(half, stage).start()
+
+    def stage_add(self, stage):
+        count = self.chips >> (stage + 1)
+        for half in range(2):
+            self._stage_copy(half, stage).wait_recv()
+            held, come, done = self._held(half, stage), self.come[half][stage], self.done[half][stage]
+            if self.in_vmem:
+
+                def body(i, carry, held=held, come=come, done=done):
+                    total = held[i].astype(jnp.float32) + come[i].astype(jnp.float32)
+                    done[i] = total.astype(done.dtype)
+                    return carry
+
+                lax.fori_loop(0, count * self.size, body, 0)
+            else:
+                plain = lambda i: (i, 0, 0)
+                add_blocks(done, held, come, count, self.block, plain, plain)
+
+    @property
+    def kept(self):
+        return [self._held(half, self.stages) for half in range(2)]
+
+    def finish(self):
+        for copy in self._core_copies():
+            copy.wait_send()
+        for half in range(2):
+            for stage in range(self.stages):
+                self._stage_copy(half, stage).wait_send()
+
+
+def reduce_shapes(src, rows, size):
+    a, b = src[1], src[2] // 2
+    chips = rows // 2
+    stages = rows.bit_length() - 2
+    shapes = [(chips * size, a, 2 * b)] + [(chips * size, a, b)] * 2
+    for _ in range(2):
+        for stage in range(stages):
+            shapes += [((chips >> (stage + 1)) * size, a, b)] * 2
+    return shapes + [(size, a, b)] * 2
+
+
+def reduce_refs(refs, rows):
+    stages = rows.bit_length() - 2
+    core, acc, rest = refs[0], refs[1:3], refs[3:-2]
+    come = [[rest[2 * (half * stages + j)] for j in range(stages)] for half in range(2)]
+    done = [[rest[2 * (half * stages + j) + 1] for j in range(stages)] for half in range(2)]
+    return (core, acc, come, done), refs[-2:]
+
+
+class ChainSum:
+    def __init__(self, part, slots, row, seq, size, sems):
+        self.part, self.slots = part, slots
+        self.row, self.seq, self.size = row, seq, size
+        self.sems = [[(sems.take(1)[0], sems.take(1)[0]) for _ in range(size - 1)] for _ in range(2)]
+
+    def _copy(self, way, step):
+        sign = 1 - 2 * way
+        peer = self.seq + sign
+        chunk = self.seq + sign * (self.size - step)
+        ok = (chunk >= 0) & (chunk < self.size) & (peer >= 0) & (peer < self.size)
+        slot = self.slots.at[way * (self.size - 1) + step - 1]
+        return ok, lambda: remote(self.part(chunk), slot, *self.sems[way][step - 1], self.row, peer)
+
+    def send(self, step):
+        for way in range(2):
+            ok, copy = self._copy(way, step)
+            pl.when(ok)(lambda copy=copy: copy().start())
+
+    def recv(self, step, use):
+        for way in range(2):
+            sign = 1 - 2 * way
+            source = self.seq - sign
+            chunk = self.seq + sign * (self.size - step - 1)
+            ok = (chunk >= 0) & (chunk < self.size) & (source >= 0) & (source < self.size)
+            slot = self.slots.at[way * (self.size - 1) + step - 1]
+
+            def take(way=way, chunk=chunk, slot=slot):
+                remote(slot, slot, *self.sems[way][step - 1], self.row, self.seq + 1 - 2 * way).wait_recv()
+                use(chunk, slot)
+
+            pl.when(ok)(take)
+
+    def finish(self):
+        for step in range(1, self.size):
+            for way in range(2):
+                ok, copy = self._copy(way, step)
+                pl.when(ok)(lambda copy=copy: copy().wait_send())
+
+
+def backward_kernel(rows, size, shard, group, counts, *refs):
+    refs = list(refs)
+
+    def take(count):
+        out = refs[:count]
+        del refs[:count]
+        return out
+
+    g2, g1, gp, gs, go, xg, qkv, cos, sin, pic_col, pic_row, wq_full, lse, small = take(14)
+    dx_out, dq_out, gs_out, g2_out, g1_out, gp_out = take(6)
+    slots = take(1)[0]
+    big = [take(counts) for _ in range(3)]
+    vm = [take(counts) for _ in range(2)]
+    (qkv_s, do_in, do_full, k_turn, gk_sum, gv_sum, gm, n_turn, x_chunk, dq, rows_sum, sem_ref, load_sem) = refs
+
+    row, seq = lax.axis_index("row"), lax.axis_index("seq")
+    length, part = qkv.shape[0], group * LANE
+    toks = length // size
+    width = xg.shape[2]
+    base = row * size
+    sems = Sems(sem_ref)
+    f32, bf = jnp.float32, jnp.bfloat16
+
+    a_do = Scatter(go, lambda j: do_in.at[j], row, seq, size, sems)
+    reducers, z_moves = [], []
+    for src, bufs, in_vmem in (
+        (g2, big[0], False), (g1, big[1], False), (gp, big[2], False), (gs, vm[0], True), (dq, vm[1], True),
+    ):
+        inner, z_refs = reduce_refs(bufs, rows)
+        r = Reduce(src, *inner, row, seq, rows, size, sems, in_vmem)
+        reducers.append(r)
+        z_moves.append(
+            [Scatter(kept, lambda j, to=to: to.at[j], row, seq, size, sems) for kept, to in zip(r.kept, z_refs)]
+        )
+    r2, r1, rp, rs, rq = reducers
+
+    def z_send(which):
+        for move in z_moves[which]:
+            move.send_all()
+
+    dx = ChainSum(lambda c: qkv_s.at[pl.ds(c * toks, toks), pl.ds(0, width)], slots, row, seq, size, sems)
+
+    greet(row, seq, rows, size)
+    a_do.send_all()
+    load_qkv = pltpu.make_async_copy(qkv, qkv_s.at[:, pl.ds(0, 3 * part)], load_sem.at[0])
+    load_qkv.start()
+    for r in (r2, r1, rp, rs):
+        r.core_send()
+    for r in (r2, r1, rp, rs):
+        r.core_add()
+        r.stage_send(0)
+    load_qkv.wait()
+    for i in range(0, part, LANE):
+        k_turn[pl.ds(i, LANE), :] = qkv_s[:, pl.ds(part + i, LANE)].astype(f32).T.astype(bf)
+    a_do.recv()
+
+    def widen(i, carry):
+        chunk, at = i // (toks // QBLK), (i % (toks // QBLK)) * QBLK
+        values = do_in[chunk, pl.ds(pl.multiple_of(at, QBLK), QBLK), :].astype(f32)
+        lanes = lax.broadcasted_iota(jnp.int32, (QBLK, LANE), 1)
+        for head in range(group):
+            first = head * HEAD_DIM
+            start = first // LANE * LANE
+            window = values[:, start : min(start + 2 * LANE, values.shape[1])]
+            shift = first - start
+            if shift:
+                window = pltpu.roll(window, window.shape[1] - shift, 1)
+            piece = jnp.where(lanes < HEAD_DIM, window[:, :LANE], 0.0)
+            do_full[pl.ds(pl.multiple_of(i * QBLK, QBLK), QBLK), pl.ds(head * LANE, LANE)] = piece.astype(bf)
+        return carry
+
+    lax.fori_loop(0, length // QBLK, widen, 0)
+
+    def unturn(grad, span):
+        return grad * cos[span, :] + pltpu.roll(grad * sin[span, :], LANE // 2, 1)
+
+    def head_back(head):
+        at = pl.multiple_of(head * LANE, LANE)
+        lane = pl.ds(at, LANE)
+        k_lane = pl.ds(pl.multiple_of(part + at, LANE), LANE)
+        v_lane = pl.ds(pl.multiple_of(2 * part + at, LANE), LANE)
+        gk_sum[...] = jnp.zeros_like(gk_sum)
+        gv_sum[...] = jnp.zeros_like(gv_sum)
+
+        def one(i, carry):
+            span = pl.ds(pl.multiple_of(i * QBLK, QBLK), QBLK)
+            q = qkv_s[span, lane]
+            do = do_full[span, lane]
+            scores = lax.dot_general(
+                qkv_s[:, k_lane], q, (((1,), (1,)), ((), ())), preferred_element_type=f32
+            )
+            probs = jnp.exp2(scores * EXP_SCALE - lse[head, :, span])
+            probs = jnp.where(pic_col[...] == pic_row[:, span], probs, 0.0)
+            gv_sum[...] += jnp.dot(probs.astype(bf), do, preferred_element_type=f32)
+            grad_probs = lax.dot_general(
+                qkv_s[:, v_lane], do, (((1,), (1,)), ((), ())), preferred_element_type=f32
+            )
+            delta = jnp.sum(probs * grad_probs, axis=0, keepdims=True)
+            grad_scores = (probs * (grad_probs - delta)).astype(bf)
+            gk_sum[...] += jnp.dot(grad_scores, q, preferred_element_type=f32)
+            gq = jnp.dot(k_turn[lane, :], grad_scores, preferred_element_type=f32).T
+            gm[span, lane] = unturn(gq * SCALE, span).astype(bf)
+            return carry
+
+        lax.fori_loop(0, length // QBLK, one, 0)
+
+        def close(i, carry):
+            span = pl.ds(pl.multiple_of(i * QBLK, QBLK), QBLK)
+            gm[span, k_lane] = unturn(gk_sum[span, :] * SCALE, span).astype(bf)
+            gm[span, v_lane] = gv_sum[span, :].astype(bf)
+            return carry
+
+        lax.fori_loop(0, length // QBLK, close, 0)
+
+    def heads_back(first, count):
+        def body(i, carry):
+            head_back(first + i)
+            return carry
+
+        lax.fori_loop(0, count, body, 0)
+
+    steps = []
+    for stage in range(r2.stages):
+        for which in (0, 1, 2, 3):
+
+            def step(which=which, stage=stage):
+                r = reducers[which]
+                r.stage_add(stage)
+                if stage + 1 < r.stages:
+                    r.stage_send(stage + 1)
+                else:
+                    z_send(which)
+
+            steps.append(step)
+    done_steps = 0
+    for head in range(group):
+        heads_back(head, 1)
+        upto = len(steps) * (head + 1) // group
+        for step in steps[done_steps:upto]:
+            step()
+        done_steps = upto
+
+    rows_sum[...] = jnp.zeros_like(rows_sum)
+
+    def chunk_back(chunk):
+        load = pltpu.make_async_copy(xg.at[chunk], x_chunk, load_sem.at[1])
+        load.start()
+        load.wait()
+        block = LANE
+
+        def one(i, carry):
+            at = pl.multiple_of(i * block, block)
+            span = pl.ds(pl.multiple_of(chunk * toks + at, block), block)
+            values = x_chunk[pl.ds(at, block), :].astype(f32)
+            centered = values - jnp.mean(values, axis=-1, keepdims=True)
+            variance = jnp.mean(centered * centered, axis=-1, keepdims=True)
+            hat = centered * lax.rsqrt(variance + NORM_EPS)
+            n_turn[:, span] = (hat * small[0:1, :] + small[1:2, :]).T.astype(bf)
+            mixed = gm[span, :]
+            grad = lax.dot_general(mixed, wq_full[...], (((1,), (1,)), ((), ())), preferred_element_type=f32)
+            rows_sum[0:1, pl.ds(0, 3 * part)] += jnp.sum(mixed.astype(f32), axis=0, keepdims=True)
+            rows_sum[1:2, pl.ds(0, width)] += jnp.sum(grad * hat, axis=0, keepdims=True)
+            rows_sum[2:3, pl.ds(0, width)] += jnp.sum(grad, axis=0, keepdims=True)
+            qkv_s[span, pl.ds(0, width)] = grad.astype(bf)
+            return carry
+
+        lax.fori_loop(0, toks // block, one, 0)
+
+    def far_chunks(distance):
+        def body(i, carry):
+            chunk = seq + (2 * i - 1) * distance
+            pl.when((chunk >= 0) & (chunk < size))(lambda: chunk_back(chunk))
+            return carry
+
+        lax.fori_loop(0, 2 if distance else 1, body, 0)
+
+    for step in range(1, size):
+        far_chunks(size - step)
+        if step == 1:
+            dx.send(1)
+    far_chunks(0)
+
+    lines = -(-width // (3 * part))
+    tall = width // 2
+    per = tall // shard
+    for i in range(2):
+
+        def columns(j, carry, i=i):
+            cols = pl.ds(pl.multiple_of(j * 2 * LANE, 2 * LANE), 2 * LANE)
+            grad = jnp.dot(n_turn[pl.ds(i * tall, tall), :], gm[:, cols], preferred_element_type=f32).astype(bf)
+            for s in range(per):
+                dq[i * per + s, pl.ds(0, shard), cols] = grad[s * shard : (s + 1) * shard]
+            return carry
+
+        lax.fori_loop(0, 3 * part // (2 * LANE), columns, 0)
+    tail = [rows_sum[0:1, pl.ds(0, 3 * part)]]
+    for line in (1, 2):
+        tail += [rows_sum[line : line + 1, pl.ds(k * 3 * part, 3 * part)] for k in range(lines)]
+    tail = jnp.concatenate(tail, axis=0).astype(bf)
+
+    def put_tail(i, carry):
+        dq[i, pl.ds(shard, tail.shape[0]), :] = tail
+        return carry
+
+    lax.fori_loop(0, rows * size, put_tail, 0)
+    rq.core_send()
+
+    def add_sum(chunk, slot):
+        load = pltpu.make_async_copy(slot, x_chunk, load_sem.at[1])
+        load.start()
+        load.wait()
+        span = pl.ds(pl.multiple_of(chunk * toks, toks), toks)
+        mine = qkv_s[span, pl.ds(0, width)].astype(f32)
+        qkv_s[span, pl.ds(0, width)] = (mine + x_chunk[...].astype(f32)).astype(bf)
+
+    for step in range(1, size):
+        if step == size - 1:
+            dx_out[...] = qkv_s[pl.ds(pl.multiple_of(seq * toks, toks), toks), pl.ds(0, width)].astype(f32)
+
+            def last_sum(chunk, slot):
+                load = pltpu.make_async_copy(slot, x_chunk, load_sem.at[1])
+                load.start()
+                load.wait()
+                dx_out[...] += x_chunk[...].astype(f32)
+
+        else:
+            dx.recv(step, add_sum)
+            dx.send(step + 1)
+        if step == 1:
+            rq.core_add()
+            rq.stage_send(0)
+        elif step == 2:
+            for stage in range(rq.stages):
+                rq.stage_add(stage)
+                if stage + 1 < rq.stages:
+                    rq.stage_send(stage + 1)
+            z_send(4)
+
+    def z_sum(which, out):
+        for half, move in enumerate(z_moves[which]):
+            move.recv()
+
+    z_buf = [reduce_refs(bufs, rows)[1] for bufs in big + vm]
+    for which, out in ((0, g2_out), (1, g1_out), (2, gp_out)):
+        z_sum(which, out)
+        half_cols = reducers[which].half
+        for half in range(2):
+
+            def body(a, o):
+                total = a[0].astype(f32)
+                for z in range(1, size):
+                    total += a[z].astype(f32)
+                o[...] = total
+
+            pltpu.emit_pipeline(
+                body,
+                grid=(1,),
+                in_specs=[pl.BlockSpec(reducers[which].block, lambda i: (0, 0, 0))],
+                out_specs=[pl.BlockSpec((reducers[which].block[1], half_cols), lambda i, half=half: (0, half))],
+            )(z_buf[which][half], out)
+    z_sum(3, None)
+    for half in range(2):
+        total = z_buf[3][half][0]
+        for z in range(1, size):
+            total += z_buf[3][half][z]
+        gs_out[:, pl.ds(half * LANE, LANE)] = total
+    z_sum(4, None)
+    for half in range(2):
+        dq_out[:, :, pl.ds(half * rq.half, rq.half)] = z_buf[4][half][...]
+    dx.recv(size - 1, last_sum)
+    for r in reducers:
+        r.finish()
+    for moves in z_moves:
+        for move in moves:
+            move.finish()
+    a_do.finish()
+    dx.finish()
+
+
+def backward_call(mesh, g2, g1, gp, gs, go, xg, qkv, cos, sin, pic_col, pic_row, wq_full, lse, small, tall):
+    rows, size = mesh.shape["row"], mesh.shape["seq"]
+    _, toks, width = xg.shape
+    length = toks * size
+    group = HEADS // size
+    part = group * LANE
+    shard = gp.shape[1]
+    total = rows * size
+    bf, f32 = jnp.bfloat16, jnp.float32
+    shape = jax.ShapeDtypeStruct
+    dq_shape = (total, tall, 3 * part)
+    big = [[shape(s, bf) for s in reduce_shapes(g.shape, rows, size)] for g in (g2, g1, gp)]
+    vm = [[pltpu.VMEM(s, t) for s in reduce_shapes(d, rows, size)] for d, t in ((gs.shape, f32), (dq_shape, bf))]
+    counts = len(vm[0])
+    outs = (
+        shape((toks, width), f32),
+        shape((size, tall, 3 * part), bf),
+        shape(gs.shape[1:], f32),
+        shape(g2.shape[1:], f32),
+        shape(g1.shape[1:], f32),
+        shape(gp.shape[1:], f32),
+        shape((2 * (size - 1), toks, width), bf),
+        *big[0], *big[1], *big[2],
+    )
+    wide = max(3 * part, width)
+    results = pl.pallas_call(
+        functools.partial(backward_kernel, rows, size, shard, group, counts),
+        out_shape=outs,
+        in_specs=[ANY] * 3 + [VMEM] + [ANY] * 3 + [VMEM] * 7,
+        out_specs=(VMEM,) * 3 + (ANY,) * (len(outs) - 3),
+        scratch_shapes=[
+            *vm[0], *vm[1],
+            pltpu.VMEM((length, wide), bf),
+            pltpu.VMEM(go.shape, bf),
+            pltpu.VMEM((length, part), bf),
+            pltpu.VMEM((part, length), bf),
+            pltpu.VMEM((length, LANE), f32),
+            pltpu.VMEM((length, LANE), f32),
+            pltpu.VMEM((length, 3 * part), bf),
+            pltpu.VMEM((width, length), bf),
+            pltpu.VMEM((toks, width), bf),
+            pltpu.VMEM(dq_shape, bf),
+            pltpu.VMEM((8, round_up(width, 3 * part)), f32),
+            pltpu.SemaphoreType.DMA((512,)),
+            pltpu.SemaphoreType.DMA((2,)),
+        ],
+        compiler_params=pltpu.CompilerParams(
+            collective_id=1, has_side_effects=True, vmem_limit_bytes=62 * 1024 * 1024
+        ),
+        name="backward",
+    )(g2, g1, gp, gs, go, xg, qkv, cos, sin, pic_col, pic_row, wq_full, lse, small)
+    return results[:6]
 
 
 def layer_norm(values, norm_gain, norm_shift):
@@ -550,9 +1065,9 @@
     small = pack_small((ln1_gain, ln1_bias, proj_bias, ln2_gain, ln2_bias, fc2_bias, fc1_bias), width, index, total)
     bias_line = lax.dynamic_update_slice(jnp.zeros((1, 3 * width), bf), qkv_bias[None], (0, index * qkv_bias.shape[0]))
     wq = jnp.concatenate([qkv_weight, bias_line], axis=0)
-    wq = jnp.pad(qkv_columns(wq, size), ((0, 0), (0, round_up(shard + 3, 16) - shard - 1), (0, 0)))
+    wq = jnp.pad(qkv_columns(wq, size), ((0, 0), (0, round_up(shard + 1 + 2 * -(-width // (3 * part)), 16) - shard - 1), (0, 0)))
     x = activations[0]
-    wp, w1, w2, att, lines, normed, qkv, wq_full, lse = forward_call(
+    wp, w1, w2, att, lines, xg, qkv, wq_full, lse = forward_call(
         mesh, x, wq, proj_weight, fc1_weight, fc2_weight, small, cos, sin, picture[:, None], picture[None, :]
     )
     wp, w1, w2 = (w.reshape(-1, w.shape[-1]) for w in (wp, w1, w2))
@@ -586,33 +1101,28 @@
     grad_proj = jnp.dot(attended.T, grad_branch, preferred_element_type=f32)
     grad_attended = jnp.dot(grad_branch, wp.T, preferred_element_type=f32).astype(bf)
 
-    grad_att = lax.all_to_all(
-        grad_attended.reshape(toks, size, group * HEAD_DIM), "seq", split_axis=1, concat_axis=0, tiled=True
-    ).reshape(length, group, HEAD_DIM)
-    heads = qkv.reshape(length, 3, group, LANE)
-    q, k, v = heads[:, 0], heads[:, 1], heads[:, 2, :, :HEAD_DIM]
-    scores = jnp.einsum("khe,qhe->hkq", k, q, preferred_element_type=f32)
-    scores = jnp.where((picture[:, None] == picture[None, :])[None], scores, -1e30)
-    probs = jnp.exp2(scores * EXP_SCALE - lse)
-    grad_probs = jnp.einsum("khe,qhe->hkq", v, grad_att, preferred_element_type=f32)
-    delta = jnp.sum(probs * grad_probs, axis=1, keepdims=True)
-    grad_scores = (probs * (grad_probs - delta)).astype(bf)
-    grad_q = jnp.einsum("hkq,khe->qhe", grad_scores, k, preferred_element_type=f32) * SCALE
-    grad_k = jnp.einsum("hkq,qhe->khe", grad_scores, q, preferred_element_type=f32) * SCALE
-    grad_v = jnp.einsum("hkq,qhe->khe", probs.astype(bf), grad_att, preferred_element_type=f32)
-    grad_v = jnp.pad(grad_v, ((0, 0), (0, 0), (0, LANE - HEAD_DIM)))
-
-    def unturn(g):
-        return g * cos[:, None] + jnp.roll(g * sin[:, None], LANE // 2, axis=-1)
-
-    grad_mixed = jnp.concatenate(
-        [g.reshape(length, part) for g in (unturn(grad_q), unturn(grad_k), grad_v)], axis=-1
-    ).astype(bf)
-    grad_normed = jnp.dot(grad_mixed, wq_full.T, preferred_element_type=f32).astype(bf)
-    grad_normed = lax.psum_scatter(grad_normed, "seq", scatter_dimension=0, tiled=True).astype(f32)
-    grad_qkv = jnp.dot(normed.T, grad_mixed, preferred_element_type=f32).astype(bf)
-    grad_qkv = lax.psum_scatter(grad_qkv, "row", scatter_dimension=0, tiled=True).reshape(size, shard, 3 * part)
-    grad_qkv = lax.all_to_all(grad_qkv, "seq", split_axis=0, concat_axis=0, tiled=True).astype(f32)
+    go = grad_attended.reshape(toks, size, group * HEAD_DIM).transpose(1, 0, 2)
+    go = jnp.pad(go, ((0, 0), (0, 0), (0, round_up(group * HEAD_DIM, LANE) - group * HEAD_DIM)))
+    smalls = jnp.concatenate(
+        [
+            g.reshape(total, -1)
+            for g in (grad_proj_bias, grad_gain_two, grad_shift_two, grad_down_bias, grad_up_bias)
+        ],
+        axis=-1,
+    )
+    smalls = jnp.pad(smalls, ((0, 0), (0, 8 * 2 * LANE - smalls.shape[1]))).reshape(total, 8, 2 * LANE)
+    grad_normed, grad_qkv, smalls, grad_down, grad_up, grad_proj = backward_call(
+        mesh,
+        grad_down.astype(bf).reshape(total, -1, width),
+        grad_up.astype(bf).reshape(total, shard, -1),
+        grad_proj.astype(bf).reshape(total, shard, width),
+        smalls, go, xg, qkv, cos, sin, picture[:, None], picture[None, :], wq_full, lse, lines, wq.shape[1],
+    )
+    smalls = smalls.reshape(-1)
+    grad_proj_bias, grad_gain_two, grad_shift_two, grad_down_bias = (
+        smalls[i * shard : (i + 1) * shard] for i in range(4)
+    )
+    grad_up_bias = smalls[4 * shard : 4 * shard + fc1_bias.shape[0]]
 
     def natural(g):
         return jnp.concatenate(
@@ -624,37 +1134,36 @@
             axis=-1,
         )
 
-    grad_qkv = natural(grad_qkv)
-    grad_bias = jnp.sum(grad_mixed.astype(f32), axis=0)
-    grad_bias = natural(lax.all_gather(lax.psum(grad_bias, "row"), "seq")[:, None, :])[0]
+    grad_qkv = grad_qkv.astype(f32)
+    grad_bias = natural(grad_qkv[:, shard : shard + 1])[0]
+    lined = -(-width // (3 * part))
+    norm_lines = jnp.sum(grad_qkv[:, shard + 1 : shard + 1 + 2 * lined], axis=0).reshape(2, -1)[:, :width]
+    grad_gain_one, grad_shift_one = (
+        lax.dynamic_slice_in_dim(norm_lines[i], index * shard, shard) for i in range(2)
+    )
+    grad_qkv = natural(grad_qkv[:, :shard])
     grad_qk = lax.dynamic_slice_in_dim(grad_bias[: 2 * width], index * 2 * shard, 2 * shard)
     grad_value = lax.dynamic_slice_in_dim(grad_bias[2 * width :], index * shard, shard)
     _, norm_one_back = jax.vjp(layer_norm, inputs, lines[0], lines[1])
-    grad_inputs, grad_gain_one, grad_shift_one = norm_one_back(grad_normed)
+    grad_inputs, _, _ = norm_one_back(grad_normed)
     grad_acts = (grad_inputs + grad_middle).astype(bf)
-
-    def owned(values):
-        return lax.psum_scatter(values, ("row", "seq"), scatter_dimension=0, tiled=True)
-
-    def owned_low(values):
-        return owned(values.astype(bf)).astype(f32)
 
     return (
         layer_out[None],
         grad_acts[None],
-        owned(grad_gain_one),
-        owned(grad_shift_one),
+        grad_gain_one,
+        grad_shift_one,
         grad_qkv,
         grad_qk,
         grad_value,
-        owned_low(grad_proj),
-        owned(grad_proj_bias),
-        owned(grad_gain_two),
-        owned(grad_shift_two),
-        owned_low(grad_up),
-        owned(grad_up_bias),
-        owned_low(grad_down),
-        owned(grad_down_bias),
+        grad_proj,
+        grad_proj_bias,
+        grad_gain_two,
+        grad_shift_two,
+        grad_up,
+        grad_up_bias,
+        grad_down,
+        grad_down_bias,
     )
 
 

time: 1550 us -> 801 us (0.52)
  waiting for transfers between devices: 696 us -> 0 us
  Pallas kernels: 311 us -> 634 us
  matrix products: 278 us -> 92.6 us
  blocking collectives: 72.7 us -> 0 us
  other arithmetic: 92.4 us -> 24.1 us
  local copies, waits for them, and re-layouts: 75 us -> 38.4 us
    reduce_scatter x5 -> x0, waiting for transfers between devices: 691 us -> none  [the longest x3 605 us: owned(): lax.psum_scatter(values, ('row', 'seq'), scatter_dimension=0, tiled=True)]
    pallas_call x0 -> x1, Pallas kernels: none -> 323 us  [backward_call(): pl.pallas_call(functools.partial(backward_kernel, rows, size, shard, grou...]
    dot_general x7 -> x0, matrix products: 169 us -> none  [the longest x1 51.6 us: shards(): scores = jnp.einsum('khe,qhe->hkq', k, q, preferred_element_type=f32)]
    convert_element_type x5 -> x1, other arithmetic: 59.8 us -> 0.12 us  [shards(): grad_qkv = grad_qkv.astype(f32)]
    unnamed x1 -> x0, blocking collectives: 45.8 us -> none
  transfers between devices with their start and end apart: 7 -> 0, of which waited for: 5 -> 0; matrix products, arithmetic and copies ran while one was open for 8% -> 0% of each run, Pallas kernels for 0% -> 0%
where the time goes in v2:
time: 801 us; the launch traced here: 791 us
  Pallas kernels  634 us (79%)
  matrix products  92.6 us (12%)
  local copies, waits for them, and re-layouts  38.4 us (5%)
  other arithmetic  24.1 us (3%)
    pallas_call x1, Pallas kernels, backward_call(): pl.pallas_call(functools.partial(backward_kernel, rows, size, shard, grou...  323 us
    pallas_call x1, Pallas kernels, forward_call(): pl.pallas_call(functools.partial(forward_kernel, rows, size, shard, group...  311 us
    dot_general x1, matrix products, shards(): grad_down = jnp.dot(activated_low.T, grad_out, preferred_element_type=f32)  16.8 us

profile of v2, /device:TPU:0, one launch (start us, length us, event | category | flops | bytes accessed | tf_op | source)
XLA Modules:
  0.0 791.0 jit_solution(3641011778538518840)
XLA Ops:
  2.2 1.6 convert_reduce_fusion.1
  12.7 1.0 fusion.27
  16.5 0.9 fusion.23.wq
  17.5 1.2 fusion.24
  19.1 1.4 copy.78.pic_col.refs_9_
  21.0 2.5 pad_maximum_fusion
  23.4 311.2 %forward.1 = (bf16[32,40,1280]{2,1,0:T(8,128)(2,1)}, bf16[32,40,5120]{2,1,0:T(8,128)(2,1)}, bf16[32,160,1280]{2,1,0:T(8,128)(2,1)}, bf16[4,512,384]{2,1,0:T(8,12...) custom-call(bf16[512,1280]{1,0:T(8,128)(2,1)} %bitcast.122, ...), custom_call_target="tpu_custom_call" | custom-call | tf_op jit(solution)/shard_map/forward/pallas_call | solution.py:417
  334.6 1.6 slice_bitcast_fusion
  336.2 2.7 concatenate.37
  339.6 4.5 fusion.45
  344.5 2.2 copy-done.21
  346.7 10.0 %fusion.40 = f32[512,5120]{1,0:T(8,128)} fusion(bf16[1280,5120]{1,0:T(8,128)(2,1)S(1)} %bitcast.153, f32[512,1280]{1,0:T(8,128)S(1)} %get-tuple-element.91, f32[1280]{0:T(1024)S(1)} %get-tuple-element.54, f32[1280]{0:T(1024)S(1)} %get-tuple-element.55, f32[512]{0:T(512)S(1)} %fusion.31, f32[512]{0:T(512)S(1)} %broadcast_multiply_fusion.3), kind=kOutput, calls=%fused_computation.122 | convolution fusion | flops 6714163200 | bytes 26228736 | tf_op jit(solution)/shard_map/dot_general | solution.py:1082
  356.7 15.9 %fusion.10 = bf16[1,512,1280]{2,1,0:T(8,128)(2,1)} fusion(f32[512,1280]{1,0:T(8,128)S(1)} %get-tuple-element.91, bf16[5120,1280]{1,0:T(8,128)(2,1)} %bitcast.154, f32[1280]{0:T(1024)S(1)} %get-tuple-element.53, f32[512,5120]{1,0:T(8,128)} %fusion.40, f32[5120]{0:T(1024)S(1)} %add.138), kind=kOutput, calls=%fused_computation.28 | convolution fusion | flops 6731202560 | bytes 27550720 | tf_op jit(solution)/shard_map/dot_general | solution.py:1085
  372.6 14.6 %convert_reduce_fusion = (f32[5120]{0:T(1024)S(1)}, bf16[512,5120]{1,0:T(8,128)(2,1)}) fusion(f32[512,5120]{1,0:T(8,128)S(1)} %copy-done.23, f32[5120]{0:T(1024)S(1)} %add.138, bf16[5120,1280]{1,0:T(8,128)(2,1)} %bitcast.155, bf16[1,512,1280]{2,1,0:T(8,128)(2,1)S(1)} %copy-done.8), kind=kOutput, calls=%fused_computation.9 | convolution fusion | flops 6750202880 | bytes 30187520 | tf_op jit(solution)/shard_map/dot_general | solution.py:1092
  387.2 14.6 %multiply_reduce_fusion = (f32[1280]{0:T(1024)S(1)}, f32[512]{0:T(512)S(1)}, f32[1280]{0:T(1024)S(1)}, f32[512,1280]{1,0:T(8,128)}) fusion(f32[512,1280]{1,0:T(8,128)S(1)} %copy-done.6, f32[512]{0:T(512)S(1)} %fusion.31, f32[512]{0:T(512)S(1)} %broadcast_multiply_fusion.3, f32[1280]{0:T(1024)S(1)} %get-tuple-element.55, ...), kind=kOutput, calls=%fused_computation.32 | convolution fusion | flops 6716126208 | bytes 23614464 | tf_op jit(solution)/shard_map/dot_general | solution.py:1096
  401.9 3.3 fusion.42
  405.4 2.6 convert_reduce_fusion.3
  408.1 1.1 copy-done.12
  409.1 1.9 convolution_convert_fusion.3
  413.6 1.3 pad.33.refs_4_
  415.9 3.6 convolution_convert_fusion.2
  419.5 16.8 %convolution_convert_fusion.1 = bf16[5120,1280]{1,0:T(8,128)(2,1)} fusion(bf16[1,512,1280]{2,1,0:T(8,128)(2,1)S(1)} %copy-done.9, f32[512,5120]{1,0:T(8,128)} %fusion.40, f32[5120]{0:T(1024)S(1)} %add.138), kind=kOutput, calls=%fused_computation.1 | convolution fusion | flops 6735790080 | bytes 24924160 | tf_op jit(solution)/shard_map/dot_general | solution.py:1090
  436.4 10.6 %convolution_convert_fusion = bf16[1280,5120]{1,0:T(8,128)(2,1)} fusion(bf16[512,5120]{1,0:T(8,128)(2,1)S(1)} %bitcast.160, f32[512,1280]{1,0:T(8,128)S(1)} %copy-done.7, f32[1280]{0:T(1024)S(1)} %get-tuple-element.54, f32[1280]{0:T(1024)S(1)} %get-tuple-element.55, f32[512]{0:T(512)S(1)} %fusion.31, f32[512]{0:T(512)S(1)} %broadcast_multiply_fusion.3), kind=kOutput, calls=%fused_computation | convolution fusion | flops 6720716800 | bytes 20985856 | tf_op jit(solution)/shard_map/dot_general | solution.py:1095
  447.0 322.9 %backward.1 = (f32[512,1280]{1,0:T(8,128)}, bf16[4,48,1536]{2,1,0:T(8,128)(2,1)}, f32[8,256]{1,0:T(8,128)}, f32[160,1280]{1,0:T(8,128)}, f32[40,5120]{1,0:T(8,12...) custom-call(bf16[32,160,1280]{2,1,0:T(8,128)(2,1)} %bitcast.123, ...), custom_call_target="tpu_custom_call" | custom-call | tf_op jit(solution)/shard_map/backward/pallas_call | solution.py:985
  772.0 2.5 fusion.11
  776.6 2.4 fusion.14
  783.0 0.9 reshape.296
  785.3 0.9 reshape.298
  786.2 0.9 pad_maximum_fusion.4
  787.1 1.6 copy.107
  788.7 0.9 copy.108
  789.6 0.9 copy.109
  (139 shorter events, 28.3 us)
Async XLA Ops:
  9.2 9.9 %copy-start.17 = (s32[2048]{0:T(1024)}, s32[2048]{0:T(1024)S(1)}, u32[]{:S(2)}) copy-start(s32[2048]{0:T(1024)S(1)} %convert_reduce_fusion.4) | copy-start | bytes 24580
  334.6 4.4 copy-start.18
  334.6 5.0 copy-start
  339.6 7.1 copy-start.21
  344.1 12.6 %copy-start.5 = (f32[512,1280]{1,0:T(8,128)}, f32[512,1280]{1,0:T(8,128)S(1)}, u32[]{:S(2)}) copy-start(f32[512,1280]{1,0:T(8,128)S(1)} %get-tuple-element.91) | copy-start | bytes 7864324
  356.7 15.9 %copy-start.8 = (bf16[1,512,1280]{2,1,0:T(8,128)(2,1)S(1)}, bf16[1,512,1280]{2,1,0:T(8,128)(2,1)}, u32[]{:S(2)}) copy-start(bf16[1,512,1280]{2,1,0:T(8,128)(2,1)} %param.17) | copy-start | bytes 3932164
  356.7 15.9 %copy-start.23 = (f32[512,5120]{1,0:T(8,128)S(1)}, f32[512,5120]{1,0:T(8,128)}, u32[]{:S(2)}) copy-start(f32[512,5120]{1,0:T(8,128)} %fusion.40) | copy-start | bytes 31457284
  372.6 14.6 %copy-start.6 = (f32[512,1280]{1,0:T(8,128)S(1)}, f32[512,1280]{1,0:T(8,128)}, u32[]{:S(2)}) copy-start(f32[512,1280]{1,0:T(8,128)} %copy-done.5) | copy-start | bytes 7864324
  405.2 2.9 copy-start.3
  405.4 3.7 copy-start.22
  408.0 1.1 copy-start.12
  413.6 1.8 copy-start.11
  413.6 2.3 copy-start.13
  415.9 3.6 copy-start.9
  415.9 20.5 %slice-start = ((s8[5242880]{0:T(1024)(128)(4,1)}), s8[1048576]{0:T(1024)(128)(4,1)S(1)}, s32[]{:S(2)}) async-start(s8[5242880]{0:T(1024)(128)(4,1)} %bitcast.159), calls=%async_computation | async-start | bytes 2097152
  419.5 16.8 %copy-start.7 = (f32[512,1280]{1,0:T(8,128)S(1)}, f32[512,1280]{1,0:T(8,128)}, u32[]{:S(2)}) copy-start(f32[512,1280]{1,0:T(8,128)} %copy-done.5) | copy-start | bytes 7864324
  419.5 16.8 %slice-start.1 = ((s8[5242880]{0:T(1024)(128)(4,1)}), s8[4194304]{0:T(1024)(128)(4,1)S(1)}, s32[]{:S(2)}) async-start(s8[5242880]{0:T(1024)(128)(4,1)} %bitcast.159), calls=%async_computation.1 | async-start | bytes 8388608
  447.0 325.0 %copy-start.1 = (bf16[1,512,1280]{2,1,0:T(8,128)(2,1)S(1)}, bf16[1,512,1280]{2,1,0:T(8,128)(2,1)}, u32[]{:S(2)}) copy-start(bf16[1,512,1280]{2,1,0:T(8,128)(2,1)} %param.16) | copy-start | bytes 3932164
  447.0 325.0 %copy-start.19 = (f32[1280]{0:T(1024)S(1)}, f32[1280]{0:T(1024)}, u32[]{:S(2)}) copy-start(f32[1280]{0:T(1024)} %get-tuple-element.52) | copy-start | bytes 15364
  447.0 325.0 %copy-start.20 = (f32[512]{0:T(512)S(1)}, f32[512]{0:T(512)}, u32[]{:S(2)}) copy-start(f32[512]{0:T(512)} %broadcast_multiply_fusion.2) | copy-start | bytes 6148
  769.9 4.7 copy-start.2
  774.5 1.7 copy-start.4
  774.5 2.1 copy-start.10
  776.6 2.4 copy-start.16
  784.2 4.6 copy-start.15
  784.9 4.7 copy-start.14

commit v3 on v1

v3 whole, which is shorter than its diff:
```python
import functools
import math

import jax
import jax.numpy as jnp
from jax import lax
from jax.experimental import pallas as pl
from jax.experimental.pallas import tpu as pltpu
from jax.sharding import PartitionSpec as P

HEADS = 16
HEAD_DIM = 80
HALF = HEAD_DIM // 2
LANE = 128
NORM_EPS = 1e-06
SCALE = 1.0 / math.sqrt(HEAD_DIM)
LOG2E = 1.4426950408889634
EXP_SCALE = SCALE * LOG2E
QBLK = 256
MESH = pl.DeviceIdType.MESH
ANY = pl.BlockSpec(memory_space=pl.ANY)
VMEM = pl.BlockSpec(memory_space=pltpu.VMEM)


def round_up(value, unit):
    return -(-value // unit) * unit


def flip(index, bit):
    return index + bit - 2 * bit * ((index // bit) % 2)


def remote(src, dst, send_sem, recv_sem, row, seq):
    return pltpu.make_async_remote_copy(
        src_ref=src,
        dst_ref=dst,
        send_sem=send_sem,
        recv_sem=recv_sem,
        device_id=(row, seq),
        device_id_type=MESH,
    )


class Sems:
    def __init__(self, ref):
        self.ref = ref
        self.used = 0

    def take(self, count):
        first = self.used
        self.used += count
        assert self.used <= self.ref.shape[0]
        return [self.ref.at[first + i] for i in range(count)]


class Chain:
    def __init__(self, own, buf, base, row, seq, size, sems):
        self.own, self.buf, self.base = own, buf, base
        self.row, self.seq, self.size = row, seq, size
        self.sems = [[(sems.take(1)[0], sems.take(1)[0]) for _ in range(size - 1)] for _ in range(2)]
        (self.local,) = sems.take(1)

    def _copies(self, step):
        seq, size = self.seq, self.size
        out = []
        for way in range(2):
            sign = 1 - 2 * way
            block = seq - sign * (step - 1)
            peer = seq + sign
            going = (peer >= 0) & (peer < size) & (block >= 0) & (block < size)
            slot = self.buf.at[self.base + block]
            src = self.own if step == 1 else slot
            copy = functools.partial(remote, src, slot, *self.sems[way][step - 1], self.row, peer)
            come = seq - sign * step
            coming = (come >= 0) & (come < size)
            into = self.buf.at[self.base + come]
            arrive = functools.partial(remote, into, into, *self.sems[way][step - 1], self.row, peer)
            out.append((going, copy, coming, arrive))
        return out

    def keep(self):
        return pltpu.make_async_copy(self.own, self.buf.at[self.base + self.seq], self.local)

    def send(self, step):
        if step == 1:
            self.keep().start()
        for going, copy, _, _ in self._copies(step):
            pl.when(going)(lambda copy=copy: copy().start())

    def recv(self, step):
        for _, _, coming, arrive in self._copies(step):
            pl.when(coming)(lambda arrive=arrive: arrive().wait_recv())

    def finish(self):
        for step in range(1, self.size):
            for going, copy, _, _ in self._copies(step):
                pl.when(going)(lambda copy=copy: copy().wait_send())


class Scatter:
    def __init__(self, src, dst_of, row, seq, size, sems):
        self.src, self.dst_of = src, dst_of
        self.row, self.seq, self.size = row, seq, size
        self.sems = [(sems.take(1)[0], sems.take(1)[0]) for _ in range(size - 1)]
        (self.local,) = sems.take(1)

    def _to(self, step):
        peer = (self.seq + step) % self.size
        return remote(self.src.at[peer], self.dst_of(self.seq), *self.sems[step - 1], self.row, peer)

    def _from(self, step):
        peer = (self.seq + self.size - step) % self.size
        into = self.dst_of(peer)
        return remote(into, into, *self.sems[step - 1], self.row, peer)

    def keep(self):
        return pltpu.make_async_copy(self.src.at[self.seq], self.dst_of(self.seq), self.local)

    def send(self, step):
        self._to(step).start()

    def send_all(self):
        self.keep().start()
        for step in range(1, self.size):
            self.send(step)

    def recv(self):
        self.keep().wait()
        for step in range(1, self.size):
            self._from(step).wait_recv()

    def finish(self):
        for step in range(1, self.size):
            self._to(step).wait_send()


class Spread:
    def __init__(self, buf, row, seq, rows, size, sems):
        self.buf, self.row, self.seq, self.size = buf, row, seq, size
        bits = [1 << i for i in range(1, rows.bit_length() - 1)]
        self.stages = len(bits)
        self.orders = (bits, bits[::-1])
        self.half = buf.shape[2] // 2
        self.sems = [
            [[(sems.take(1)[0], sems.take(1)[0]) for _ in range(1 << j)] for j in range(self.stages)]
            for _ in range(2)
        ]
        self.core_sems = [(sems.take(1)[0], sems.take(1)[0])]
        self.core_sems += [
            (sems.take(1)[0], sems.take(1)[0]) for _ in range(2 * ((1 << self.stages) - 1))
        ]

    def _block(self, row, half):
        first = row * self.size
        if half is None:
            return self.buf.at[pl.ds(first, self.size)]
        return self.buf.at[pl.ds(first, self.size), :, pl.ds(half * self.half, self.half)]

    def _rows(self, start, half, stage):
        rows = [start]
        for bit in self.orders[half][:stage]:
            rows += [flip(row, bit) for row in rows]
        return rows

    def _pairs(self, stage):
        out = []
        for half in range(2):
            bit = self.orders[half][stage]
            peer = flip(self.row, bit)
            for i, row in enumerate(self._rows(self.row, half, stage)):
                here = self._block(row, half)
                there = self._block(flip(row, bit), half)
                pair = self.sems[half][stage][i]
                out.append((here, there, pair, peer))
        return out

    def _core(self, index, block):
        return remote(block, block, *self.core_sems[index], flip(self.row, 1), self.seq)

    def _core_blocks(self, row):
        out = [[self._block(row, None)]]
        for stage in range(self.stages):
            out.append([])
            for half in range(2):
                bit = self.orders[half][stage]
                for other in self._rows(row, half, stage):
                    out[-1].append(self._block(flip(other, bit), half))
        return out

    def _first(self, stage):
        return 0 if stage == 0 else 1 + 2 * ((1 << (stage - 1)) - 1)

    def send(self, stage):
        if stage < self.stages:
            for here, _, pair, peer in self._pairs(stage):
                remote(here, here, *pair, peer, self.seq).start()
        for i, block in enumerate(self._core_blocks(self.row)[stage]):
            self._core(self._first(stage) + i, block).start()

    def recv(self, stage):
        for _, there, pair, peer in self._pairs(stage):
            remote(there, there, *pair, peer, self.seq).wait_recv()

    def finish(self):
        for stage in range(self.stages):
            for here, _, pair, peer in self._pairs(stage):
                remote(here, here, *pair, peer, self.seq).wait_send()
        mine, theirs = self._core_blocks(self.row), self._core_blocks(flip(self.row, 1))
        for stage in range(self.stages + 1):
            for i, block in enumerate(theirs[stage]):
                self._core(self._first(stage) + i, block).wait_recv()
            for i, block in enumerate(mine[stage]):
                self._core(self._first(stage) + i, block).wait_send()


def greet(row, seq, rows, size):
    barrier = pltpu.get_barrier_semaphore()
    count = 0
    bit = 1
    while bit < rows:
        pl.semaphore_signal(barrier, inc=1, device_id=(flip(row, bit), seq), device_id_type=MESH)
        bit *= 2
        count += 1
    for step in range(1, size):
        pl.semaphore_signal(barrier, inc=1, device_id=(row, (seq + step) % size), device_id_type=MESH)
        count += 1
    pl.semaphore_wait(barrier, count)


def pieces(own, buf):
    a, b = own.shape
    if b % (8 * LANE) == 0:
        cut = [(slice(None), pl.ds(i * (b // 2), b // 2)) for i in range(2)]
    elif a % 32 == 0:
        cut = [(pl.ds(i * (a // 2), a // 2), slice(None)) for i in range(2)]
    else:
        cut = [(slice(None), slice(None))]
    return [(own.at[p], buf.at[(slice(None),) + p]) for p in cut]


def forward_kernel(
    rows, size, group,
    x, wq, wp, w1, w2, small, sel_t, cos, sin, pic_col, pic_row,
    wp_all, w1_all, w2_all, att, hat_out, qkv_out, k_out, wq_out, o_out, small_sum, lse,
    xg, normed, wq_buf, small_buf, wide, wq_full, bias, qkv, v_turn, k_turn, hat_turn, o_turn, o_part, o_send, sem_ref, out_sem,
):
    row, seq = lax.axis_index("row"), lax.axis_index("seq")
    toks, width = x.shape
    shard = wp.shape[0]
    packed = 2 * LANE
    sems = Sems(sem_ref)
    base = row * size

    def gather(own, buf):
        return Chain(own, buf, base, row, seq, size, sems), Spread(buf, row, seq, rows, size, sems)

    small_g, wp_g = gather(small, small_buf), gather(wp, wp_all)
    a_wq, s_wq = Scatter(wq, lambda j: wq_buf.at[base + j], row, seq, size, sems), Spread(wq_buf, row, seq, rows, size, sems)
    w1_g = [gather(*p) for p in pieces(w1, w1_all)]
    w2_g = [gather(*p) for p in pieces(w2, w2_all)]
    first, second, third = [small_g], w1_g, w2_g + [wp_g]
    g_x = Chain(x, xg, 0, row, seq, size, sems)
    a_o = Scatter(o_send, lambda j: att.at[j], row, seq, size, sems)
    last = small_g[1].stages

    def chain(group, step):
        for g, _ in group:
            if step > 0:
                g.recv(step)
            if step < size - 1:
                g.send(step + 1)
            else:
                g.keep().wait()

    def spread(group, stage):
        for _, s in group:
            if stage > 0:
                s.recv(stage - 1)
            s.send(stage)

    greet(row, seq, rows, size)
    chain(first, 0)
    a_wq.send_all()
    chain(second, 0)
    for step in range(1, size):
        chain(first, step)
        if step < size - 1:
            chain(second, step)
    a_wq.recv()
    early = first + [(a_wq, s_wq)]
    spread(early, 0)
    g_x.send(1)
    chain(second, size - 1)
    spread(second, 0)
    chain(third, 0)
    if last > 0:
        spread(early, 1)
    for step in range(1, size - 1):
        chain(third, step)
    for stage in range(2, last + 1):
        spread(early, stage)
    for _, s in early:
        s.finish()
    total = jnp.zeros(small_sum.shape, jnp.float32)
    for i in range(rows * size):
        total += small_buf[i].astype(jnp.float32)
    small_sum[...] = total
    for i in range(rows * size):
        wide[pl.ds(i * shard, shard), :] = wq_buf[i].astype(jnp.float32)
    own_bias = small_sum[pl.ds(10 + seq, 1), pl.ds(0, group * packed)]
    for head in range(group):
        cols = pl.ds(head * packed, packed)
        out = pl.ds(head * 3 * LANE, 3 * LANE)
        part = jnp.dot(wide[:, cols].astype(jnp.bfloat16), sel_t[...], preferred_element_type=jnp.float32)
        wq_full[:, out] = part.astype(jnp.bfloat16)
        line = jnp.broadcast_to(own_bias[:, head * packed : (head + 1) * packed], (16, packed))
        bias[:, out] = jnp.dot(line.astype(jnp.bfloat16), sel_t[...], preferred_element_type=jnp.float32)

    def project(chunk):
        start = pl.multiple_of(chunk * toks, toks)
        block = 128

        def norm(i, carry):
            at = pl.multiple_of(i * block, block)
            values = xg[chunk, pl.ds(at, block), :].astype(jnp.float32)
            centered = values - jnp.mean(values, axis=-1, keepdims=True)
            variance = jnp.mean(centered * centered, axis=-1, keepdims=True)
            hat = centered * lax.rsqrt(variance + NORM_EPS)
            hat_turn[:, pl.ds(pl.multiple_of(start + at, block), block)] = hat.T.astype(jnp.bfloat16)
            out = hat * small_sum[0:1, :] + small_sum[1:2, :]
            normed[pl.ds(at, block), :] = out.astype(jnp.bfloat16)
            return carry

        lax.fori_loop(0, toks // block, norm, 0)
        span = pl.ds(start, toks)

        def two_heads(i, carry):
            at = pl.multiple_of(i * 6 * LANE, 6 * LANE)
            mixed = jnp.dot(normed[...], wq_full[:, pl.ds(at, 6 * LANE)], preferred_element_type=jnp.float32)
            mixed += bias[0:1, pl.ds(at, 6 * LANE)]
            for j in range(6):
                u = mixed[:, j * LANE : (j + 1) * LANE]
                if j % 3 < 2:
                    u = u * cos[span, :] + pltpu.roll(u, LANE // 2, 1) * sin[span, :]
                if j % 3:
                    turned = pl.ds(pl.multiple_of((2 * i + j // 3) * LANE, LANE), LANE)
                    (k_turn, v_turn)[j % 3 - 1][turned, span] = u.T.astype(jnp.bfloat16)
                qkv[span, pl.ds(pl.multiple_of(at + j * LANE, LANE), LANE)] = u.astype(jnp.bfloat16)
            return carry

        lax.fori_loop(0, group // 2, two_heads, 0)

    g_x.keep().wait()
    project(seq)
    for step in range(1, size):
        g_x.recv(step)
        if step < size - 1:
            g_x.send(step + 1)
        def arrived(i, carry):
            chunk = seq + (2 * i - 1) * step
            pl.when((chunk >= 0) & (chunk < size))(lambda: project(chunk))
            return carry

        lax.fori_loop(0, 2, arrived, 0)
        if step == 1:
            chain(third, size - 1)
            spread(third, 0)
        if step == size - 2 and last > 0:
            spread(second, 1)
        if step == size - 1 and last > 0:
            spread(third, 1)
    outs = [
        pltpu.make_async_copy(a, b, out_sem.at[1 + i])
        for i, (a, b) in enumerate(((hat_turn, hat_out), (qkv, qkv_out), (k_turn, k_out), (wq_full, wq_out)))
    ]
    for copy in outs:
        copy.start()

    def attend(chunk):
        def one(i, carry):
            head = i % group
            block = chunk * (toks // QBLK) + i // group
            span = pl.ds(pl.multiple_of(block * QBLK, QBLK), QBLK)
            at = pl.multiple_of(head * 3 * LANE, LANE)
            q = qkv[span, pl.ds(at, LANE)]
            k = qkv[:, pl.ds(pl.multiple_of(at + LANE, LANE), LANE)]
            scores = lax.dot_general(k, q, (((1,), (1,)), ((), ())), preferred_element_type=jnp.float32)
            scores = jnp.where(pic_col[...] == pic_row[:, span], scores, -1e30)
            top = jnp.max(scores, axis=0, keepdims=True)
            weights = jnp.exp2((scores - top) * EXP_SCALE)
            sums = jnp.sum(weights, axis=0, keepdims=True)
            turned = pl.ds(pl.multiple_of(head * LANE, LANE), LANE)
            out = jnp.dot(v_turn[turned, :], weights.astype(jnp.bfloat16), preferred_element_type=jnp.float32)
            out = out / sums
            o_part[pl.ds(pl.multiple_of(head * HEAD_DIM, 8), HEAD_DIM), :] = out[:HEAD_DIM]
            lse[head, :, span] = top * EXP_SCALE + jnp.log2(sums)

            @pl.when(head == group - 1)
            def _():
                within = pl.multiple_of((i // group) * QBLK, QBLK)
                o_send[chunk, pl.ds(within, QBLK), :] = o_part[...].T.astype(jnp.bfloat16)
                o_turn[:, span] = o_part[...]

            return carry

        lax.fori_loop(0, group * (toks // QBLK), one, 0)

    o_part[...] = jnp.zeros_like(o_part)
    later = [(second, stage) for stage in range(2, last + 1)] + [(third, stage) for stage in range(2, last + 1)]
    for step in range(1, size + 1):
        attend((seq + step) % size)
        if step < size:
            a_o.send(step)
        else:
            a_o.keep().start()
        if step > 1 and later:
            spread(*later.pop(0))
    for group_of, stage in later:
        spread(group_of, stage)
    o_copy = pltpu.make_async_copy(o_turn, o_out, out_sem.at[0])
    o_copy.start()
    for _, s in second + third:
        s.finish()
    a_o.recv()
    for g, _ in early + second + third:
        g.finish()
    g_x.finish()
    a_o.finish()
    for copy in outs + [o_copy]:
        copy.wait()


def forward_call(mesh, x, wq, wp, w1, w2, small, sel_t, cos, sin, pic_col, pic_row):
    rows, size = mesh.shape["row"], mesh.shape["seq"]
    toks, width = x.shape
    length = toks * size
    group = HEADS // size
    shard = wp.shape[0]
    out_width = round_up(group * HEAD_DIM, LANE)
    total = rows * size
    wide = group * 3 * LANE
    bf, f32 = jnp.bfloat16, jnp.float32
    shape = jax.ShapeDtypeStruct
    return pl.pallas_call(
        functools.partial(forward_kernel, rows, size, group),
        out_shape=(
            shape((total,) + wp.shape, bf),
            shape((total,) + w1.shape, bf),
            shape((total,) + w2.shape, bf),
            shape((size, toks, out_width), bf),
            shape((width, length), bf),
            shape((length, wide), bf),
            shape((group * LANE, length), bf),
            shape((width, wide), bf),
            shape((out_width, length), f32),
            shape(small.shape, f32),
            shape((group, 1, length), f32),
        ),
        in_specs=[ANY] * 6 + [VMEM] * 5,
        out_specs=(ANY,) * 9 + (VMEM,) * 2,
        scratch_shapes=[
            pltpu.VMEM((size, toks, width), bf),
            pltpu.VMEM((toks, width), bf),
            pltpu.VMEM((total, shard, group * 2 * LANE), bf),
            pltpu.VMEM((total,) + small.shape, bf),
            pltpu.VMEM((width, group * 2 * LANE), f32),
            pltpu.VMEM((width, wide), bf),
            pltpu.VMEM((16, wide), f32),
            pltpu.VMEM((length, wide), bf),
            pltpu.VMEM((group * LANE, length), bf),
            pltpu.VMEM((group * LANE, length), bf),
            pltpu.VMEM((width, length), bf),
            pltpu.VMEM((out_width, length), f32),
            pltpu.VMEM((out_width, QBLK), f32),
            pltpu.VMEM((size, toks, out_width), bf),
            pltpu.SemaphoreType.DMA((640,)),
            pltpu.SemaphoreType.DMA((5,)),
        ],
        compiler_params=pltpu.CompilerParams(
            collective_id=0, has_side_effects=True, vmem_limit_bytes=62 * 1024 * 1024
        ),
        name="forward",
    )(x, wq, wp, w1, w2, small, sel_t, cos, sin, pic_col, pic_row)


def token_layout(lengths, widths, row_len):
    pic_ends = jnp.cumsum(lengths)
    pic_starts = pic_ends - lengths
    positions = jnp.arange(row_len, dtype=jnp.int32)
    picture = jnp.sum((positions[:, None] >= pic_ends[None, :]).astype(jnp.int32), axis=1)
    matches = picture[:, None] == jnp.arange(lengths.shape[0], dtype=jnp.int32)[None, :]
    first = jnp.sum(jnp.where(matches, pic_starts[None, :], 0), axis=1)
    grid_width = jnp.maximum(jnp.sum(jnp.where(matches, widths[None, :], 0), axis=1), 1)
    within = positions - first
    down = (within // grid_width).astype(jnp.float32)
    side = (within % grid_width).astype(jnp.float32)
    quarter = HEAD_DIM // 4
    frequency = 1.0 / 10000.0 ** (jnp.arange(quarter, dtype=jnp.float32) * 4.0 / HEAD_DIM)
    angles = jnp.concatenate([down[:, None] * frequency, side[:, None] * frequency], axis=-1)
    cosine, sine = jnp.cos(angles), jnp.sin(angles)
    gap = jnp.zeros((row_len, LANE // 2 - HALF), jnp.float32)
    return (
        picture,
        jnp.concatenate([cosine, gap, cosine, gap], axis=-1),
        jnp.concatenate([-sine, gap, sine, gap], axis=-1),
    )


def pack_heads(values):
    a = values.shape[0]
    values = values.reshape(a, 3, HEADS, HEAD_DIM).transpose(0, 2, 1, 3).reshape(a, HEADS, 3 * HEAD_DIM)
    return jnp.pad(values, ((0, 0), (0, 0), (0, 2 * LANE - 3 * HEAD_DIM))).reshape(a, HEADS * 2 * LANE)


def pick_lanes():
    spread = jnp.arange(3 * LANE)
    kind, lane = spread // LANE, spread % LANE
    turned = jnp.where(lane < LANE // 2, lane, lane - LANE // 2 + HALF)
    inside = jnp.where(kind < 2, lane % (LANE // 2) < HALF, lane < HEAD_DIM)
    target = jnp.where(inside, kind * HEAD_DIM + jnp.where(kind < 2, turned, lane), -1)
    return (target[:, None] == jnp.arange(2 * LANE)[None, :]).astype(jnp.bfloat16)


def natural(values):
    size, a, _ = values.shape
    values = values.reshape(size, a, HEADS // size, 3, LANE)
    turned = values[:, :, :, :2].reshape(size, a, HEADS // size, 2, 2, LANE // 2)[..., :HALF]
    turned = turned.reshape(size, a, HEADS // size, 2, HEAD_DIM)
    values = jnp.concatenate([turned, values[:, :, :, 2:, :HEAD_DIM]], axis=3)
    return values.transpose(1, 3, 0, 2, 4).reshape(a, 3 * HEADS * HEAD_DIM)


def add_blocks(outs, firsts, seconds, count, block, first_maps, second_maps):
    n = len(outs)

    def body(*refs):
        for a, b, o in zip(refs[:n], refs[n : 2 * n], refs[2 * n :]):
            o[...] = (a[...].astype(jnp.float32) + b[...].astype(jnp.float32)).astype(o.dtype)

    pltpu.emit_pipeline(
        body,
        grid=(count,),
        in_specs=[pl.BlockSpec(block, m, pipeline_mode=pl.Buffered(4)) for m in list(first_maps) + list(second_maps)],
        out_specs=[pl.BlockSpec(block, lambda i: (i, 0, 0))] * n,
    )(*firsts, *seconds, *outs)


class Reduce:
    def __init__(self, src, core, acc, come, done, row, seq, rows, size, sems, in_vmem):
        self.src, self.core, self.acc, self.come, self.done = src, core, acc, come, done
        self.row, self.seq, self.size, self.in_vmem = row, seq, size, in_vmem
        bits = [1 << i for i in range(1, rows.bit_length() - 1)]
        self.orders = (bits, bits[::-1])
        self.stages = len(bits)
        self.chips = rows // 2
        self.half = src.shape[2] // 2
        self.block = (size, src.shape[1], self.half)
        self.core_sems = [(sems.take(1)[0], sems.take(1)[0]) for _ in range(self.chips)]
        self.sems = [[(sems.take(1)[0], sems.take(1)[0]) for _ in bits] for _ in range(2)]

    def _core_copies(self):
        size = self.size
        other = flip(self.row, 1)
        for chip in range(self.chips):
            theirs = 2 * chip + other % 2
            yield remote(
                self.src.at[pl.ds(theirs * size, size)],
                self.core.at[pl.ds(chip * size, size)],
                *self.core_sems[chip],
                other,
                self.seq,
            )

    def core_send(self):
        for copy in self._core_copies():
            copy.start()

    def _chip(self, half, i):
        chip = self.row // 2
        for k in range(self.stages):
            bit = self.orders[half][self.stages - 1 - k] // 2
            chip = chip + ((i // (1 << k)) % 2) * (flip(chip, bit) - chip)
        return chip

    def core_add(self):
        size = self.size
        for copy in self._core_copies():
            copy.wait_recv()
        core = self.row % 2
        if not self.in_vmem:
            place = lambda half, i: (self._chip(half, i // size), i % size)
            mine = [lambda i, h=h: ((2 * place(h, i)[0] + core) * size + place(h, i)[1], 0, h) for h in range(2)]
            theirs = [lambda i, h=h: (place(h, i)[0] * size + place(h, i)[1], 0, h) for h in range(2)]
            block = (1,) + self.block[1:]
            count = self.chips * size
            add_blocks(self.acc, [self.src] * 2, [self.core] * 2, count, block, mine, theirs)
            return
        for half in range(2):
            cols = pl.ds(half * self.half, self.half)

            def body(i, carry, half=half, cols=cols):
                chip, z = self._chip(half, i // size), i % size
                mine = self.src[(2 * chip + core) * size + z, :, cols].astype(jnp.float32)
                total = mine + self.core[chip * size + z, :, cols].astype(jnp.float32)
                self.acc[half][i] = total.astype(self.acc[half].dtype)
                return carry

            lax.fori_loop(0, self.chips * size, body, 0)

    def _held(self, half, stage):
        return self.acc[half] if stage == 0 else self.done[half][stage - 1]

    def _stage_copy(self, half, stage):
        count = (self.chips >> (stage + 1)) * self.size
        return remote(
            self._held(half, stage).at[pl.ds(count, count)],
            self.come[half][stage],
            *self.sems[half][stage],
            flip(self.row, self.orders[half][stage]),
            self.seq,
        )

    def stage_send(self, stage):
        for half in range(2):
            self._stage_copy(half, stage).start()

    def stage_add(self, stage):
        count = (self.chips >> (stage + 1)) * self.size
        for half in range(2):
            self._stage_copy(half, stage).wait_recv()
        held = [self._held(half, stage) for half in range(2)]
        come, done = ([refs[half][stage] for half in range(2)] for refs in (self.come, self.done))
        if not self.in_vmem:
            plain = [lambda i: (i, 0, 0)] * 2
            add_blocks(done, held, come, count, (1,) + self.block[1:], plain, plain)
            return
        for half in range(2):

            def body(i, carry, half=half):
                total = held[half][i].astype(jnp.float32) + come[half][i].astype(jnp.float32)
                done[half][i] = total.astype(done[half].dtype)
                return carry

            lax.fori_loop(0, count, body, 0)

    @property
    def kept(self):
        return [self._held(half, self.stages) for half in range(2)]

    def finish(self):
        for copy in self._core_copies():
            copy.wait_send()
        for half in range(2):
            for stage in range(self.stages):
                self._stage_copy(half, stage).wait_send()


def reduce_shapes(src, rows, size):
    a, b = src[1], src[2] // 2
    chips = rows // 2
    stages = rows.bit_length() - 2
    shapes = [(chips * size, a, 2 * b)] + [(chips * size, a, b)] * 2
    for _ in range(2):
        for stage in range(stages):
            shapes += [((chips >> (stage + 1)) * size, a, b)] * 2
    return shapes + [(size, a, b)] * 2


def reduce_refs(refs, rows):
    stages = rows.bit_length() - 2
    core, acc, rest = refs[0], refs[1:3], refs[3:-2]
    come = [[rest[2 * (half * stages + j)] for j in range(stages)] for half in range(2)]
    done = [[rest[2 * (half * stages + j) + 1] for j in range(stages)] for half in range(2)]
    return (core, acc, come, done), refs[-2:]


FF_BLK = 1024
FF_CUT = 1280


def backward_kernel(rows, size, shard, group, counts, *refs):
    refs = list(refs)

    def take(count):
        out = refs[:count]
        del refs[:count]
        return out

    attd, x, cot, wp, w1, w2, b1, hat, qkv, k_t, o_t, wh, wq, cos, sin, pic_col, pic_row, lse, small, sel = take(20)
    dx_out, dq_out, layer_out, g_mid, g2_out, g1_out, gp_out, g2, g1, gp, go, b1_sum, wh_all, act, g_act = take(15)
    big = [take(counts) for _ in range(4)]
    vm = take(counts)
    do_in, packed_in, dq, rows_sum, sem_ref, load_sem = refs

    row, seq = lax.axis_index("row"), lax.axis_index("seq")
    length = qkv.shape[0]
    toks = length // size
    width = x.shape[1]
    wide = 3 * LANE
    packed = 2 * LANE
    sems = Sems(sem_ref)
    f32, bf = jnp.float32, jnp.bfloat16

    a_do = Scatter(go, lambda j: do_in.at[j], row, seq, size, sems)
    sources = []
    half_ff = w1.shape[1] // 2
    for i in range(2):
        cols = pl.ds(i * half_ff, half_ff)
        sources.append((g1.at[:, :, cols], g1_out.at[:, cols], big[i]))
    sources += [(g2, g2_out, big[2]), (gp, gp_out, big[3])]
    sources.append((dq, dq_out, vm))
    reducers, z_moves, z_bufs = [], [], []
    for src, out, bufs in sources:
        inner, z_refs = reduce_refs(bufs, rows)
        r = Reduce(src, *inner, row, seq, rows, size, sems, len(reducers) >= len(big))
        reducers.append(r)
        z_bufs.append(z_refs)
        z_moves.append(
            [Scatter(kept, lambda j, to=to: to.at[j], row, seq, size, sems) for kept, to in zip(r.kept, z_refs)]
        )
    rq = reducers[-1]
    rq_at = len(reducers) - 1
    stages = rq.stages

    def z_send(which):
        for move in z_moves[which]:
            move.send_all()

    def start(which):
        reducers[which].core_add()
        if stages:
            reducers[which].stage_send(0)
        else:
            z_send(which)

    def advance(which, stage):
        r = reducers[which]
        r.stage_add(stage)
        if stage + 1 < stages:
            r.stage_send(stage + 1)
        else:
            z_send(which)

    def z_sum(which):
        r, out = reducers[which], sources[which][1]
        cols = r.half // 2 if r.half % (4 * LANE) == 0 else r.half
        for half in range(2):
            z_moves[which][half].recv()
            buf = z_bufs[which][half]
            if which == rq_at:
                out[:, :, pl.ds(half * r.half, r.half)] = buf[...]
            else:

                def body(a, o):
                    total = a[0].astype(f32)
                    for z in range(1, size):
                        total += a[z].astype(f32)
                    o[...] = total

                pltpu.emit_pipeline(
                    body,
                    grid=(r.half // cols,),
                    in_specs=[pl.BlockSpec(r.block[:2] + (cols,), lambda i: (0, 0, i))],
                    out_specs=[pl.BlockSpec((r.block[1], cols), lambda i, half=half: (0, half * (r.half // cols) + i))],
                )(buf, out)

    ready = rq_at

    def load(src, dst, sem=0):
        return pltpu.make_async_copy(src, dst, load_sem.at[sem])

    ff = w1.shape[1]
    ff_blocks = ff // FF_BLK

    wh_chain = Chain(wh, wh_all, row * size, row, seq, size, sems)
    wh_spread = Spread(wh_all, row, seq, rows, size, sems)

    def chain_wh(step):
        wh_chain.recv(step)
        if step < size - 1:
            wh_chain.send(step + 1)
        else:
            wh_chain.keep().wait()

    def spread_wh(stage):
        if stage > wh_spread.stages:
            return
        if stage:
            wh_spread.recv(stage - 1)
        wh_spread.send(stage)

    def mlp(middle, n2, n2_turn, cot_v, out_sum, dn2, g_low, lines):
        loads = [load(cot, cot_v, 3)]
        loads[0].start()

        def head(attd_v, x_v, wp_v):
            copies = [load(attd, attd_v, 0), load(x, x_v, 1), load(wp, wp_v, 2)]
            for copy in copies:
                copy.start()
            for copy in copies:
                copy.wait()

            def one(i, carry):
                span = pl.ds(pl.multiple_of(i * QBLK, QBLK), QBLK)
                values = x_v[span, :].astype(f32) + small[2:3, :]
                values += jnp.dot(attd_v[span, :], wp_v[...], preferred_element_type=f32)
                middle[span, :] = values
                centered = values - jnp.mean(values, axis=-1, keepdims=True)
                variance = jnp.mean(centered * centered, axis=-1, keepdims=True)
                out = centered * lax.rsqrt(variance + NORM_EPS) * small[3:4, :] + small[4:5, :]
                n2[span, :] = out.astype(bf)
                n2_turn[:, span] = out.T.astype(bf)
                return carry

            lax.fori_loop(0, toks // QBLK, one, 0)

        pl.run_scoped(
            head, pltpu.VMEM((toks, width), bf), pltpu.VMEM((toks, width), bf), pltpu.VMEM((width, width), bf)
        )
        loads[0].wait()
        out_sum[...] = jnp.zeros_like(out_sum)
        dn2[...] = jnp.zeros_like(dn2)

        def body(w1_b, w2_b, b1_b, act_b, grad_b, sum_b):
            before = jnp.dot(n2[...], w1_b[...], preferred_element_type=f32) + b1_b[...]
            gate = jax.nn.sigmoid(1.702 * before)
            active = before * gate
            slope = gate + active * (1.702 * (1.0 - gate))
            low = active.astype(bf)
            act_b[...] = low
            out_sum[...] += jnp.dot(low, w2_b[...], preferred_element_type=f32)
            grad = lax.dot_general(cot_v[...], w2_b[...], (((1,), (1,)), ((), ())), preferred_element_type=f32)
            grad = (grad * slope).astype(bf)
            grad_b[...] = grad
            sum_b[...] = jnp.sum(grad.astype(f32), axis=0, keepdims=True)
            dn2[...] += lax.dot_general(grad, w1_b[...], (((1,), (1,)), ((), ())), preferred_element_type=f32)

        by_column = lambda i: (0, i)
        by_row = lambda i: (i, 0)
        chain_wh(1)
        pltpu.emit_pipeline(
            body,
            grid=(ff // FF_BLK,),
            in_specs=[
                pl.BlockSpec((width, FF_BLK), by_column),
                pl.BlockSpec((FF_BLK, width), by_row),
                pl.BlockSpec((1, FF_BLK), by_column),
            ],
            out_specs=[
                pl.BlockSpec((toks, FF_BLK), by_column),
                pl.BlockSpec((toks, FF_BLK), by_column),
                pl.BlockSpec((1, FF_BLK), by_column),
            ],
        )(w1, w2, b1, act, g_act, b1_sum)
        for step in range(2, size):
            chain_wh(step)
        spread_wh(0)

        def up_body(grad_b, g1_b):
            up = jnp.dot(n2_turn[...], grad_b[...], preferred_element_type=f32)
            for s in range(rows * size):
                g1_b[s] = up[s * shard : (s + 1) * shard].astype(bf)

        def up_range(first, count):
            pltpu.emit_pipeline(
                up_body,
                grid=(count,),
                in_specs=[pl.BlockSpec((toks, FF_CUT), lambda i: (0, i + first))],
                out_specs=[pl.BlockSpec((rows * size, shard, FF_CUT), lambda i: (0, 0, i + first))],
            )(g_act, g1)

        def down_body(act_b, g2_b):
            turned = act_b[...].astype(f32).T.astype(bf)
            down = jnp.dot(turned, cot_v[...], preferred_element_type=f32)
            rows_of = g2_b.shape[1]
            for s in range(g2_b.shape[0]):
                g2_b[s] = down[s * rows_of : (s + 1) * rows_of].astype(bf)

        def down_all():
            pltpu.emit_pipeline(
                down_body,
                grid=(ff // FF_CUT,),
                in_specs=[pl.BlockSpec((toks, FF_CUT), by_column)],
                out_specs=[pl.BlockSpec((FF_CUT // g2.shape[1], g2.shape[1], width), lambda i: (i, 0, 0))],
            )(act, g2)

        def tail(wp_v, go_v, out_v):
            copies = [load(wp, wp_v, 1)]
            for copy in copies:
                copy.start()
            lines[...] = jnp.zeros_like(lines)
            go_v[...] = jnp.zeros_like(go_v)

            def one(i, carry):
                span = pl.ds(pl.multiple_of(i * LANE, LANE), LANE)
                values = middle[span, :]
                out_v[span, :] = (values + out_sum[span, :] + small[5:6, :]).astype(bf)
                centered = values - jnp.mean(values, axis=-1, keepdims=True)
                variance = jnp.mean(centered * centered, axis=-1, keepdims=True)
                scale = lax.rsqrt(variance + NORM_EPS)
                hat = centered * scale
                grad = dn2[span, :]
                lines[1:2, :] += jnp.sum(grad * hat, axis=0, keepdims=True)
                lines[2:3, :] += jnp.sum(grad, axis=0, keepdims=True)
                grad = grad * small[3:4, :]
                grad -= jnp.mean(grad, axis=-1, keepdims=True) + hat * jnp.mean(grad * hat, axis=-1, keepdims=True)
                outer = cot_v[span, :].astype(f32)
                lines[3:4, :] += jnp.sum(outer, axis=0, keepdims=True)
                grad = grad * scale + outer
                dn2[span, :] = grad
                low = grad.astype(bf)
                lines[0:1, :] += jnp.sum(low.astype(f32), axis=0, keepdims=True)
                g_low[span, :] = low
                return carry

            lax.fori_loop(0, toks // LANE, one, 0)
            outs = [load(out_v, layer_out, 2), load(dn2, g_mid, 3)]
            for copy in outs:
                copy.start()
            for copy in copies:
                copy.wait()
            heads = group * HEAD_DIM
            for g in range(size):
                part = lax.dot_general(
                    g_low[...], wp_v[pl.ds(g * heads, heads), :], (((1,), (1,)), ((), ())), preferred_element_type=f32
                )
                go_v[g, :, pl.ds(0, heads)] = part.astype(bf)
            send = load(go_v, go, 0)
            send.start()
            send.wait()
            a_do.send_all()
            for copy in outs:
                copy.wait()

        def proj(attd_v, gp_v):
            get = load(attd, attd_v, 1)
            get.start()
            sums = load(b1_sum, rows_sum.at[0:1, pl.ds(0, ff)], 0)
            sums.start()
            sums.wait()
            for i in range(ff // width):
                lines[4 + i : 5 + i, :] = rows_sum[0:1, pl.ds(i * width, width)]
            low_lines = lines[0 : gp_v.shape[1] - shard, :].astype(bf)
            get.wait()
            tall = width // 2
            per = tall // shard
            for i in range(2):
                turned = attd_v[:, pl.ds(i * tall, tall)].astype(f32).T.astype(bf)
                grad = jnp.dot(turned, g_low[...], preferred_element_type=f32)
                for s in range(per):
                    gp_v[s, pl.ds(0, shard), :] = grad[s * shard : (s + 1) * shard].astype(bf)
                    gp_v[s, pl.ds(shard, low_lines.shape[0]), :] = low_lines
                put = load(gp_v, gp.at[pl.ds(i * per, per)], 0)
                put.start()
                put.wait()

        pl.run_scoped(
            tail,
            pltpu.VMEM((width, width), bf),
            pltpu.VMEM(go.shape, bf),
            pltpu.VMEM((toks, width), bf),
        )
        count = ff // FF_CUT
        up_range(0, count // 2)
        reducers[0].core_send()
        spread_wh(1)
        up_range(count // 2, count - count // 2)
        reducers[1].core_send()
        start(0)
        down_all()
        reducers[2].core_send()
        start(1)
        pl.run_scoped(
            proj, pltpu.VMEM((toks, width), bf), pltpu.VMEM((rows * size // 2,) + gp.shape[1:], bf)
        )
        reducers[3].core_send()
        for stage in range(2, wh_spread.stages + 1):
            spread_wh(stage)

    greet(row, seq, rows, size)
    wh_chain.send(1)
    pl.run_scoped(
        mlp,
        pltpu.VMEM((toks, width), f32),
        pltpu.VMEM((toks, width), bf),
        pltpu.VMEM((width, toks), bf),
        pltpu.VMEM((toks, width), bf),
        pltpu.VMEM((toks, width), f32),
        pltpu.VMEM((toks, width), f32),
        pltpu.VMEM((toks, width), bf),
        pltpu.VMEM((round_up(gp.shape[1] - shard, 8), width), f32),
    )
    start(2)
    if stages:
        advance(0, 0)
    start(3)
    wh_spread.finish()
    pl.run_scoped(
        functools.partial(
            attention_back, rows, size, shard, group, row, seq, sems, start, advance, z_sum, a_do, rq, rq_at,
            (hat, qkv, k_t, o_t, wh_all, wq, cos, sin, pic_col, pic_row, lse, small, sel, dx_out, do_in, packed_in, dq, rows_sum),
            load_sem,
        ),
        pltpu.VMEM((length, group * wide), bf),
        pltpu.VMEM((length, group * LANE), bf),
        pltpu.VMEM((group * LANE, length), bf),
        pltpu.VMEM((length, LANE), f32),
        pltpu.VMEM((length, LANE), f32),
        pltpu.VMEM((length, wide), bf),
        pltpu.VMEM((width, length), bf),
        pltpu.VMEM((width, LANE), f32),
        pltpu.VMEM((group, size, toks, packed), bf),
        pltpu.VMEM((2, rows * size, shard, packed), bf),
        pltpu.VMEM((width, packed), f32),
        pltpu.VMEM((width, wide), bf),
        pltpu.VMEM(o_t.shape, f32),
        pltpu.VMEM((group, 1, length), f32),
    )
    wh_chain.finish()
    for r in reducers:
        r.finish()
    for moves in z_moves:
        for move in moves:
            move.finish()
    a_do.finish()


EVENTS = (
    (0.15, ("advance", 1, 0)),
    (0.35, ("advance", 0, 1)),
    (0.45, ("advance", 1, 1)),
    (0.5, ("advance", 2, 0)),
    (0.55, ("advance", 3, 0)),
    (0.75, ("z_sum", 0)),
    (0.8, ("z_sum", 1)),
    (0.8, ("advance", 2, 1)),
    (0.85, ("advance", 3, 1)),
    (1, ("z_sum", 2)),
    (1, ("z_sum", 3)),
)


def attention_back(
    rows, size, shard, group, row, seq, sems, start, advance, z_sum, a_do, rq, rq_at, refs, load_sem,
    qkv_s, do_full, k_turn, gk_sum, gv_sum, gm, n_turn, columns, packs, w_cols, w_wide, wq_cols, o_turn, delta,
):
    hat, qkv, k_t, o_t, wh, wq, cos, sin, pic_col, pic_row, lse, small, sel, dx_out, do_in, packed_in, dq, rows_sum = refs
    length = qkv.shape[0]
    toks = length // size
    width = hat.shape[0]
    wide = 3 * LANE
    packed = 2 * LANE
    stages = rq.stages
    f32, bf = jnp.float32, jnp.bfloat16
    a_heads = [
        Scatter(packs.at[h], lambda j, h=h: packed_in.at[h, j], row, seq, size, sems) for h in range(group)
    ]
    loads = [
        pltpu.make_async_copy(a, b, load_sem.at[i])
        for i, (a, b) in enumerate(((qkv, qkv_s), (k_t, k_turn), (hat, n_turn), (o_t, o_turn)))
    ]
    for copy in loads:
        copy.start()
    columns[...] = jnp.zeros_like(columns)
    columns[:, pl.ds(8, 8)] = small[0:8, :].T
    for copy in loads:
        copy.wait()
    a_do.recv()

    def widen(i, carry):
        chunk, at = i // (toks // QBLK), (i % (toks // QBLK)) * QBLK
        values = do_in[chunk, pl.ds(pl.multiple_of(at, QBLK), QBLK), :].astype(f32)
        lanes = lax.broadcasted_iota(jnp.int32, (QBLK, LANE), 1)
        span = pl.ds(pl.multiple_of(i * QBLK, QBLK), QBLK)
        products = values.T * o_turn[:, span]
        for head in range(group):
            delta[head, :, span] = jnp.sum(
                products[head * HEAD_DIM : (head + 1) * HEAD_DIM], axis=0, keepdims=True
            )
        for head in range(group):
            first = head * HEAD_DIM
            begin = first // LANE * LANE
            window = values[:, begin : min(begin + 2 * LANE, values.shape[1])]
            shift = first - begin
            if shift:
                window = pltpu.roll(window, window.shape[1] - shift, 1)
            piece = jnp.where(lanes < HEAD_DIM, window[:, :LANE], 0.0)
            do_full[pl.ds(pl.multiple_of(i * QBLK, QBLK), QBLK), pl.ds(head * LANE, LANE)] = piece.astype(bf)
        return carry

    lax.fori_loop(0, length // QBLK, widen, 0)

    def unturn(grad, span):
        return grad * cos[span, :] + pltpu.roll(grad * sin[span, :], LANE // 2, 1)

    blocks = length // QBLK
    tile = min(length, 512)

    def query_block(head, i):
        at = pl.multiple_of(head * wide, LANE)
        q_lane, k_lane, v_lane = (pl.ds(pl.multiple_of(at + j * LANE, LANE), LANE) for j in range(3))
        lane = pl.ds(pl.multiple_of(head * LANE, LANE), LANE)
        span = pl.ds(pl.multiple_of(i * QBLK, QBLK), QBLK)
        q = qkv_s[span, q_lane]
        do = do_full[span, lane]
        shift = lse[head, :, span]
        less = delta[head, :, span]
        pic = pic_row[:, span]
        gq = jnp.zeros((LANE, QBLK), f32)
        for j in range(length // tile):
            part = pl.ds(j * tile, tile)
            scores = lax.dot_general(
                qkv_s[part, k_lane], q, (((1,), (1,)), ((), ())), preferred_element_type=f32
            )
            grad_probs = lax.dot_general(
                qkv_s[part, v_lane], do, (((1,), (1,)), ((), ())), preferred_element_type=f32
            )
            probs = jnp.exp2(scores * EXP_SCALE - shift)
            probs = jnp.where(pic_col[part, :] == pic, probs, 0.0)
            gv_sum[part, :] += jnp.dot(probs.astype(bf), do, preferred_element_type=f32)
            grad_scores = (probs * (grad_probs - less)).astype(bf)
            gk_sum[part, :] += jnp.dot(grad_scores, q, preferred_element_type=f32)
            gq += jnp.dot(k_turn[lane, part], grad_scores, preferred_element_type=f32)
        gm[span, pl.ds(0, LANE)] = unturn(gq.T * SCALE, span).astype(bf)

    def head_close(head):
        at = pl.multiple_of(head * wide, LANE)
        load_wq = pltpu.make_async_copy(wq.at[:, pl.ds(at, wide)], wq_cols, load_sem.at[0])
        load_wq.start()

        def close(i, line):
            span = pl.ds(pl.multiple_of(i * QBLK, QBLK), QBLK)
            gm[span, pl.ds(LANE, LANE)] = unturn(gk_sum[span, :] * SCALE, span).astype(bf)
            gm[span, pl.ds(2 * LANE, LANE)] = gv_sum[span, :].astype(bf)
            grads = gm[span, :]
            chunk, within = i // (toks // QBLK), (i % (toks // QBLK)) * QBLK
            packs[head, chunk, pl.ds(pl.multiple_of(within, QBLK), QBLK), :] = jnp.dot(
                grads, sel[...], preferred_element_type=f32
            ).astype(bf)
            return line + jnp.sum(grads.astype(f32), axis=0, keepdims=True)

        line = lax.fori_loop(0, blocks, close, jnp.zeros((1, wide), f32))
        rows_sum[0:1, pl.ds(at, wide)] = line

    def weight_back(head):
        at = pl.multiple_of(head * wide, LANE)
        line = rows_sum[0:1, pl.ds(at, wide)]
        pltpu.make_async_copy(wq.at[:, pl.ds(at, wide)], wq_cols, load_sem.at[0]).wait()
        tall = width // 2
        per = tall // shard
        for i in range(2):
            span = pl.ds(i * tall, tall)
            grad = jnp.dot(n_turn[span, :], gm[...], preferred_element_type=f32)
            weight = wq_cols[span, :].astype(f32)
            columns[span, 0:1] += jnp.sum(weight * grad, axis=1, keepdims=True)
            columns[span, 1:2] += jnp.sum(weight * line, axis=1, keepdims=True)
            grad = grad * columns[span, 8:9] + columns[span, 9:10] * line
            for s in range(per):
                dq[i * per + s, pl.ds(0, shard), pl.ds(at, wide)] = grad[s * shard : (s + 1) * shard].astype(bf)

    def load_cols(head, g):
        cols = pl.ds(pl.multiple_of((g * group + head) * packed, packed), packed)
        return pltpu.make_async_copy(wh.at[:, :, cols], w_cols.at[g % 2], load_sem.at[2 + g % 2])

    def input_back(head):
        for g in range(2):
            load_cols(head, g).start()
        for g in range(size):
            load_cols(head, g).wait()
            for s in range(rows * size):
                w_wide[pl.ds(s * shard, shard), :] = w_cols[g % 2, s].astype(f32)
            dx_out[...] += lax.dot_general(
                packed_in[head, g], w_wide[...].astype(bf), (((1,), (1,)), ((), ())), preferred_element_type=f32
            )
            if g + 2 < size:
                load_cols(head, g + 2).start()

    dx_out[...] = jnp.zeros_like(dx_out)
    rows_sum[...] = jnp.zeros_like(rows_sum)
    total = group * blocks
    events = []
    for where, event in EVENTS:
        if event[0] == "z_sum":
            events.append((where, functools.partial(z_sum, event[1])))
        else:
            _, which, stage = event
            for later in range(stage, min(stage + 1, stages) if stage == 0 else stages):
                events.append((where, functools.partial(advance, which, later)))

    def step(i, carry):
        head, block = i // blocks, i % blocks
        for where, event in events:
            if where < 1:
                pl.when(i == int(where * total))(event)

        @pl.when(block == 0)
        def _():
            gk_sum[...] = jnp.zeros_like(gk_sum)
            gv_sum[...] = jnp.zeros_like(gv_sum)

        query_block(head, block)

        @pl.when(block == blocks - 1)
        def _():
            head_close(head)
            for h in range(group):
                pl.when(head == h)(a_heads[h].send_all)
            weight_back(head)

        @pl.when((block == blocks - 1) & (head > 0))
        def _():
            for h in range(1, group):
                pl.when(head == h)(a_heads[h - 1].recv)
            input_back(head - 1)

        return carry

    lax.fori_loop(0, total, step, 0)

    lines = -(-width // (group * wide))
    turned = columns[:, pl.ds(0, 8)].T
    tail = [rows_sum[0:1, pl.ds(0, group * wide)]]
    for line in (0, 1):
        rows_sum[1 + line : 2 + line, pl.ds(0, width)] = turned[line : line + 1]
        tail += [rows_sum[1 + line : 2 + line, pl.ds(k * group * wide, group * wide)] for k in range(lines)]
    tail = jnp.concatenate(tail, axis=0).astype(bf)

    def put_tail(i, carry):
        dq[i, pl.ds(shard, tail.shape[0]), :] = tail
        return carry

    lax.fori_loop(0, rows * size, put_tail, 0)
    rq.core_send()
    start(rq_at)
    for where, event in events:
        if where >= 1:
            event()
    a_heads[group - 1].recv()
    input_back(group - 1)
    for stage in range(stages):
        advance(rq_at, stage)
    z_sum(rq_at)
    for move in a_heads:
        move.finish()


def backward_call(
    mesh, attd, x, cot, wp, w1, w2, b1, hat, qkv, k_t, o_t, wh, wq, cos, sin, pic_col, pic_row, lse, small, sel, tall
):
    rows, size = mesh.shape["row"], mesh.shape["seq"]
    toks, width = x.shape
    length = toks * size
    group = HEADS // size
    wide = group * 3 * LANE
    total = rows * size
    shard = width // total
    ff = w1.shape[1]
    bf, f32 = jnp.bfloat16, jnp.float32
    shape = jax.ShapeDtypeStruct
    dq_shape = (total, tall, wide)
    g1, g2 = shape((total, shard, ff), bf), shape((total, ff // total, width), bf)
    gp = shape((total, round_up(shard + 4 + ff // width, 16), width), bf)
    half = (total, shard, ff // 2)
    big = [[shape(s, bf) for s in reduce_shapes(g, rows, size)] for g in (half, half, g2.shape, gp.shape)]
    vm = [pltpu.VMEM(s, bf) for s in reduce_shapes(dq_shape, rows, size)]
    go_shape = (size, toks, round_up(group * HEAD_DIM, LANE))
    outs = (
        shape((toks, width), f32),
        shape((size, tall, wide), bf),
        shape((toks, width), bf),
        shape((toks, width), f32),
        shape(g2.shape[1:], f32),
        shape(g1.shape[1:], f32),
        shape(gp.shape[1:], f32),
        g2, g1, gp,
        shape(go_shape, bf),
        shape((1, ff), f32),
        shape((total,) + wh.shape, bf),
        shape((toks, ff), bf),
        shape((toks, ff), bf),
        *(s for group_of in big for s in group_of),
    )
    results = pl.pallas_call(
        functools.partial(backward_kernel, rows, size, shard, group, len(vm)),
        out_shape=outs,
        in_specs=[ANY] * 13 + [VMEM] * 7,
        out_specs=(VMEM,) * 2 + (ANY,) * (len(outs) - 2),
        scratch_shapes=[
            *vm,
            pltpu.VMEM(go_shape, bf),
            pltpu.VMEM((group, size, toks, 2 * LANE), bf),
            pltpu.VMEM(dq_shape, bf),
            pltpu.VMEM((8, max(ff, round_up(width, wide))), f32),
            pltpu.SemaphoreType.DMA((640,)),
            pltpu.SemaphoreType.DMA((4,)),
        ],
        compiler_params=pltpu.CompilerParams(
            collective_id=1, has_side_effects=True, vmem_limit_bytes=63 * 1024 * 1024
        ),
        name="backward",
    )(attd, x, cot, wp, w1, w2, b1, hat, qkv, k_t, o_t, wh, wq, cos, sin, pic_col, pic_row, lse, small, sel)
    return results[:7]


def layer_norm(values, norm_gain, norm_shift):
    centre = jnp.mean(values, axis=-1, keepdims=True)
    centered = values - centre
    variance = jnp.mean(centered * centered, axis=-1, keepdims=True)
    return centered * lax.rsqrt(variance + NORM_EPS) * norm_gain + norm_shift


def pack_small(vectors, more, width, index, total):
    lines = []
    for values in vectors:
        full = values.shape[0] * total
        line = lax.dynamic_update_slice(jnp.zeros((full,), values.dtype), values, (index * values.shape[0],))
        lines.append(line.reshape(-1, width))
    lines = jnp.concatenate(lines + [more], axis=0)
    return jnp.pad(lines, ((0, round_up(lines.shape[0], 16) - lines.shape[0]), (0, 0)))


def shards(
    mesh,
    activations,
    cotangent,
    pic_lengths,
    pic_widths,
    ln1_gain,
    ln1_bias,
    qkv_weight,
    qkv_bias,
    proj_weight,
    proj_bias,
    ln2_gain,
    ln2_bias,
    fc1_weight,
    fc1_bias,
    fc2_weight,
    fc2_bias,
):
    rows, size = mesh.shape["row"], mesh.shape["seq"]
    total = rows * size
    index = lax.axis_index("row") * size + lax.axis_index("seq")
    _, toks, width = activations.shape
    length = toks * size
    group = HEADS // size
    shard = proj_weight.shape[0]
    bf, f32 = jnp.bfloat16, jnp.float32

    picture, cos, sin = token_layout(pic_lengths[0], pic_widths[0], length)
    bias_line = lax.dynamic_update_slice(jnp.zeros((1, 3 * width), bf), qkv_bias[None], (0, index * qkv_bias.shape[0]))
    bias_lines = pack_heads(bias_line).reshape(size, -1)
    bias_lines = jnp.pad(bias_lines, ((0, 0), (0, width - bias_lines.shape[1])))
    small = pack_small(
        (ln1_gain, ln1_bias, proj_bias, ln2_gain, ln2_bias, fc2_bias, fc1_bias), bias_lines, width, index, total
    )
    sel = pick_lanes()
    x = activations[0]
    wh = pack_heads(qkv_weight)
    wq = wh.reshape(shard, size, -1).transpose(1, 0, 2)
    wp, w1, w2, att, hat, qkv, k_t, wq_full, o_t, lines, lse = forward_call(
        mesh, x, wq, proj_weight, fc1_weight, fc2_weight, small, sel.T, cos, sin,
        picture[:, None], picture[None, :],
    )
    wp, w1, w2 = (w.reshape(-1, w.shape[-1]) for w in (wp, w1, w2))
    attended = jnp.concatenate([att[g, :, : group * HEAD_DIM] for g in range(size)], axis=-1)
    b_up = lines[6 : 6 + w1.shape[1] // width].reshape(1, -1)
    grad_normed, grad_qkv, layer_out, grad_middle, grad_down, grad_up, grad_proj = backward_call(
        mesh, attended, x, cotangent[0], wp, w1, w2, b_up, hat, qkv, k_t, o_t, wh, wq_full, cos, sin,
        picture[:, None], picture[None, :], lse, lines, sel,
        round_up(shard + 1 + 2 * -(-width // (group * 3 * LANE)), 16),
    )
    own = [lax.dynamic_slice_in_dim(grad_proj[shard + i], index * shard, shard) for i in range(4)]
    grad_proj_bias, grad_gain_two, grad_shift_two, grad_down_bias = own
    up_lines = grad_proj[shard + 4 : shard + 4 + w1.shape[1] // width].reshape(-1)
    grad_up_bias = lax.dynamic_slice_in_dim(up_lines, index * fc1_bias.shape[0], fc1_bias.shape[0])
    grad_proj = grad_proj[:shard]

    grad_qkv = grad_qkv.astype(f32)
    grad_bias = natural(grad_qkv[:, shard : shard + 1])[0]
    lined = -(-width // (group * 3 * LANE))
    norm_lines = jnp.sum(grad_qkv[:, shard + 1 : shard + 1 + 2 * lined], axis=0).reshape(2, -1)[:, :width]
    grad_gain_one, grad_shift_one = (
        lax.dynamic_slice_in_dim(norm_lines[i], index * shard, shard) for i in range(2)
    )
    grad_qkv = natural(grad_qkv[:, :shard])
    grad_qk = lax.dynamic_slice_in_dim(grad_bias[: 2 * width], index * 2 * shard, 2 * shard)
    grad_value = lax.dynamic_slice_in_dim(grad_bias[2 * width :], index * shard, shard)
    _, norm_one_back = jax.vjp(layer_norm, x.astype(f32), lines[0], lines[1])
    grad_inputs, _, _ = norm_one_back(grad_normed)
    grad_acts = (grad_inputs + grad_middle).astype(bf)

    return (
        layer_out[None],
        grad_acts[None],
        grad_gain_one,
        grad_shift_one,
        grad_qkv,
        grad_qk,
        grad_value,
        grad_proj,
        grad_proj_bias,
        grad_gain_two,
        grad_shift_two,
        grad_up,
        grad_up_bias,
        grad_down,
        grad_down_bias,
    )


def solution(mesh):
    one, two = P(("row", "seq")), P(("row", "seq"), None)
    tokens = P("row", "seq", None)
    return jax.shard_map(
        functools.partial(shards, mesh),
        mesh=mesh,
        in_specs=(tokens, tokens, P("row", None), P("row", None), one, one, two, one, two, one, one, one, two, one, two, one),
        out_specs=(tokens, tokens, one, one, two, one, one, two, one, one, one, two, one, two, one),
        check_vma=False,
    )
```

time: 1550 us -> 669 us (0.43)
  waiting for transfers between devices: 696 us -> 0 us
  Pallas kernels: 311 us -> 603 us
  matrix products: 278 us -> 0 us
  other arithmetic: 92.4 us -> 16.2 us
  blocking collectives: 72.7 us -> 0 us
  local copies, waits for them, and re-layouts: 75 us -> 37.5 us
    reduce_scatter x5 -> x0, waiting for transfers between devices: 691 us -> none  [the longest x3 605 us: owned(): lax.psum_scatter(values, ('row', 'seq'), scatter_dimension=0, tiled=True)]
    pallas_call x1 -> x2, Pallas kernels: 311 us -> 603 us  [the longest x1 365 us: backward_call(): pl.pallas_call(functools.partial(backward_kernel, rows, size, shard, grou...]
    dot_general x16 -> x0, matrix products: 278 us -> none  [the longest x1 51.6 us: shards(): scores = jnp.einsum('khe,qhe->hkq', k, q, preferred_element_type=f32)]
    convert_element_type x5 -> x3, other arithmetic: 59.8 us -> 2.7 us  [the longest x2 1.52 us: pick_lanes(): (target[:, None] == jnp.arange(2 * LANE)[None, :]).astype(jnp.bfloat16)]
    unnamed x1 -> x0, blocking collectives: 45.8 us -> none
  transfers between devices with their start and end apart: 7 -> 0, of which waited for: 5 -> 0; matrix products, arithmetic and copies ran while one was open for 8% -> 0% of each run, Pallas kernels for 0% -> 0%
where the time goes in v3:
time: 669 us; the launch traced here: 658 us
  Pallas kernels  603 us (90%)
  local copies, waits for them, and re-layouts  37.5 us (6%)
  other arithmetic  16.2 us (2%)
    pallas_call x1, Pallas kernels, backward_call(): pl.pallas_call(functools.partial(backward_kernel, rows, size, shard, grou...  365 us
    pallas_call x1, Pallas kernels, forward_call(): pl.pallas_call(functools.partial(forward_kernel, rows, size, group), out_...  238 us

profile of v3, /device:TPU:0, one launch (start us, length us, event | category | flops | bytes accessed | tf_op | source)
XLA Modules:
  0.0 658.1 jit_solution(7039938071511259100)
XLA Ops:
  5.5 0.9 dynamic_update_slice.36
  6.4 0.8 dynamic_update_slice.37
  8.3 0.8 reduce-window.4
  11.0 1.2 fusion.10
  13.1 2.5 pad_maximum_fusion
  15.6 1.4 copy.72.pic_col.refs_15_
  16.9 0.8 reshape.241
  18.6 0.8 copy.84
  20.1 237.8 %forward.1 = (bf16[32,40,1280]{2,1,0:T(8,128)(2,1)}, bf16[32,40,5120]{2,1,0:T(8,128)(2,1)}, bf16[32,160,1280]{2,1,0:T(8,128)(2,1)}, bf16[4,512,384]{2,1,0:T(8,12...) custom-call(bf16[512,1280]{1,0:T(8,128)(2,1)} %bitcast.78, ...), custom_call_target="tpu_custom_call" | custom-call | tf_op jit(solution)/shard_map/forward/pallas_call | solution.py:444
  258.0 1.5 slice_bitcast_fusion
  259.5 2.7 concatenate.25.refs_0_
  262.2 0.9 slice_bitcast_fusion.4
  263.7 0.8 copy.80
  264.5 0.8 fusion.9.refs_19_
  265.3 365.1 %backward.1 = (f32[512,1280]{1,0:T(8,128)}, bf16[4,48,1536]{2,1,0:T(8,128)(2,1)}, bf16[512,1280]{1,0:T(8,128)(2,1)}, f32[512,1280]{1,0:T(8,128)}, f32[160,1280]{...) custom-call(bf16[512,1280]{1,0:T(8,128)(2,1)} %concatenate.25.refs_0, ...), custom_call_target="tpu_custom_call" | custom-call | tf_op jit(solution)/shard_map/backward/pallas_call | solution.py:1283
  630.4 1.0 fusion.39
  632.0 1.2 convert_element_type.46
  633.2 1.0 copy-done.4
  635.9 1.0 slice.114
  637.0 1.8 reshape.260
  639.1 1.2 reshape.261
  640.2 1.1 reshape.262
  642.3 1.6 reshape.263
  643.9 1.0 slice_reduce_fusion
  646.1 0.8 slice_reduce_fusion.2
  647.1 2.7 fusion.3
  649.8 0.9 fusion.38
  650.7 0.8 copy-done.3
  651.5 2.0 fusion.5
  654.9 1.1 copy.100
  655.9 0.9 copy.101
  656.8 0.9 copy.102
  (92 shorter events, 16.8 us)
Async XLA Ops:
  9.2 6.3 copy-start.10
  13.1 3.9 copy-start.8
  630.4 5.5 copy-start.2
  633.2 1.0 copy-start.4
  641.6 5.3 copy-start
  646.9 2.9 copy-start.1
  649.8 1.7 copy-start.3
  651.5 2.0 copy-start.9
  651.5 3.3 copy-start.5
  653.5 2.4 copy-start.7
  653.5 3.3 copy-start.6

commit v4 on v3

--- a/solution.py
+++ b/solution.py
@@ -7,6 +7,8 @@
 from jax.experimental import pallas as pl
 from jax.experimental.pallas import tpu as pltpu
 from jax.sharding import PartitionSpec as P
+import ml_dtypes
+import numpy as np
 
 HEADS = 16
 HEAD_DIM = 80
@@ -484,7 +486,8 @@
 
 
 def token_layout(lengths, widths, row_len):
-    pic_ends = jnp.cumsum(lengths)
+    slots = jnp.arange(lengths.shape[0])
+    pic_ends = jnp.sum(jnp.where(slots[:, None] >= slots[None, :], lengths[None, :], 0), axis=1)
     pic_starts = pic_ends - lengths
     positions = jnp.arange(row_len, dtype=jnp.int32)
     picture = jnp.sum((positions[:, None] >= pic_ends[None, :]).astype(jnp.int32), axis=1)
@@ -513,20 +516,18 @@
 
 
 def pick_lanes():
-    spread = jnp.arange(3 * LANE)
+    spread = np.arange(3 * LANE)
     kind, lane = spread // LANE, spread % LANE
-    turned = jnp.where(lane < LANE // 2, lane, lane - LANE // 2 + HALF)
-    inside = jnp.where(kind < 2, lane % (LANE // 2) < HALF, lane < HEAD_DIM)
-    target = jnp.where(inside, kind * HEAD_DIM + jnp.where(kind < 2, turned, lane), -1)
-    return (target[:, None] == jnp.arange(2 * LANE)[None, :]).astype(jnp.bfloat16)
-
-
-def natural(values):
+    turned = np.where(lane < LANE // 2, lane, lane - LANE // 2 + HALF)
+    inside = np.where(kind < 2, lane % (LANE // 2) < HALF, lane < HEAD_DIM)
+    target = np.where(inside, kind * HEAD_DIM + np.where(kind < 2, turned, lane), -1)
+    return (target[:, None] == np.arange(2 * LANE)[None, :]).astype(ml_dtypes.bfloat16)
+
+
+def unpack_heads(values):
     size, a, _ = values.shape
-    values = values.reshape(size, a, HEADS // size, 3, LANE)
-    turned = values[:, :, :, :2].reshape(size, a, HEADS // size, 2, 2, LANE // 2)[..., :HALF]
-    turned = turned.reshape(size, a, HEADS // size, 2, HEAD_DIM)
-    values = jnp.concatenate([turned, values[:, :, :, 2:, :HEAD_DIM]], axis=3)
+    values = values.reshape(size, a, HEADS // size, 2 * LANE)[..., : 3 * HEAD_DIM]
+    values = values.reshape(size, a, HEADS // size, 3, HEAD_DIM)
     return values.transpose(1, 3, 0, 2, 4).reshape(a, 3 * HEADS * HEAD_DIM)
 
 
@@ -687,7 +688,7 @@
         return out
 
     attd, x, cot, wp, w1, w2, b1, hat, qkv, k_t, o_t, wh, wq, cos, sin, pic_col, pic_row, lse, small, sel = take(20)
-    dx_out, dq_out, layer_out, g_mid, g2_out, g1_out, gp_out, g2, g1, gp, go, b1_sum, wh_all, act, g_act = take(15)
+    dx_out, dq_out, dq_pack, layer_out, g_mid, g2, g1, gp, go, b1_sum, wh_all, act, g_act = take(13)
     big = [take(counts) for _ in range(4)]
     vm = take(counts)
     do_in, packed_in, dq, rows_sum, sem_ref, load_sem = refs
@@ -706,11 +707,11 @@
     half_ff = w1.shape[1] // 2
     for i in range(2):
         cols = pl.ds(i * half_ff, half_ff)
-        sources.append((g1.at[:, :, cols], g1_out.at[:, cols], big[i]))
-    sources += [(g2, g2_out, big[2]), (gp, gp_out, big[3])]
-    sources.append((dq, dq_out, vm))
+        sources.append((g1.at[:, :, cols], big[i]))
+    sources += [(g2, big[2]), (gp, big[3])]
+    sources.append((dq, vm))
     reducers, z_moves, z_bufs = [], [], []
-    for src, out, bufs in sources:
+    for src, bufs in sources:
         inner, z_refs = reduce_refs(bufs, rows)
         r = Reduce(src, *inner, row, seq, rows, size, sems, len(reducers) >= len(big))
         reducers.append(r)
@@ -741,28 +742,11 @@
         else:
             z_send(which)
 
-    def z_sum(which):
-        r, out = reducers[which], sources[which][1]
-        cols = r.half // 2 if r.half % (4 * LANE) == 0 else r.half
+    def z_wait(which):
         for half in range(2):
             z_moves[which][half].recv()
-            buf = z_bufs[which][half]
             if which == rq_at:
-                out[:, :, pl.ds(half * r.half, r.half)] = buf[...]
-            else:
-
-                def body(a, o):
-                    total = a[0].astype(f32)
-                    for z in range(1, size):
-                        total += a[z].astype(f32)
-                    o[...] = total
-
-                pltpu.emit_pipeline(
-                    body,
-                    grid=(r.half // cols,),
-                    in_specs=[pl.BlockSpec(r.block[:2] + (cols,), lambda i: (0, 0, i))],
-                    out_specs=[pl.BlockSpec((r.block[1], cols), lambda i, half=half: (0, half * (r.half // cols) + i))],
-                )(buf, out)
+                dq_out[:, :, pl.ds(half * rq.half, rq.half)] = z_bufs[which][half][...]
 
     ready = rq_at
 
@@ -990,15 +974,16 @@
         pltpu.VMEM((toks, width), bf),
         pltpu.VMEM((round_up(gp.shape[1] - shard, 8), width), f32),
     )
+    if stages:
+        advance(0, 0)
     start(2)
     if stages:
-        advance(0, 0)
-    start(3)
+        advance(1, 0)
     wh_spread.finish()
     pl.run_scoped(
         functools.partial(
-            attention_back, rows, size, shard, group, row, seq, sems, start, advance, z_sum, a_do, rq, rq_at,
-            (hat, qkv, k_t, o_t, wh_all, wq, cos, sin, pic_col, pic_row, lse, small, sel, dx_out, do_in, packed_in, dq, rows_sum),
+            attention_back, rows, size, shard, group, row, seq, sems, start, advance, z_wait, a_do, rq, rq_at,
+            (hat, qkv, k_t, o_t, wh_all, wq, cos, sin, pic_col, pic_row, lse, small, sel, dx_out, do_in, packed_in, dq, rows_sum, dq_out, dq_pack),
             load_sem,
         ),
         pltpu.VMEM((length, group * wide), bf),
@@ -1026,25 +1011,25 @@
 
 
 EVENTS = (
-    (0.15, ("advance", 1, 0)),
-    (0.35, ("advance", 0, 1)),
-    (0.45, ("advance", 1, 1)),
-    (0.5, ("advance", 2, 0)),
-    (0.55, ("advance", 3, 0)),
-    (0.75, ("z_sum", 0)),
-    (0.8, ("z_sum", 1)),
+    (0.15, ("advance", 0, 1)),
+    (0.2, ("start", 3)),
+    (0.3, ("advance", 1, 1)),
+    (0.55, ("advance", 2, 0)),
+    (0.6, ("advance", 3, 0)),
     (0.8, ("advance", 2, 1)),
     (0.85, ("advance", 3, 1)),
-    (1, ("z_sum", 2)),
-    (1, ("z_sum", 3)),
+    (1, ("wait", 0)),
+    (1, ("wait", 1)),
+    (1, ("wait", 2)),
+    (1, ("wait", 3)),
 )
 
 
 def attention_back(
-    rows, size, shard, group, row, seq, sems, start, advance, z_sum, a_do, rq, rq_at, refs, load_sem,
+    rows, size, shard, group, row, seq, sems, start, advance, z_wait, a_do, rq, rq_at, refs, load_sem,
     qkv_s, do_full, k_turn, gk_sum, gv_sum, gm, n_turn, columns, packs, w_cols, w_wide, wq_cols, o_turn, delta,
 ):
-    hat, qkv, k_t, o_t, wh, wq, cos, sin, pic_col, pic_row, lse, small, sel, dx_out, do_in, packed_in, dq, rows_sum = refs
+    hat, qkv, k_t, o_t, wh, wq, cos, sin, pic_col, pic_row, lse, small, sel, dx_out, do_in, packed_in, dq, rows_sum, dq_out, dq_pack = refs
     length = qkv.shape[0]
     toks = length // size
     width = hat.shape[0]
@@ -1063,7 +1048,7 @@
         copy.start()
     columns[...] = jnp.zeros_like(columns)
     columns[:, pl.ds(8, 8)] = small[0:8, :].T
-    for copy in loads:
+    for copy in loads[:2] + loads[3:]:
         copy.wait()
     a_do.recv()
 
@@ -1089,6 +1074,7 @@
         return carry
 
     lax.fori_loop(0, length // QBLK, widen, 0)
+    loads[2].wait()
 
     def unturn(grad, span):
         return grad * cos[span, :] + pltpu.roll(grad * sin[span, :], LANE // 2, 1)
@@ -1180,8 +1166,10 @@
     total = group * blocks
     events = []
     for where, event in EVENTS:
-        if event[0] == "z_sum":
-            events.append((where, functools.partial(z_sum, event[1])))
+        if event[0] == "wait":
+            events.append((where, functools.partial(z_wait, event[1])))
+        elif event[0] == "start":
+            events.append((where, functools.partial(start, event[1])))
         else:
             _, which, stage = event
             for later in range(stage, min(stage + 1, stages) if stage == 0 else stages):
@@ -1207,9 +1195,9 @@
                 pl.when(head == h)(a_heads[h].send_all)
             weight_back(head)
 
-        @pl.when((block == blocks - 1) & (head > 0))
+        @pl.when((block == blocks - 1) & (head > 0) & (head < group - 1))
         def _():
-            for h in range(1, group):
+            for h in range(1, group - 1):
                 pl.when(head == h)(a_heads[h - 1].recv)
             input_back(head - 1)
 
@@ -1232,14 +1220,27 @@
     lax.fori_loop(0, rows * size, put_tail, 0)
     rq.core_send()
     start(rq_at)
+    for head in range(max(0, group - 2), group):
+        a_heads[head].recv()
+        input_back(head)
+        if head == group - 2 and stages:
+            advance(rq_at, 0)
+    for stage in range(0 if group < 2 else 1, stages):
+        advance(rq_at, stage)
     for where, event in events:
         if where >= 1:
             event()
-    a_heads[group - 1].recv()
-    input_back(group - 1)
-    for stage in range(stages):
-        advance(rq_at, stage)
-    z_sum(rq_at)
+    z_wait(rq_at)
+
+    def pack(i, carry):
+        g, head = i // group, i % group
+        raw = dq_out[g, :, pl.ds(pl.multiple_of(head * wide, LANE), wide)]
+        dq_pack[g, :, pl.ds(pl.multiple_of(head * packed, LANE), packed)] = jnp.dot(
+            raw, sel[...], preferred_element_type=f32
+        ).astype(bf)
+        return carry
+
+    lax.fori_loop(0, size * group, pack, 0)
     for move in a_heads:
         move.finish()
 
@@ -1267,11 +1268,9 @@
     outs = (
         shape((toks, width), f32),
         shape((size, tall, wide), bf),
+        shape((size, tall, group * 2 * LANE), bf),
         shape((toks, width), bf),
         shape((toks, width), f32),
-        shape(g2.shape[1:], f32),
-        shape(g1.shape[1:], f32),
-        shape(gp.shape[1:], f32),
         g2, g1, gp,
         shape(go_shape, bf),
         shape((1, ff), f32),
@@ -1284,7 +1283,7 @@
         functools.partial(backward_kernel, rows, size, shard, group, len(vm)),
         out_shape=outs,
         in_specs=[ANY] * 13 + [VMEM] * 7,
-        out_specs=(VMEM,) * 2 + (ANY,) * (len(outs) - 2),
+        out_specs=(VMEM,) * 3 + (ANY,) * (len(outs) - 3),
         scratch_shapes=[
             *vm,
             pltpu.VMEM(go_shape, bf),
@@ -1299,7 +1298,11 @@
         ),
         name="backward",
     )(attd, x, cot, wp, w1, w2, b1, hat, qkv, k_t, o_t, wh, wq, cos, sin, pic_col, pic_row, lse, small, sel)
-    return results[:7]
+    sums = [
+        jnp.concatenate([jnp.sum(r.astype(f32), axis=0) for r in results[i - 2 : i]], axis=-1)
+        for i in range(len(results) - 3 * len(vm), len(results) + 1, len(vm))
+    ]
+    return (*results[:5], sums[2], jnp.concatenate(sums[:2], axis=-1), sums[3])
 
 
 def layer_norm(values, norm_gain, norm_shift):
@@ -1309,12 +1312,13 @@
     return centered * lax.rsqrt(variance + NORM_EPS) * norm_gain + norm_shift
 
 
+def at_own_place(values, index, total):
+    mine = jnp.arange(total, dtype=jnp.int32)[:, None] == index
+    return jnp.where(mine, values[None, :], jnp.zeros((), values.dtype)).reshape(-1)
+
+
 def pack_small(vectors, more, width, index, total):
-    lines = []
-    for values in vectors:
-        full = values.shape[0] * total
-        line = lax.dynamic_update_slice(jnp.zeros((full,), values.dtype), values, (index * values.shape[0],))
-        lines.append(line.reshape(-1, width))
+    lines = [at_own_place(values, index, total).reshape(-1, width) for values in vectors]
     lines = jnp.concatenate(lines + [more], axis=0)
     return jnp.pad(lines, ((0, round_up(lines.shape[0], 16) - lines.shape[0]), (0, 0)))
 
@@ -1348,7 +1352,7 @@
     bf, f32 = jnp.bfloat16, jnp.float32
 
     picture, cos, sin = token_layout(pic_lengths[0], pic_widths[0], length)
-    bias_line = lax.dynamic_update_slice(jnp.zeros((1, 3 * width), bf), qkv_bias[None], (0, index * qkv_bias.shape[0]))
+    bias_line = at_own_place(qkv_bias, index, total)[None]
     bias_lines = pack_heads(bias_line).reshape(size, -1)
     bias_lines = jnp.pad(bias_lines, ((0, 0), (0, width - bias_lines.shape[1])))
     small = pack_small(
@@ -1365,25 +1369,20 @@
     wp, w1, w2 = (w.reshape(-1, w.shape[-1]) for w in (wp, w1, w2))
     attended = jnp.concatenate([att[g, :, : group * HEAD_DIM] for g in range(size)], axis=-1)
     b_up = lines[6 : 6 + w1.shape[1] // width].reshape(1, -1)
-    grad_normed, grad_qkv, layer_out, grad_middle, grad_down, grad_up, grad_proj = backward_call(
+    grad_normed, grad_qkv, packed, layer_out, grad_middle, grad_down, grad_up, grad_proj = backward_call(
         mesh, attended, x, cotangent[0], wp, w1, w2, b_up, hat, qkv, k_t, o_t, wh, wq_full, cos, sin,
         picture[:, None], picture[None, :], lse, lines, sel,
         round_up(shard + 1 + 2 * -(-width // (group * 3 * LANE)), 16),
     )
-    own = [lax.dynamic_slice_in_dim(grad_proj[shard + i], index * shard, shard) for i in range(4)]
-    grad_proj_bias, grad_gain_two, grad_shift_two, grad_down_bias = own
-    up_lines = grad_proj[shard + 4 : shard + 4 + w1.shape[1] // width].reshape(-1)
-    grad_up_bias = lax.dynamic_slice_in_dim(up_lines, index * fc1_bias.shape[0], fc1_bias.shape[0])
+    lined = -(-width // (group * 3 * LANE))
+    norm_lines = jnp.sum(grad_qkv[:, shard + 1 : shard + 1 + 2 * lined].astype(f32), axis=0).reshape(2, -1)[:, :width]
+    sums = jnp.concatenate([grad_proj[shard : shard + 4], norm_lines], axis=0).reshape(6, total, shard)
+    sums = lax.dynamic_index_in_dim(sums, index, 1, keepdims=False)
+    up_lines = grad_proj[shard + 4 : shard + 4 + w1.shape[1] // width].reshape(total, -1)
+    grad_up_bias = lax.dynamic_index_in_dim(up_lines, index, 0, keepdims=False)
     grad_proj = grad_proj[:shard]
-
-    grad_qkv = grad_qkv.astype(f32)
-    grad_bias = natural(grad_qkv[:, shard : shard + 1])[0]
-    lined = -(-width // (group * 3 * LANE))
-    norm_lines = jnp.sum(grad_qkv[:, shard + 1 : shard + 1 + 2 * lined], axis=0).reshape(2, -1)[:, :width]
-    grad_gain_one, grad_shift_one = (
-        lax.dynamic_slice_in_dim(norm_lines[i], index * shard, shard) for i in range(2)
-    )
-    grad_qkv = natural(grad_qkv[:, :shard])
+    grad_qkv = unpack_heads(packed[:, :shard].astype(f32))
+    grad_bias = unpack_heads(packed[:, shard : shard + 1].astype(f32))[0]
     grad_qk = lax.dynamic_slice_in_dim(grad_bias[: 2 * width], index * 2 * shard, 2 * shard)
     grad_value = lax.dynamic_slice_in_dim(grad_bias[2 * width :], index * shard, shard)
     _, norm_one_back = jax.vjp(layer_norm, x.astype(f32), lines[0], lines[1])
@@ -1393,19 +1392,19 @@
     return (
         layer_out[None],
         grad_acts[None],
-        grad_gain_one,
-        grad_shift_one,
+        sums[4],
+        sums[5],
         grad_qkv,
         grad_qk,
         grad_value,
         grad_proj,
-        grad_proj_bias,
-        grad_gain_two,
-        grad_shift_two,
+        sums[0],
+        sums[1],
+        sums[2],
         grad_up,
         grad_up_bias,
         grad_down,
-        grad_down_bias,
+        sums[3],
     )
 
 

time: 669 us -> 650 us (0.972)
  local copies, waits for them, and re-layouts: 37.5 us -> 23.9 us
  Pallas kernels: 603 us -> 596 us
    pallas_call x1, Pallas kernels: 365 us -> 358 us  [backward_call(): pl.pallas_call(functools.partial(backward_kernel, rows, size, shard, grou...]
where the time goes in v4:
time: 650 us; the launch traced here: 639 us
  Pallas kernels  596 us (92%)
  local copies, waits for them, and re-layouts  23.9 us (4%)
  other arithmetic  18.1 us (3%)
    pallas_call x1, Pallas kernels, backward_call(): pl.pallas_call(functools.partial(backward_kernel, rows, size, shard, grou...  358 us
    pallas_call x1, Pallas kernels, forward_call(): pl.pallas_call(functools.partial(forward_kernel, rows, size, group), out_...  238 us

profile of v4, /device:TPU:0, one launch (start us, length us, event | category | flops | bytes accessed | tf_op | source)
XLA Modules:
  0.0 639.1 jit_solution(12731181186304779520)
XLA Ops:
  0.6 0.8 select_reduce_fusion.2
  1.5 0.7 fusion.22
  2.2 0.8 select_reduce_fusion
  3.3 1.2 fusion.8
  5.4 2.5 pad_maximum_fusion
  9.5 0.6 pad.19.small
  10.2 1.4 copy.77.pic_col.refs_15_
  11.5 0.8 reshape.342
  13.2 0.8 copy.89
  14.0 237.5 %forward.1 = (bf16[32,40,1280]{2,1,0:T(8,128)(2,1)}, bf16[32,40,5120]{2,1,0:T(8,128)(2,1)}, bf16[32,160,1280]{2,1,0:T(8,128)(2,1)}, bf16[4,512,384]{2,1,0:T(8,12...) custom-call(bf16[512,1280]{1,0:T(8,128)(2,1)} %bitcast.69, ...), custom_call_target="tpu_custom_call" | custom-call | tf_op jit(solution)/shard_map/forward/pallas_call | solution.py:446
  251.5 1.5 slice_bitcast_fusion
  253.0 2.7 concatenate.31.refs_0_
  255.7 0.9 slice_bitcast_fusion.4
  256.6 0.6 copy.83
  257.3 0.8 copy.84
  258.1 358.1 %backward.1 = (f32[512,1280]{1,0:T(8,128)}, bf16[4,48,1536]{2,1,0:T(8,128)(2,1)}, bf16[4,48,1024]{2,1,0:T(8,128)(2,1)}, bf16[512,1280]{1,0:T(8,128)(2,1)}, f32[5...) custom-call(bf16[512,1280]{1,0:T(8,128)(2,1)} %concatenate.31.refs_0, ...), custom_call_target="tpu_custom_call" | custom-call | tf_op jit(solution)/shard_map/backward/pallas_call | solution.py:1282
  616.2 1.9 convert_reduce_fusion.1
  618.1 0.9 pad_maximum_fusion.5
  619.2 0.6 constant_dynamic-slice_fusion.5
  620.0 0.9 pad_maximum_fusion.4
  621.0 0.7 fusion.10
  622.6 1.6 copy.80
  624.2 2.9 reshape.359
  627.0 0.9 convert_reduce_fusion.10
  628.6 0.8 slice_reduce_fusion.2
  629.7 2.6 fusion.3
  632.4 0.9 fusion.23
  633.3 0.8 copy-done.2
  634.1 2.0 fusion.5
  636.3 0.6 dynamic_slice.15
  637.1 0.6 dynamic_slice.16
  637.6 1.1 copy.91
  (101 shorter events, 6.1 us)
Async XLA Ops:
  1.5 8.7 %copy-start.12 = (s32[2048]{0:T(1024)}, s32[2048]{0:T(1024)S(1)}, u32[]{:S(2)}) copy-start(s32[2048]{0:T(1024)S(1)} %convert_reduce_fusion.9) | copy-start | bytes 24580
  5.3 2.6 copy-start.13
  5.3 2.6 copy-start.14
  5.4 2.6 copy-start.15
  5.4 2.6 copy-start.16
  5.4 2.6 copy-start.17
  5.4 2.6 copy-start.18
  5.4 3.3 copy-start.19
  5.4 3.8 copy-start.20
  5.4 6.1 copy-start.8
  616.2 2.9 copy-start.10
  616.2 2.9 copy-start.11
  616.2 3.6 copy-start.6
  616.2 3.6 copy-start.7
  616.2 3.7 copy-start.4
  616.2 3.7 copy-start.5
  619.1 2.6 copy-start.9
  622.6 6.9 %copy-start = (bf16[1,512,1280]{2,1,0:T(8,128)(2,1)S(1)}, bf16[1,512,1280]{2,1,0:T(8,128)(2,1)}, u32[]{:S(2)}) copy-start(bf16[1,512,1280]{2,1,0:T(8,128)(2,1)} %param.18) | copy-start | bytes 3932164
  629.5 2.9 copy-start.1
  632.4 1.7 copy-start.2
  634.1 3.5 copy-start.3

commit v5 on v4

--- a/solution.py
+++ b/solution.py
@@ -754,7 +754,7 @@
         return pltpu.make_async_copy(src, dst, load_sem.at[sem])
 
     ff = w1.shape[1]
-    ff_blocks = ff // FF_BLK
+    heads = group * HEAD_DIM
 
     wh_chain = Chain(wh, wh_all, row * size, row, seq, size, sems)
     wh_spread = Spread(wh_all, row, seq, rows, size, sems)
@@ -787,7 +787,10 @@
             def one(i, carry):
                 span = pl.ds(pl.multiple_of(i * QBLK, QBLK), QBLK)
                 values = x_v[span, :].astype(f32) + small[2:3, :]
-                values += jnp.dot(attd_v[span, :], wp_v[...], preferred_element_type=f32)
+                for g in range(size):
+                    values += jnp.dot(
+                        attd_v[g, span, pl.ds(0, heads)], wp_v[pl.ds(g * heads, heads), :], preferred_element_type=f32
+                    )
                 middle[span, :] = values
                 centered = values - jnp.mean(values, axis=-1, keepdims=True)
                 variance = jnp.mean(centered * centered, axis=-1, keepdims=True)
@@ -799,7 +802,7 @@
             lax.fori_loop(0, toks // QBLK, one, 0)
 
         pl.run_scoped(
-            head, pltpu.VMEM((toks, width), bf), pltpu.VMEM((toks, width), bf), pltpu.VMEM((width, width), bf)
+            head, pltpu.VMEM(attd.shape, bf), pltpu.VMEM((toks, width), bf), pltpu.VMEM((width, width), bf)
         )
         loads[0].wait()
         out_sum[...] = jnp.zeros_like(out_sum)
@@ -903,7 +906,6 @@
                 copy.start()
             for copy in copies:
                 copy.wait()
-            heads = group * HEAD_DIM
             for g in range(size):
                 part = lax.dot_general(
                     g_low[...], wp_v[pl.ds(g * heads, heads), :], (((1,), (1,)), ((), ())), preferred_element_type=f32
@@ -926,10 +928,9 @@
                 lines[4 + i : 5 + i, :] = rows_sum[0:1, pl.ds(i * width, width)]
             low_lines = lines[0 : gp_v.shape[1] - shard, :].astype(bf)
             get.wait()
-            tall = width // 2
-            per = tall // shard
-            for i in range(2):
-                turned = attd_v[:, pl.ds(i * tall, tall)].astype(f32).T.astype(bf)
+            per = heads // shard
+            for i in range(size):
+                turned = attd_v[i].astype(f32).T[:heads].astype(bf)
                 grad = jnp.dot(turned, g_low[...], preferred_element_type=f32)
                 for s in range(per):
                     gp_v[s, pl.ds(0, shard), :] = grad[s * shard : (s + 1) * shard].astype(bf)
@@ -955,7 +956,7 @@
         reducers[2].core_send()
         start(1)
         pl.run_scoped(
-            proj, pltpu.VMEM((toks, width), bf), pltpu.VMEM((rows * size // 2,) + gp.shape[1:], bf)
+            proj, pltpu.VMEM(attd.shape, bf), pltpu.VMEM((rows,) + gp.shape[1:], bf)
         )
         reducers[3].core_send()
         for stage in range(2, wh_spread.stages + 1):
@@ -1367,10 +1368,9 @@
         picture[:, None], picture[None, :],
     )
     wp, w1, w2 = (w.reshape(-1, w.shape[-1]) for w in (wp, w1, w2))
-    attended = jnp.concatenate([att[g, :, : group * HEAD_DIM] for g in range(size)], axis=-1)
     b_up = lines[6 : 6 + w1.shape[1] // width].reshape(1, -1)
     grad_normed, grad_qkv, packed, layer_out, grad_middle, grad_down, grad_up, grad_proj = backward_call(
-        mesh, attended, x, cotangent[0], wp, w1, w2, b_up, hat, qkv, k_t, o_t, wh, wq_full, cos, sin,
+        mesh, att, x, cotangent[0], wp, w1, w2, b_up, hat, qkv, k_t, o_t, wh, wq_full, cos, sin,
         picture[:, None], picture[None, :], lse, lines, sel,
         round_up(shard + 1 + 2 * -(-width // (group * 3 * LANE)), 16),
     )

time: 650 us -> 646 us (level)
  no operation moved by 1% of the time
where the time goes in v5:
time: 646 us; the launch traced here: 635 us
  Pallas kernels  596 us (92%)
  local copies, waits for them, and re-layouts  19.7 us (3%)
  other arithmetic  18 us (3%)
    pallas_call x1, Pallas kernels, backward_call(): pl.pallas_call(functools.partial(backward_kernel, rows, size, shard, grou...  358 us
    pallas_call x1, Pallas kernels, forward_call(): pl.pallas_call(functools.partial(forward_kernel, rows, size, group), out_...  238 us

profile of v5, /device:TPU:0, one launch (start us, length us, event | category | flops | bytes accessed | tf_op | source)
XLA Modules:
  0.0 635.1 jit_solution(8660153586924219874)
XLA Ops:
  0.6 0.8 select_reduce_fusion.2
  1.5 0.7 fusion.22
  2.2 0.8 select_reduce_fusion
  3.3 1.2 fusion.8
  5.4 2.5 pad_maximum_fusion
  9.5 0.6 pad.19.small
  10.1 1.3 copy.77.pic_col.refs_15_
  11.5 0.8 reshape.342
  13.1 0.8 copy.89
  14.0 237.5 %forward.1 = (bf16[32,40,1280]{2,1,0:T(8,128)(2,1)}, bf16[32,40,5120]{2,1,0:T(8,128)(2,1)}, bf16[32,160,1280]{2,1,0:T(8,128)(2,1)}, bf16[4,512,384]{2,1,0:T(8,12...) custom-call(bf16[512,1280]{1,0:T(8,128)(2,1)} %bitcast.61, ...), custom_call_target="tpu_custom_call" | custom-call | tf_op jit(solution)/shard_map/forward/pallas_call | solution.py:446
  251.5 0.9 slice_bitcast_fusion
  252.4 0.6 copy.83
  253.0 0.8 copy.84
  253.8 358.3 %backward.1 = (f32[512,1280]{1,0:T(8,128)}, bf16[4,48,1536]{2,1,0:T(8,128)(2,1)}, bf16[4,48,1024]{2,1,0:T(8,128)(2,1)}, bf16[512,1280]{1,0:T(8,128)(2,1)}, f32[5...) custom-call(bf16[4,512,384]{2,1,0:T(8,128)(2,1)} %get-tuple-element., ...), custom_call_target="tpu_custom_call" | custom-call | tf_op jit(solution)/shard_map/backward/pallas_call | solution.py:1283
  612.2 1.9 convert_reduce_fusion.1
  614.0 0.9 pad_maximum_fusion.5
  615.2 0.6 constant_dynamic-slice_fusion.5
  616.0 0.9 pad_maximum_fusion.4
  616.9 0.7 fusion.10
  618.0 0.5 reshape.363
  618.5 1.6 copy.80
  620.1 2.9 reshape.359
  623.0 0.9 convert_reduce_fusion.10
  624.0 0.6 fusion.16
  624.6 0.8 slice_reduce_fusion.2
  625.7 2.6 fusion.3
  628.3 0.9 fusion.23
  629.2 0.8 copy-done.2
  630.1 2.0 fusion.5
  632.3 0.6 dynamic_slice.15
  633.0 0.6 dynamic_slice.16
  633.6 1.1 copy.91
  (99 shorter events, 5.0 us)
Async XLA Ops:
  1.5 8.6 %copy-start.12 = (s32[2048]{0:T(1024)}, s32[2048]{0:T(1024)S(1)}, u32[]{:S(2)}) copy-start(s32[2048]{0:T(1024)S(1)} %convert_reduce_fusion.9) | copy-start | bytes 24580
  5.3 2.6 copy-start.13
  5.3 2.6 copy-start.14
  5.4 2.6 copy-start.15
  5.4 2.6 copy-start.16
  5.4 2.6 copy-start.17
  5.4 2.6 copy-start.18
  5.4 3.2 copy-start.19
  5.4 3.7 copy-start.20
  5.4 6.1 copy-start.8
  612.1 2.9 copy-start.10
  612.1 2.9 copy-start.11
  612.1 3.6 copy-start.6
  612.1 3.6 copy-start.7
  612.1 3.7 copy-start.4
  612.1 3.7 copy-start.5
  615.0 2.6 copy-start.9
  618.5 6.9 %copy-start = (bf16[1,512,1280]{2,1,0:T(8,128)(2,1)S(1)}, bf16[1,512,1280]{2,1,0:T(8,128)(2,1)}, u32[]{:S(2)}) copy-start(bf16[1,512,1280]{2,1,0:T(8,128)(2,1)} %param.18) | copy-start | bytes 3932164
  625.4 2.9 copy-start.1
  628.3 1.7 copy-start.2
  630.1 3.5 copy-start.3
